TPU v7x, 32 devices: a whole 2x2x4 slice. The times are simulated.
32 devices in a mesh: wide: 8 (over z, y), narrow: 4 (over x, core).
Axes of the slice: x: 2, y: 2, z: 4, core: 2. Of those that a mesh axis runs over, the one named last changes fastest.
Arguments:
- residual_input: bfloat16 [65536, 768], P(('wide', 'narrow')), may hold values from -12 to 12
- extents_per_device: int32 [32, 4], P(('wide', 'narrow')), may hold values from 1 to 1024, 2048 in all within a row
- attention_lookup_lerp: bfloat16 [768], P(('wide', 'narrow')), may hold values from 0 to 1
- attention_payload_lerp: bfloat16 [768], P(('wide', 'narrow')), may hold values from 0 to 1
- attention_receptance_lerp: bfloat16 [768], P(('wide', 'narrow')), may hold values from 0 to 1
- logarithmic_fading_speed: bfloat16 [768], P(('wide', 'narrow')), may hold values from -9 to -3
- present_reward: bfloat16 [768], P(('wide', 'narrow')), may hold values from -1 to 1
- attention_lookup_proj: bfloat16 [768, 768], P(('wide', 'narrow')), may hold values from -0.21875 to 0.21875
- attention_payload_proj: bfloat16 [768, 768], P(('wide', 'narrow')), may hold values from -0.21875 to 0.21875
- attention_receptance_proj: bfloat16 [768, 768], P(('wide', 'narrow')), may hold values from -0.21875 to 0.21875
- attention_result_proj: bfloat16 [768, 768], P(('wide', 'narrow')), may hold values from -0.875 to 0.875
- feedforward_lookup_lerp: bfloat16 [768], P(('wide', 'narrow')), may hold values from 0 to 1
- feedforward_receptance_lerp: bfloat16 [768], P(('wide', 'narrow')), may hold values from 0 to 1
- feedforward_lookup_proj: bfloat16 [768, 3072], P(('wide', 'narrow')), may hold values from -0.21875 to 0.21875
- feedforward_payload_proj: bfloat16 [3072, 768], P(('wide', 'narrow')), may hold values from -0.109375 to 0.109375
- feedforward_receptance_proj: bfloat16 [768, 768], P(('wide', 'narrow')), may hold values from -0.21875 to 0.21875
- first_normalizer_scaling: bfloat16 [768], P(('wide', 'narrow')), may hold values from 0.5 to 1.5
- first_normalizer_offset: bfloat16 [768], P(('wide', 'narrow')), may hold values from -1 to 1
- second_normalizer_scaling: bfloat16 [768], P(('wide', 'narrow')), may hold values from 0.5 to 1.5
- second_normalizer_offset: bfloat16 [768], P(('wide', 'narrow')), may hold values from -1 to 1
- upstream_adjoint: bfloat16 [65536, 768], P(('wide', 'narrow')), may hold values from -6 to 6
Outputs:
- output: bfloat16 [65536, 768], P(('wide', 'narrow'))
- stream_gradient: bfloat16 [65536, 768], P(('wide', 'narrow'))
- shift_key_gradient: float32 [768], P(('wide', 'narrow'))
- shift_value_gradient: float32 [768], P(('wide', 'narrow'))
- shift_gate_gradient: float32 [768], P(('wide', 'narrow'))
- decay_log_gradient: float32 [768], P(('wide', 'narrow'))
- first_bonus_gradient: float32 [768], P(('wide', 'narrow'))
- mixer_key_gradient: float32 [768, 768], P(('wide', 'narrow'))
- mixer_value_gradient: float32 [768, 768], P(('wide', 'narrow'))
- mixer_gate_gradient: float32 [768, 768], P(('wide', 'narrow'))
- mixer_output_gradient: float32 [768, 768], P(('wide', 'narrow'))
- hidden_shift_gradient: float32 [768], P(('wide', 'narrow'))
- gating_shift_gradient: float32 [768], P(('wide', 'narrow'))
- hidden_key_gradient: float32 [768, 3072], P(('wide', 'narrow'))
- hidden_value_gradient: float32 [3072, 768], P(('wide', 'narrow'))
- hidden_gate_gradient: float32 [768, 768], P(('wide', 'narrow'))
- first_gain_gradient: float32 [768], P(('wide', 'narrow'))
- first_bias_gradient: float32 [768], P(('wide', 'narrow'))
- second_gain_gradient: float32 [768], P(('wide', 'narrow'))
- second_bias_gradient: float32 [768], P(('wide', 'narrow'))
- rms_values: float32 [3], replicated
Inputs may be any that keep to these rules, and one draw needn't show every extreme that they name: `extents_per_device`: row i lists, in order, the lengths of the sequences held by device i of wide+narrow; each row sums to 2048 and its largest entry is 1024.
All inputs are finite; a program needn't handle non-finite values.
Results may differ from a plain program's by a relative error of at most 0.011.
Values may be sent and summed in bfloat16 or wider, within the bound.
A program may use at most 320 MiB of HBM per device.

v0:
```python
import jax
import jax.numpy as jnp
from jax import lax
from jax.sharding import PartitionSpec as P

HIGHEST = lax.Precision.HIGHEST


def product(left, right):
    return jnp.dot(left, right, precision=HIGHEST, preferred_element_type=jnp.float32)


def matmul(left, right):
    return jnp.dot(left, right, preferred_element_type=jnp.float32)


def weight_grad(inputs, upstream):
    return jnp.einsum("nd,nf->df", inputs, upstream, preferred_element_type=jnp.float32)


def input_grad(upstream, coefficient_table):
    return jnp.einsum("nf,df->nd", upstream, coefficient_table, preferred_element_type=jnp.float32)


def token_starts(row_lengths, total_rows):
    offsets = jnp.cumsum(row_lengths) - row_lengths
    places = jnp.arange(total_rows, dtype=jnp.int32)
    chosen = jnp.where(offsets[None, :] <= places[:, None], offsets[None, :], 0)
    return jnp.max(chosen, axis=1)


def norm_rows(inputs, gain_vec, bias_vec):
    centered = inputs - jnp.mean(inputs, axis=1, keepdims=True)
    variance = jnp.mean(centered * centered, axis=1, keepdims=True)
    return centered * lax.rsqrt(variance + 1e-05) * gain_vec + bias_vec


def earlier_rows(inputs, segment_beginnings):
    places = jnp.arange(inputs.shape[0], dtype=jnp.int32)
    moved = jnp.concatenate([jnp.zeros((1, inputs.shape[1]), inputs.dtype), inputs[:-1]], axis=0)
    return moved * (places != segment_beginnings).astype(inputs.dtype)[:, None]


def time_inputs(inputs, gain_vec, bias_vec, mix_key, mix_value, mix_gate, segment_beginnings):
    normed = norm_rows(inputs, gain_vec, bias_vec)
    before = earlier_rows(normed, segment_beginnings)
    return (
        normed * mix_key + before * (1.0 - mix_key),
        normed * mix_value + before * (1.0 - mix_value),
        normed * mix_gate + before * (1.0 - mix_gate),
    )


def channel_inputs(inputs, gain_vec, bias_vec, mix_key, mix_gate, segment_beginnings):
    normed = norm_rows(inputs, gain_vec, bias_vec)
    before = earlier_rows(normed, segment_beginnings)
    return (
        normed * mix_key + before * (1.0 - mix_key),
        normed * mix_gate + before * (1.0 - mix_gate),
    )


def faded_lookup_lines(
    lookup_lines, payload_lines, segment_beginnings, logarithmic_fading_speed, reward_array
):
    total_rows = lookup_lines.shape[0]
    width = lookup_lines.shape[1]
    block_rows = min(128, total_rows)
    blocks = total_rows // block_rows
    rates = jnp.exp(logarithmic_fading_speed)
    local = jnp.arange(block_rows, dtype=jnp.int32)
    local_real = local.astype(jnp.float32)
    growth = jnp.exp((local_real + 1.0)[:, None] * rates)
    shrink = jnp.exp(-local_real[:, None] * rates)
    fading = jnp.exp(-(block_rows - 1.0 - local_real)[:, None] * rates)
    whole_fade = jnp.exp(-block_rows * rates)

    def advance(carried, pieces):
        top_state, bottom_state = carried
        lookup_segment_lines, value_block, start_block, first_row = pieces
        positions = first_row + local
        paired = (
            (local[None, :] < local[:, None]) & (positions[None, :] >= start_block[:, None])
        ).astype(lookup_segment_lines.dtype)
        inherit = (start_block < first_row).astype(lookup_segment_lines.dtype)[:, None]
        key_weight = jnp.exp(lookup_segment_lines)
        key_value = key_weight * value_block
        owned_coefficient_slice = jnp.exp(reward_array + lookup_segment_lines)
        upper = (
            shrink * product(paired, growth * key_value)
            + owned_coefficient_slice * value_block
            + inherit * shrink * top_state
        )
        lower = (
            shrink * product(paired, growth * key_weight)
            + owned_coefficient_slice
            + inherit * shrink * bottom_state
        )
        tail_mask = (positions >= start_block[block_rows - 1]).astype(lookup_segment_lines.dtype)[
            :, None
        ]
        carry_last = inherit[block_rows - 1]
        new_top = (
            jnp.sum(tail_mask * fading * key_value, axis=0) + carry_last * whole_fade * top_state
        )
        new_bottom = (
            jnp.sum(tail_mask * fading * key_weight, axis=0)
            + carry_last * whole_fade * bottom_state
        )
        return ((new_top, new_bottom), upper / lower)

    pieces = (
        lookup_lines.reshape(blocks, block_rows, width),
        payload_lines.reshape(blocks, block_rows, width),
        segment_beginnings.reshape(blocks, block_rows),
        jnp.arange(blocks, dtype=jnp.int32) * block_rows,
    )
    empty_state = jnp.zeros_like(rates)
    unused, outcome = lax.scan(jax.checkpoint(advance), (empty_state, empty_state), pieces)
    return outcome.reshape(total_rows, width)


def body(
    residual_input,
    extents_per_device,
    attention_lookup_lerp,
    attention_payload_lerp,
    attention_receptance_lerp,
    logarithmic_fading_speed,
    present_reward,
    attention_lookup_proj,
    attention_payload_proj,
    attention_receptance_proj,
    attention_result_proj,
    feedforward_lookup_lerp,
    feedforward_receptance_lerp,
    feedforward_lookup_proj,
    feedforward_payload_proj,
    feedforward_receptance_proj,
    first_normalizer_scaling,
    first_normalizer_offset,
    second_normalizer_scaling,
    second_normalizer_offset,
    upstream_adjoint,
):
    assembled_coefficients = (
        lax.all_gather(attention_lookup_lerp, ("wide", "narrow"), axis=0, tiled=True),
        lax.all_gather(attention_payload_lerp, ("wide", "narrow"), axis=0, tiled=True),
        lax.all_gather(attention_receptance_lerp, ("wide", "narrow"), axis=0, tiled=True),
        lax.all_gather(logarithmic_fading_speed, ("wide", "narrow"), axis=0, tiled=True),
        lax.all_gather(present_reward, ("wide", "narrow"), axis=0, tiled=True),
        lax.all_gather(attention_lookup_proj, ("wide", "narrow"), axis=0, tiled=True),
        lax.all_gather(attention_payload_proj, ("wide", "narrow"), axis=0, tiled=True),
        lax.all_gather(attention_receptance_proj, ("wide", "narrow"), axis=0, tiled=True),
        lax.all_gather(attention_result_proj, ("wide", "narrow"), axis=0, tiled=True),
        lax.all_gather(feedforward_lookup_lerp, ("wide", "narrow"), axis=0, tiled=True),
        lax.all_gather(feedforward_receptance_lerp, ("wide", "narrow"), axis=0, tiled=True),
        lax.all_gather(feedforward_lookup_proj, ("wide", "narrow"), axis=0, tiled=True),
        lax.all_gather(feedforward_payload_proj, ("wide", "narrow"), axis=0, tiled=True),
        lax.all_gather(feedforward_receptance_proj, ("wide", "narrow"), axis=0, tiled=True),
        lax.all_gather(first_normalizer_scaling, ("wide", "narrow"), axis=0, tiled=True),
        lax.all_gather(first_normalizer_offset, ("wide", "narrow"), axis=0, tiled=True),
        lax.all_gather(second_normalizer_scaling, ("wide", "narrow"), axis=0, tiled=True),
        lax.all_gather(second_normalizer_offset, ("wide", "narrow"), axis=0, tiled=True),
    )
    key_mix = assembled_coefficients[0].astype(jnp.float32)
    value_mix = assembled_coefficients[1].astype(jnp.float32)
    gate_mix = assembled_coefficients[2].astype(jnp.float32)
    fading_array = assembled_coefficients[3].astype(jnp.float32)
    reward_array = assembled_coefficients[4].astype(jnp.float32)
    feed_mix = assembled_coefficients[9].astype(jnp.float32)
    gating_mix = assembled_coefficients[10].astype(jnp.float32)
    gain_one = assembled_coefficients[14].astype(jnp.float32)
    bias_one = assembled_coefficients[15].astype(jnp.float32)
    gain_two = assembled_coefficients[16].astype(jnp.float32)
    bias_two = assembled_coefficients[17].astype(jnp.float32)
    total_rows = residual_input.shape[0]
    segment_beginnings = token_starts(extents_per_device[0], total_rows)
    inputs = residual_input.astype(jnp.float32)

    def time_piece(source, gain_vec, bias_vec, mix_key, mix_value, mix_gate):
        return time_inputs(
            source, gain_vec, bias_vec, mix_key, mix_value, mix_gate, segment_beginnings
        )

    mixed, time_back = jax.vjp(time_piece, inputs, gain_one, bias_one, key_mix, value_mix, gate_mix)
    key_low = mixed[0].astype(jnp.bfloat16)
    value_low = mixed[1].astype(jnp.bfloat16)
    gate_low = mixed[2].astype(jnp.bfloat16)
    lookup_lines = matmul(key_low, assembled_coefficients[5])
    payload_lines = matmul(value_low, assembled_coefficients[6])
    receptance_lines = matmul(gate_low, assembled_coefficients[7])

    def receptance_piece(lookup_slice, payload_slice, receptance_slice, fading_slice, reward_slice):
        return jax.nn.sigmoid(receptance_slice) * faded_lookup_lines(
            lookup_slice, payload_slice, segment_beginnings, fading_slice, reward_slice
        )

    combined_lerp, gate_gradient_rows = jax.vjp(
        receptance_piece, lookup_lines, payload_lines, receptance_lines, fading_array, reward_array
    )
    blend_low = combined_lerp.astype(jnp.bfloat16)
    attended = matmul(blend_low, assembled_coefficients[8])
    middle = inputs + attended

    def channel_piece(source, gain_vec, bias_vec, mix_key, mix_gate):
        return channel_inputs(source, gain_vec, bias_vec, mix_key, mix_gate, segment_beginnings)

    feeding, channel_back = jax.vjp(channel_piece, middle, gain_two, bias_two, feed_mix, gating_mix)
    feed_low = feeding[0].astype(jnp.bfloat16)
    gating_low = feeding[1].astype(jnp.bfloat16)
    lifted = matmul(feed_low, assembled_coefficients[11])
    squared_low = jnp.square(jax.nn.relu(lifted)).astype(jnp.bfloat16)
    lowered = matmul(squared_low, assembled_coefficients[12])
    gate_in = matmul(gating_low, assembled_coefficients[13])
    gate_sig = jax.nn.sigmoid(gate_in)
    feed_out = gate_sig * lowered
    result = middle + feed_out
    square_sums = jnp.stack(
        [jnp.sum(result * result), jnp.sum(attended * attended), jnp.sum(feed_out * feed_out)]
    )
    totals = lax.psum(square_sums, ("wide", "narrow"))
    entries = total_rows * residual_input.shape[1] * lax.axis_size(("wide", "narrow"))
    rms_values = jnp.sqrt(totals / entries)
    weights = (
        lax.all_gather(attention_lookup_lerp, ("wide", "narrow"), axis=0, tiled=True),
        lax.all_gather(attention_payload_lerp, ("wide", "narrow"), axis=0, tiled=True),
        lax.all_gather(attention_receptance_lerp, ("wide", "narrow"), axis=0, tiled=True),
        lax.all_gather(logarithmic_fading_speed, ("wide", "narrow"), axis=0, tiled=True),
        lax.all_gather(present_reward, ("wide", "narrow"), axis=0, tiled=True),
        lax.all_gather(attention_lookup_proj, ("wide", "narrow"), axis=0, tiled=True),
        lax.all_gather(attention_payload_proj, ("wide", "narrow"), axis=0, tiled=True),
        lax.all_gather(attention_receptance_proj, ("wide", "narrow"), axis=0, tiled=True),
        lax.all_gather(attention_result_proj, ("wide", "narrow"), axis=0, tiled=True),
        lax.all_gather(feedforward_lookup_lerp, ("wide", "narrow"), axis=0, tiled=True),
        lax.all_gather(feedforward_receptance_lerp, ("wide", "narrow"), axis=0, tiled=True),
        lax.all_gather(feedforward_lookup_proj, ("wide", "narrow"), axis=0, tiled=True),
        lax.all_gather(feedforward_payload_proj, ("wide", "narrow"), axis=0, tiled=True),
        lax.all_gather(feedforward_receptance_proj, ("wide", "narrow"), axis=0, tiled=True),
        lax.all_gather(first_normalizer_scaling, ("wide", "narrow"), axis=0, tiled=True),
        lax.all_gather(first_normalizer_offset, ("wide", "narrow"), axis=0, tiled=True),
        lax.all_gather(second_normalizer_scaling, ("wide", "narrow"), axis=0, tiled=True),
        lax.all_gather(second_normalizer_offset, ("wide", "narrow"), axis=0, tiled=True),
    )
    upstream = upstream_adjoint.astype(jnp.float32)
    back_lowered = (upstream * gate_sig).astype(jnp.bfloat16)
    back_gate = (upstream * lowered * gate_sig * (1.0 - gate_sig)).astype(jnp.bfloat16)
    value_grad = weight_grad(squared_low, back_lowered)
    back_squared = input_grad(back_lowered, weights[12])
    back_lifted = (2.0 * jax.nn.relu(lifted) * back_squared).astype(jnp.bfloat16)
    hkey_grad = weight_grad(feed_low, back_lifted)
    hgate_grad = weight_grad(gating_low, back_gate)
    back_feed = input_grad(back_lifted, weights[11])
    back_gating = input_grad(back_gate, weights[13])
    middle_part, gain_two_grad, bias_two_grad, feed_mix_grad, gating_mix_grad = channel_back(
        (back_feed, back_gating)
    )
    back_middle = upstream + middle_part
    back_attended = back_middle.astype(jnp.bfloat16)
    output_grad = weight_grad(blend_low, back_attended)
    blended_mix_gradient = input_grad(back_attended, weights[8])
    (
        key_rows_gradient,
        value_rows_gradient,
        gate_rows_gradient,
        decay_gradient_rows,
        reward_cotangent_lines,
    ) = gate_gradient_rows(blended_mix_gradient)
    keys_low = key_rows_gradient.astype(jnp.bfloat16)
    values_low = value_rows_gradient.astype(jnp.bfloat16)
    gates_low = gate_rows_gradient.astype(jnp.bfloat16)
    mkey_grad = weight_grad(key_low, keys_low)
    mvalue_grad = weight_grad(value_low, values_low)
    mgate_grad = weight_grad(gate_low, gates_low)
    back_key = input_grad(keys_low, weights[5])
    back_value = input_grad(values_low, weights[6])
    back_gate_in = input_grad(gates_low, weights[7])
    source_grad, gain_one_grad, bias_one_grad, key_mix_grad, value_mix_grad, gate_mix_grad = (
        time_back((back_key, back_value, back_gate_in))
    )
    stream_back = (back_middle + source_grad).astype(jnp.bfloat16)
    shards = (
        lax.psum_scatter(key_mix_grad, ("wide", "narrow"), scatter_dimension=0, tiled=True),
        lax.psum_scatter(value_mix_grad, ("wide", "narrow"), scatter_dimension=0, tiled=True),
        lax.psum_scatter(gate_mix_grad, ("wide", "narrow"), scatter_dimension=0, tiled=True),
        lax.psum_scatter(decay_gradient_rows, ("wide", "narrow"), scatter_dimension=0, tiled=True),
        lax.psum_scatter(
            reward_cotangent_lines, ("wide", "narrow"), scatter_dimension=0, tiled=True
        ),
        lax.psum_scatter(mkey_grad, ("wide", "narrow"), scatter_dimension=0, tiled=True),
        lax.psum_scatter(mvalue_grad, ("wide", "narrow"), scatter_dimension=0, tiled=True),
        lax.psum_scatter(mgate_grad, ("wide", "narrow"), scatter_dimension=0, tiled=True),
        lax.psum_scatter(output_grad, ("wide", "narrow"), scatter_dimension=0, tiled=True),
        lax.psum_scatter(feed_mix_grad, ("wide", "narrow"), scatter_dimension=0, tiled=True),
        lax.psum_scatter(gating_mix_grad, ("wide", "narrow"), scatter_dimension=0, tiled=True),
        lax.psum_scatter(hkey_grad, ("wide", "narrow"), scatter_dimension=0, tiled=True),
        lax.psum_scatter(value_grad, ("wide", "narrow"), scatter_dimension=0, tiled=True),
        lax.psum_scatter(hgate_grad, ("wide", "narrow"), scatter_dimension=0, tiled=True),
        lax.psum_scatter(gain_one_grad, ("wide", "narrow"), scatter_dimension=0, tiled=True),
        lax.psum_scatter(bias_one_grad, ("wide", "narrow"), scatter_dimension=0, tiled=True),
        lax.psum_scatter(gain_two_grad, ("wide", "narrow"), scatter_dimension=0, tiled=True),
        lax.psum_scatter(bias_two_grad, ("wide", "narrow"), scatter_dimension=0, tiled=True),
    )
    return (
        result.astype(jnp.bfloat16),
        stream_back,
        shards[0],
        shards[1],
        shards[2],
        shards[3],
        shards[4],
        shards[5],
        shards[6],
        shards[7],
        shards[8],
        shards[9],
        shards[10],
        shards[11],
        shards[12],
        shards[13],
        shards[14],
        shards[15],
        shards[16],
        shards[17],
        rms_values,
    )


def solution(mesh):
    in_specs = (
        P(("wide", "narrow"), None),
        P(("wide", "narrow"), None),
        P(("wide", "narrow")),
        P(("wide", "narrow")),
        P(("wide", "narrow")),
        P(("wide", "narrow")),
        P(("wide", "narrow")),
        P(("wide", "narrow"), None),
        P(("wide", "narrow"), None),
        P(("wide", "narrow"), None),
        P(("wide", "narrow"), None),
        P(("wide", "narrow")),
        P(("wide", "narrow")),
        P(("wide", "narrow"), None),
        P(("wide", "narrow"), None),
        P(("wide", "narrow"), None),
        P(("wide", "narrow")),
        P(("wide", "narrow")),
        P(("wide", "narrow")),
        P(("wide", "narrow")),
        P(("wide", "narrow"), None),
    )
    out_specs = (
        P(("wide", "narrow"), None),
        P(("wide", "narrow"), None),
        P(("wide", "narrow")),
        P(("wide", "narrow")),
        P(("wide", "narrow")),
        P(("wide", "narrow")),
        P(("wide", "narrow")),
        P(("wide", "narrow"), None),
        P(("wide", "narrow"), None),
        P(("wide", "narrow"), None),
        P(("wide", "narrow"), None),
        P(("wide", "narrow")),
        P(("wide", "narrow")),
        P(("wide", "narrow"), None),
        P(("wide", "narrow"), None),
        P(("wide", "narrow"), None),
        P(("wide", "narrow")),
        P(("wide", "narrow")),
        P(("wide", "narrow")),
        P(("wide", "narrow")),
        P(),
    )
    return jax.shard_map(body, mesh=mesh, in_specs=in_specs, out_specs=out_specs, check_vma=False)
```

profile of v0, /device:TPU:0, one launch (start us, length us, event | category | flops | bytes accessed | tf_op | source)
XLA Modules:
  0.0 1243.5 jit_solution(17473528570327738466)
XLA Ops:
  21.2 42.6 %all-reduce.27 = (bf16[768]{0:T(1024)(128)(2,1)S(1)}, bf16[768]{0:T(1024)(128)(2,1)S(1)}, bf16[768]{0:T(1024)(128)(2,1)S(1)}, bf16[768]{0:T(1024)(128)(2,1)S(1)}...) all-reduce(bf16[768]{0:T(1024)(128)(2,1)S(1)} %dynamic-update-slice, ...), channel_id=1, replica_groups=mesh['wide'=8,'narrow'=4] {'wide','narrow'}, use_global_device_ids=true, to_apply=%add.6 | all-reduce | flops 8448 | bytes 33792
  76.1 6.5 add_convert_fusion.3
  82.6 7.5 fusion.102
  90.1 33.5 %all-gather.10.cloned.1.call-done = bf16[768,768]{1,0:T(8,128)(2,1)} async-done(((bf16[24,768]{1,0:T(8,128)(2,1)}), bf16[768,768]{1,0:T(8,128)(2,1)}) %all-gather.10.cloned.1.call-update) | async-done | bytes 1179664 | tf_op jit(solution)/shard_map/all_gather | solution.py:152
  123.7 7.5 fusion.101
  131.1 219.5 %while.56 = (s32[]{:T(128)}, f32[768]{0:T(1024)S(1)}, f32[768]{0:T(1024)S(1)}, f32[16,128,768]{2,1,0:T(8,128)}, f32[16,768]{1,0:T(8,128)}, /*index=5*/f32[16,768...) while((s32[]{:T(128)}, f32[768]{0:T(1024)S(1)}, ...), condition=%wide.region_7.8_spmd.clone.clone.clone.clone, body=%wide.region_4.7_spmd.clone.clone.clone.sunk.clone | while | flops 304845312 | bytes 4436715 | solution.py:119
  350.7 11.1 fusion.83
  361.9 6.5 fusion.98
  373.0 4.7 add_convert_fusion.1
  379.4 15.4 %fusion.103 = f32[2048,3072]{1,0:T(8,128)} fusion(bf16[2048,768]{1,0:T(8,128)(2,1)S(1)} %get-tuple-element.1146, bf16[768,3072]{1,0:T(8,128)(2,1)} %all-gather.18.cloned.1.call-done), kind=kOutput, calls=%fused_computation.219 | convolution fusion | flops 9663676416 | bytes 33030144 | tf_op jit(solution)/shard_map/dot_general | solution.py:14
  394.8 18.0 %fusion.86 = f32[2048,768]{1,0:T(8,128)} fusion(bf16[3072,768]{1,0:T(8,128)(2,1)} %all-gather.20.cloned.1.call-done, f32[2048,3072]{1,0:T(8,128)} %fusion.103), kind=kOutput, calls=%fused_computation.170 | convolution fusion | flops 9682550784 | bytes 36175872 | tf_op jit(solution)/shard_map/dot_general | solution.py:14
  412.8 9.0 all-gather.16.cloned.1.call-done
  421.7 10.5 fusion.74
  438.1 7.2 fusion.104
  445.3 23.6 %multiply_convert_fusion = bf16[2048,3072]{1,0:T(8,128)(2,1)} fusion(f32[2048,3072]{1,0:T(8,128)} %fusion.103, bf16[3072,768]{1,0:T(8,128)(2,1)} %all-gather.20.cloned.1.call-done, f32[2048,768]{1,0:T(8,128)} %get-tuple-element.1168, bf16[2048,768]{1,0:T(8,128)(2,1)} %param.45), kind=kOutput, calls=%fused_computation.99 | convolution fusion | flops 9693560832 | bytes 51904512 | tf_op jit(solution)/shard_map/nf,df->nd/dot_general | solution.py:22
  468.9 14.6 %fusion.105 = f32[2048,768]{1,0:T(8,128)S(1)} fusion(bf16[2048,3072]{1,0:T(8,128)(2,1)} %multiply_convert_fusion, bf16[768,3072]{1,0:T(8,128)(2,1)} %all-gather.18.cloned.1.call-done), kind=kOutput, calls=%fused_computation.221 | convolution fusion | flops 9663676416 | bytes 23592960 | tf_op jit(solution)/shard_map/nf,df->nd/dot_general | solution.py:22
  491.2 16.0 %multiply_reduce_fusion.7 = (f32[768]{0:T(1024)S(1)}, f32[768]{0:T(1024)S(1)}, f32[768]{0:T(1024)S(1)}, f32[768]{0:T(1024)S(1)}, bf16[2048,768]{1,0:T(8,128)(2,1...) fusion(f32[2048,768]{1,0:T(8,128)S(1)} %copy-done.11, ...), kind=kLoop, calls=%fused_computation.144 | loop fusion | flops 47179264 | bytes 53534728 | tf_op jit(solution)/shard_map/transpose(jvp())/reduce_sum | solution.py:59
  512.8 9.7 fusion.99
  537.7 191.1 %while.57 = (s32[]{:T(128)}, f32[768]{0:T(1024)S(1)}, f32[128,768]{1,0:T(8,128)S(1)}, f32[128,768]{1,0:T(8,128)S(1)}, f32[128,768]{1,0:T(8,128)S(1)}, /*index=5*...) while((s32[]{:T(128)}, f32[768]{0:T(1024)S(1)}, ...), condition=%wide.region_16.17_spmd.clone.clone.clone.clone, body=%wide.region_12.16_spmd.clone.clone.clone.sunk.clone | while | flops 611657344 | bytes 18209584 | solution.py:119
  728.9 6.9 fusion.110
  735.8 6.9 fusion.109
  742.9 20.1 %fusion.85 = f32[3072,768]{1,0:T(8,128)} fusion(f32[2048,3072]{1,0:T(8,128)} %fusion.103, f32[2048,768]{1,0:T(8,128)} %get-tuple-element.1168, bf16[2048,768]{1,0:T(8,128)(2,1)} %param.45), kind=kOutput, calls=%fused_computation.169 | convolution fusion | flops 9687269376 | bytes 44040192 | tf_op jit(solution)/shard_map/nd,nf->df/dot_general | solution.py:18
  763.1 16.6 %fusion.113 = f32[768,3072]{1,0:T(8,128)} fusion(bf16[2048,768]{1,0:T(8,128)(2,1)} %copy-done.22, bf16[2048,3072]{1,0:T(8,128)(2,1)} %multiply_convert_fusion), kind=kOutput, calls=%fused_computation.229 | convolution fusion | flops 9663676416 | bytes 25165824 | tf_op jit(solution)/shard_map/nd,nf->df/dot_general | solution.py:18
  782.1 5.1 fusion.107
  797.2 4.7 fusion.79
  802.0 10.2 fusion.95
  812.3 12.9 %multiply_reduce_fusion.11 = (f32[768]{0:T(1024)S(1)}, f32[768]{0:T(1024)S(1)}, f32[768]{0:T(1024)S(1)}, f32[768]{0:T(1024)S(1)}, f32[768]{0:T(1024)S(1)}, /*ind...) fusion(f32[2048,768]{1,0:T(8,128)} %copy-done.9, f32[2048]{0:T(1024)S(1)} %fusion.87, ...), kind=kLoop, calls=%fused_computation.148 | loop fusion | flops 40887040 | bytes 34668544 | tf_op jit(solution)/shard_map/transpose(jvp())/reduce_sum | solution.py:50
  825.3 40.4 %all-reduce.26 = (f32[768]{0:T(1024)S(1)}, f32[768]{0:T(1024)S(1)}, f32[768]{0:T(1024)S(1)}, f32[768]{0:T(1024)S(1)}, f32[768]{0:T(1024)S(1)}, /*index=5*/f32[76...) all-reduce(f32[768]{0:T(1024)S(1)} %negate_add_fusion.4, ...), channel_id=2, replica_groups=mesh['wide'=8,'narrow'=4] {'wide','narrow'}, use_global_device_ids=true, to_apply=%region_21.22.clone | all-reduce | flops 8451 | bytes 67608
  872.7 9.0 add_convert_fusion
  881.7 71.7 %reduce-scatter.8.cloned.1.call-done = f32[24,768]{1,0:T(8,128)} async-done(((f32[768,768]{1,0:T(8,128)}), f32[24,768]{1,0:T(8,128)}) %reduce-scatter.8.cloned.1.call-update) | async-done | bytes 73744 | tf_op jit(solution)/shard_map/reduce_scatter | solution.py:290
  953.5 142.1 %reduce-scatter.18.cloned.1.call-done = f32[96,768]{1,0:T(8,128)} async-done(((f32[3072,768]{1,0:T(8,128)}), f32[96,768]{1,0:T(8,128)}) %reduce-scatter.18.cloned.1.call-update) | async-done | bytes 294928 | tf_op jit(solution)/shard_map/reduce_scatter | solution.py:297
  1095.6 140.9 %reduce-scatter.16.cloned.1.call-done = f32[24,3072]{1,0:T(8,128)} async-done(((f32[768,3072]{1,0:T(8,128)}), f32[24,3072]{1,0:T(8,128)}) %reduce-scatter.16.cloned.1.call-update) | async-done | bytes 294928 | tf_op jit(solution)/shard_map/reduce_scatter | solution.py:296
  (831 shorter events, 493.4 us)
Async XLA Ops:
  7.2 65.1 %copy-start.1 = (bf16[2048,768]{1,0:T(8,128)(2,1)S(1)}, bf16[2048,768]{1,0:T(8,128)(2,1)}, u32[]{:S(2)}) copy-start(bf16[2048,768]{1,0:T(8,128)(2,1)} %param.25) | copy-start | bytes 9437188
  7.2 75.4 %all-gather.12.cloned.1.call-start = ((), (), s32[]{:S(2)}) async-start(), calls=%async_computation.9 | async-start | bytes 1216512 | tf_op jit(solution)/shard_map/all_gather | solution.py:153
  7.9 115.7 %all-gather.10.cloned.1.call-start = ((), (), s32[]{:S(2)}) async-start(), calls=%async_computation.8 | async-start | bytes 1216512 | tf_op jit(solution)/shard_map/all_gather | solution.py:152
  8.7 342.1 %all-gather.8.cloned.1.call-start = ((), (), s32[]{:S(2)}) async-start(), calls=%async_computation.7 | async-start | bytes 1216512 | tf_op jit(solution)/shard_map/all_gather | solution.py:154
  9.4 352.5 %all-gather.14.cloned.1.call-start = ((), (), s32[]{:S(2)}) async-start(), calls=%async_computation.10 | async-start | bytes 1216512 | tf_op jit(solution)/shard_map/all_gather | solution.py:155
  10.0 367.7 %all-gather.18.cloned.1.call-start = ((), (), s32[]{:S(2)}) async-start(), calls=%async_computation.12 | async-start | bytes 4866048 | tf_op jit(solution)/shard_map/all_gather | solution.py:158
  10.6 384.2 %all-gather.20.cloned.1.call-start = ((), (), s32[]{:S(2)}) async-start(), calls=%async_computation.13 | async-start | bytes 4866048 | tf_op jit(solution)/shard_map/all_gather | solution.py:159
  11.2 410.6 %all-gather.16.cloned.1.call-start = ((), (), s32[]{:S(2)}) async-start(), calls=%async_computation.11 | async-start | bytes 1216512 | tf_op jit(solution)/shard_map/all_gather | solution.py:160
  11.9 869.8 %reduce-scatter.20.cloned.1.call-start = ((), (), s32[]{:S(2)}) async-start(), calls=%async_computation.20 | async-start | bytes 2433024 | tf_op jit(solution)/shard_map/reduce_scatter | solution.py:298
  350.6 11.2 copy-start.25
  350.6 11.2 copy-start.27
  350.7 11.2 copy-start.40
  350.7 11.2 copy-start.42
  350.7 11.2 copy-start.55
  350.7 11.2 copy-start.57
  350.7 11.2 copy-start.66
  394.8 27.0 %copy-start.17 = (bf16[2048,768]{1,0:T(8,128)(2,1)S(1)}, bf16[2048,768]{1,0:T(8,128)(2,1)}, u32[]{:S(2)}) copy-start(bf16[2048,768]{1,0:T(8,128)(2,1)} %param.45) | copy-start | bytes 9437188
  421.7 12.1 copy-start.23
  438.0 443.6 %reduce-scatter.12.cloned.1.call-start = ((), (), s32[]{:S(2)}) async-start(), calls=%async_computation.16 | async-start | bytes 2433024 | tf_op jit(solution)/shard_map/reduce_scatter | solution.py:292
  445.3 45.0 %slice-start = ((s8[6291456]{0:T(1024)(128)(4,1)}), s8[2097152]{0:T(1024)(128)(4,1)S(1)}, s32[]{:S(2)}) async-start(s8[6291456]{0:T(1024)(128)(4,1)} %bitcast.173), calls=%async_computation.21 | async-start | bytes 4194304
  468.9 17.3 %copy-start.10 = (f32[2048,768]{1,0:T(8,128)S(1)}, f32[2048,768]{1,0:T(8,128)}, u32[]{:S(2)}) copy-start(f32[2048,768]{1,0:T(8,128)} %fusion.104) | copy-start | bytes 18874372
  468.9 17.3 %copy-start.35 = (f32[2047]{0:T(1024)S(1)}, f32[2047]{0:T(1024)}, u32[]{:S(2)}) copy-start(f32[2047]{0:T(1024)} %slice.49) | copy-start | bytes 24568
  468.9 21.3 %slice-start.1 = ((s8[6291456]{0:T(1024)(128)(4,1)}), s8[4194304]{0:T(1024)(128)(4,1)S(1)}, s32[]{:S(2)}) async-start(s8[6291456]{0:T(1024)(128)(4,1)} %bitcast.173), calls=%async_computation.22 | async-start | bytes 8388608
  512.8 11.3 copy-start.21
  528.2 353.5 %reduce-scatter.14.cloned.1.call-start = ((), (), s32[]{:S(2)}) async-start(), calls=%async_computation.17 | async-start | bytes 2433024 | tf_op jit(solution)/shard_map/reduce_scatter | solution.py:293
  537.6 344.1 %reduce-scatter.10.cloned.1.call-start = ((), (), s32[]{:S(2)}) async-start(), calls=%async_computation.15 | async-start | bytes 2433024 | tf_op jit(solution)/shard_map/reduce_scatter | solution.py:291
  735.8 217.7 %reduce-scatter.8.cloned.1.call-start = ((), (), s32[]{:S(2)}) async-start(), calls=%async_computation.14 | async-start | bytes 2433024 | tf_op jit(solution)/shard_map/reduce_scatter | solution.py:290
  742.8 352.8 %reduce-scatter.18.cloned.1.call-start = ((), (), s32[]{:S(2)}) async-start(), calls=%async_computation.19 | async-start | bytes 9732096 | tf_op jit(solution)/shard_map/reduce_scatter | solution.py:297
  763.0 473.5 %reduce-scatter.16.cloned.1.call-start = ((), (), s32[]{:S(2)}) async-start(), calls=%async_computation.18 | async-start | bytes 9732096 | tf_op jit(solution)/shard_map/reduce_scatter | solution.py:296
  797.2 15.0 %slice-start.2 = ((s8[6291456]{0:T(1024)(128)(4,1)}), s8[4194304]{0:T(1024)(128)(4,1)S(1)}, s32[]{:S(2)}) async-start(s8[6291456]{0:T(1024)(128)(4,1)} %bitcast.176), calls=%async_computation.23 | async-start | bytes 8388608
  812.2 13.0 %copy-start.6 = (f32[2048,768]{1,0:T(8,128)}, f32[2048,768]{1,0:T(8,128)S(1)}, u32[]{:S(2)}) copy-start(f32[2048,768]{1,0:T(8,128)S(1)} %get-tuple-element.1120) | copy-start | bytes 18874372
  812.3 13.0 %copy-start.62 = (bf16[768]{0:T(1024)(128)(2,1)S(1)}, bf16[768]{0:T(1024)(128)(2,1)}, u32[]{:S(2)}) copy-start(bf16[768]{0:T(1024)(128)(2,1)} %copy-done.61) | copy-start | bytes 4612
  (56 other events, 301.5 us)
Sparse Core Ops, SparseCore 0:
  10.9 56.7 all-gather.11
  70.6 52.9 all-gather.9
  126.6 53.0 all-gather.7
  182.4 52.8 all-gather.13
  238.1 62.5 all-gather.17
  303.4 62.5 all-gather.19
  368.9 52.8 all-gather.15
  438.2 97.9 reduce-scatter.19
  542.9 97.9 reduce-scatter.11
  646.7 98.0 reduce-scatter.13
  751.5 98.1 reduce-scatter.9
  855.4 98.0 reduce-scatter.7
  960.9 134.5 reduce-scatter.17
  1101.9 134.5 reduce-scatter.15
where the time goes:
time: 1250 us; the launch traced here: 1240 us
  waiting for transfers between devices  402 us (32%)
  matrix products  317 us (25%)
  other arithmetic  222 us (18%)
  local copies, waits for them, and re-layouts  200 us (16%)
  blocking collectives  83 us (7%)
  between operations  15.7 us (1%)
    reduce_scatter x1, waiting for transfers between devices, body(): lax.psum_scatter(value_grad, ('wide', 'narrow'), scatter_dimension=0, til...  142 us
    reduce_scatter x1, waiting for transfers between devices, body(): lax.psum_scatter(hkey_grad, ('wide', 'narrow'), scatter_dimension=0, tile...  141 us
    dot_general x96, matrix products, product(): jnp.dot(left, right, precision=HIGHEST, preferred_element_type=jnp.float32)  112 us
    unnamed x2, blocking collectives  83 us
    dot_general x7, matrix products, matmul(): return jnp.dot(left, right, preferred_element_type=jnp.float32)  76.4 us
    reduce_scatter x1, waiting for transfers between devices, body(): lax.psum_scatter(mkey_grad, ('wide', 'narrow'), scatter_dimension=0, tile...  71.7 us
    dot_general x7, matrix products, input_grad(): jnp.einsum('nf,df->nd', upstream, coefficient_table, preferred_element_ty...  65.6 us
    dot_general x7, matrix products, weight_grad(): jnp.einsum('nd,nf->df', inputs, upstream, preferred_element_type=jnp.floa...  62.9 us
  transfers between devices with their start and end apart: 14, of which 5 were waited for; matrix products, arithmetic and copies ran while one was open for 56% of the time, Pallas kernels for 0%

commit v1 on v0

v1 whole, which is shorter than its diff:
```python
import functools

import jax
import jax.numpy as jnp
from jax import lax
from jax.experimental import pallas as pl
from jax.experimental.pallas import tpu as pltpu
from jax.sharding import PartitionSpec as P

F32 = jnp.float32
LOW = jnp.bfloat16
AXES = ("wide", "narrow")
BLOCK = 128
EDGE = 8
MIB = 2**20

(KEY_MIX, VALUE_MIX, GATE_MIX, FADING, REWARD, FEED_MIX, GATING_MIX, GAIN_ONE, BIAS_ONE, GAIN_TWO, BIAS_TWO) = range(11)
VECTORS = 16


def dot(left, right):
    return jnp.dot(left, right, preferred_element_type=F32)


def dot_nt(left, right):
    return lax.dot_general(left, right, (((1,), (1,)), ((), ())), preferred_element_type=F32)


def dot_tn(left, right):
    return lax.dot_general(left, right, (((0,), (0,)), ((), ())), preferred_element_type=F32)


def offsets_of(extents):
    offsets, total = [], 0
    for j in range(extents.shape[1] - 1):
        total = total + extents[0, j]
        offsets.append(total)
    return offsets


def start_of(places, offsets):
    begun = jnp.zeros_like(places)
    for offset in offsets:
        begun = jnp.where(places >= offset, offset, begun)
    return begun


def normed(x):
    centered = x - jnp.mean(x, axis=1, keepdims=True)
    scale = lax.rsqrt(jnp.mean(centered * centered, axis=1, keepdims=True) + 1e-05)
    return centered * scale, scale


def fold(x):
    return jnp.sum(x.reshape(x.shape[0] // 8, 8, x.shape[1]), axis=0)


def rows_of(shape, axis=0):
    return lax.broadcasted_iota(jnp.int32, shape, axis)


def shift_down(x, first, keep):
    return jnp.where(rows_of((x.shape[0], 1)) == 0, first, pltpu.roll(x, 1, 0)) * keep


def shift_up(x, last):
    rows = x.shape[0]
    return jnp.where(rows_of((rows, 1)) == rows - 1, last, pltpu.roll(x, rows - 1, 0))


def split(top, bottom):
    both = jnp.concatenate([top, bottom], axis=1)
    high = both.astype(LOW)
    low = (both - high.astype(F32)).astype(LOW)
    return jnp.concatenate([high, low], axis=0)


def norm_grad(back_normed, hat, scale, gain):
    back_hat = back_normed * gain
    return scale * (
        back_hat
        - jnp.mean(back_hat, axis=1, keepdims=True)
        - hat * jnp.mean(back_hat * hat, axis=1, keepdims=True)
    )


def vec(vectors, row):
    return vectors[row : row + 1, :]


def front_kernel(
    extents, vectors, x_ref, wk, wv, wr, wo,
    k_out, v_out, s_out, y_out, d_out, blend_out, mid_out, state_out, square_out,
    grow, shrink, last, state,
):
    tile = pl.program_id(0)
    rows, width = x_ref.shape
    half = BLOCK // 2
    offsets = offsets_of(extents)
    rate = jnp.exp(vec(vectors, FADING))

    @pl.when(tile == 0)
    def _():
        local = rows_of((BLOCK + EDGE, 1)).astype(F32)
        shrink[...] = jnp.exp((half - local) * rate)
        grow[...] = jnp.exp((local[:BLOCK] + (1 - half)) * rate)
        last[...] = jnp.zeros_like(last)
        state[...] = jnp.zeros_like(state)
        square_out[...] = jnp.zeros_like(square_out)

    x = x_ref[...].astype(F32)
    hat, _ = normed(x)
    norm = hat * vec(vectors, GAIN_ONE) + vec(vectors, BIAS_ONE)
    places = tile * rows + rows_of((rows, 1))
    keep = (places != start_of(places, offsets)).astype(F32)
    before = shift_down(norm, last[0:1, :], keep)
    last[0:1, :] = norm[rows - 1 : rows, :]

    def mixed(row):
        mix = vec(vectors, row)
        return (norm * mix + before * (1.0 - mix)).astype(LOW)

    keys = dot(mixed(KEY_MIX), wk[...])
    values = dot(mixed(VALUE_MIX), wv[...])
    sig = jax.nn.sigmoid(dot(mixed(GATE_MIX), wr[...]))
    k_out[...] = keys
    v_out[...] = values
    s_out[...] = sig
    fade_half = jnp.exp(-half * rate)
    reward = vec(vectors, REWARD)
    for block in range(rows // BLOCK):
        here = slice(block * BLOCK, (block + 1) * BLOCK)
        key, value = keys[here], values[here]
        weight = grow[...] * jnp.exp(key)
        first = tile * rows + block * BLOCK
        after = first + rows_of((BLOCK + EDGE, 1))
        column = rows_of((1, 2 * BLOCK), 1)
        source = first + jnp.where(column >= BLOCK, column - BLOCK, column)
        begun = start_of(after, offsets)
        paired = ((source < after) & (source >= begun)).astype(LOW)
        sums = dot(paired, split(weight * value, weight))
        inherit = (begun < first).astype(F32)
        top = shrink[...] * (sums[:, :width] + inherit * (fade_half * state[0:1, :]))
        bottom = shrink[...] * (sums[:, width:] + inherit * (fade_half * state[1:2, :]))
        state[0:1, :] = top[BLOCK : BLOCK + 1]
        state[1:2, :] = bottom[BLOCK : BLOCK + 1]
        state_out[block, :, :] = state[...]
        own = jnp.exp(reward + key)
        inverse = 1.0 / (bottom[:BLOCK] + own)
        wkv = (top[:BLOCK] + own * value) * inverse
        y_out[here, :] = wkv
        d_out[here, :] = inverse
        blend_out[here, :] = (sig[here] * wkv).astype(LOW)
    attended = dot(blend_out[...], wo[...])
    mid_out[...] = x + attended
    square_out[...] += fold(attended * attended)


def feed_kernel(
    extents, vectors, mid_ref, edge_ref, up_ref, w1, w2, wg,
    out_out, back_out, fk_out, fg_out, sq_out, bl_out, bg_out, lift_out, sums_out,
    lift, carry,
):
    step = pl.program_id(0)
    tile = pl.num_programs(0) - 1 - step
    rows, width = mid_ref.shape
    hidden = w1.shape[1]
    offsets = offsets_of(extents)

    @pl.when(step == 0)
    def _():
        carry[...] = jnp.zeros_like(carry)
        sums_out[...] = jnp.zeros_like(sums_out)

    gain, bias = vec(vectors, GAIN_TWO), vec(vectors, BIAS_TWO)
    mid = mid_ref[...]
    hat, scale = normed(mid)
    norm = hat * gain + bias
    edge_hat, _ = normed(edge_ref[...])
    edge = (edge_hat * gain + bias)[EDGE - 1 : EDGE]
    places = tile * rows + rows_of((rows, 1))
    keep = (places != start_of(places, offsets)).astype(F32)
    before = shift_down(norm, edge, keep)
    mix_k, mix_g = vec(vectors, FEED_MIX), vec(vectors, GATING_MIX)
    feed_key = (norm * mix_k + before * (1.0 - mix_k)).astype(LOW)
    feed_gate = (norm * mix_g + before * (1.0 - mix_g)).astype(LOW)
    fk_out[...] = feed_key
    fg_out[...] = feed_gate
    lowered = None
    for j in range(hidden // width):
        chunk = slice(j * width, (j + 1) * width)
        lifted = jnp.maximum(dot(feed_key, w1[:, chunk]), 0.0)
        lift[:, chunk] = lifted
        squared = (lifted * lifted).astype(LOW)
        sq_out[:, chunk] = squared
        part = dot(squared, w2[chunk, :])
        lowered = part if lowered is None else lowered + part
    sig = jax.nn.sigmoid(dot(feed_gate, wg[...]))
    feed_out = sig * lowered
    result = mid + feed_out
    out_out[...] = result.astype(LOW)
    upstream = up_ref[...].astype(F32)
    back_lowered = (upstream * sig).astype(LOW)
    back_gate = (upstream * lowered * sig * (1.0 - sig)).astype(LOW)
    bl_out[...] = back_lowered
    bg_out[...] = back_gate
    back_key = None
    for j in range(hidden // width):
        chunk = slice(j * width, (j + 1) * width)
        back_lifted = (2.0 * lift[:, chunk] * dot_nt(back_lowered, w2[chunk, :])).astype(LOW)
        lift_out[:, chunk] = back_lifted
        part = dot_nt(back_lifted, w1[:, chunk])
        back_key = part if back_key is None else back_key + part
    back_gating = dot_nt(back_gate, wg[...])
    late = norm - before
    back_before = keep * (back_key * (1.0 - mix_k) + back_gating * (1.0 - mix_g))
    back_norm = back_key * mix_k + back_gating * mix_g + shift_up(back_before, carry[0:1, :])
    carry[0:1, :] = back_before[0:1]
    back_out[...] = upstream + norm_grad(back_norm, hat, scale, gain)
    for row, piece in enumerate(
        (back_key * late, back_gating * late, back_norm * hat, back_norm, result * result, feed_out * feed_out)
    ):
        sums_out[8 * row : 8 * row + 8, :] += fold(piece)


def back_kernel(
    extents, vectors, x_ref, edge_ref, k_ref, v_ref, s_ref, y_ref, d_ref, state_ref, mid_ref, wk, wv, wr, wo,
    stream_out, ba_out, bk_out, bv_out, bg_out, mk_out, mv_out, mg_out, sums_out,
    grow, shrink, carry, state,
):
    step = pl.program_id(0)
    tile = pl.num_programs(0) - 1 - step
    rows, width = x_ref.shape
    half = BLOCK // 2
    offsets = offsets_of(extents)
    rate = jnp.exp(vec(vectors, FADING))

    @pl.when(step == 0)
    def _():
        local = rows_of((BLOCK + EDGE, 1)).astype(F32)
        shrink[...] = jnp.exp((half - local[:BLOCK]) * rate)
        grow[...] = jnp.exp((local + (1 - EDGE - half)) * rate)
        carry[...] = jnp.zeros_like(carry)
        state[...] = jnp.zeros_like(state)
        sums_out[...] = jnp.zeros_like(sums_out)

    back_mid = mid_ref[...]
    back_attended = back_mid.astype(LOW)
    ba_out[...] = back_attended
    back_blend = dot_nt(back_attended, wo[...])
    sig = s_ref[...]
    wkv = y_ref[...]
    bg_out[...] = (back_blend * wkv * sig * (1.0 - sig)).astype(LOW)
    back_top = back_blend * sig * d_ref[...]
    fade_half = jnp.exp(-half * rate)
    reward = vec(vectors, REWARD)
    for block in reversed(range(rows // BLOCK)):
        here = slice(block * BLOCK, (block + 1) * BLOCK)
        key, value = k_ref[here, :], v_ref[here, :]
        first = tile * rows + block * BLOCK
        source = first - EDGE + rows_of((BLOCK + EDGE, 1))
        column = rows_of((1, 2 * BLOCK), 1)
        after = first + jnp.where(column >= BLOCK, column - BLOCK, column)
        paired = ((source < after) & (source >= start_of(after, offsets))).astype(LOW)
        bt = back_top[here]
        weighted = shrink[...] * bt
        sums = dot(paired, split(weighted, -weighted * wkv[here]))
        following = start_of(first + BLOCK + jnp.zeros((1, 1), jnp.int32), offsets)
        tail = (source >= following).astype(F32)
        top = grow[...] * (sums[:, :width] + tail * (fade_half * state[0:1, :]))
        bottom = grow[...] * (sums[:, width:] + tail * (fade_half * state[1:2, :]))
        crossing = state_ref[block, :, :] * state[...]
        sums_out[32:40, :] += jnp.where(rows_of((8, 1)) < 2, crossing * (-1.0 * BLOCK), 0.0)
        state[0:1, :] = top[EDGE - 1 : EDGE]
        state[1:2, :] = bottom[EDGE - 1 : EDGE]
        weight = jnp.exp(key)
        own = jnp.exp(reward + key) * bt
        passed = weight * (value * top[EDGE:] + bottom[EDGE:])
        bonus = own * (value - wkv[here])
        back_key = passed + bonus
        bk_out[here, :] = back_key.astype(LOW)
        bv_out[here, :] = (weight * top[EDGE:] + own).astype(LOW)
        local = rows_of((BLOCK, 1)).astype(F32)
        sums_out[24:32, :] += fold(bonus)
        sums_out[32:40, :] += fold(local * back_key + passed)

    gain, bias = vec(vectors, GAIN_ONE), vec(vectors, BIAS_ONE)
    hat, scale = normed(x_ref[...].astype(F32))
    norm = hat * gain + bias
    edge_hat, _ = normed(edge_ref[...].astype(F32))
    edge = (edge_hat * gain + bias)[edge_ref.shape[0] - 1 : edge_ref.shape[0]]
    places = tile * rows + rows_of((rows, 1))
    keep = (places != start_of(places, offsets)).astype(F32)
    before = shift_down(norm, edge, keep)
    late = norm - before
    back_norm, back_before = None, None
    for number, (mix_row, back_ref, weights, mixed_ref) in enumerate(
        ((KEY_MIX, bk_out, wk, mk_out), (VALUE_MIX, bv_out, wv, mv_out), (GATE_MIX, bg_out, wr, mg_out))
    ):
        mix = vec(vectors, mix_row)
        mixed_ref[...] = (norm * mix + before * (1.0 - mix)).astype(LOW)
        back_mixed = dot_nt(back_ref[...], weights[...])
        sums_out[8 * number : 8 * number + 8, :] += fold(back_mixed * late)
        one, two = back_mixed * mix, back_mixed * (1.0 - mix)
        back_norm = one if back_norm is None else back_norm + one
        back_before = two if back_before is None else back_before + two
    back_before = back_before * keep
    back_norm = back_norm + shift_up(back_before, carry[0:1, :])
    carry[0:1, :] = back_before[0:1]
    sums_out[40:48, :] += fold(back_norm * hat)
    sums_out[48:56, :] += fold(back_norm)
    stream_out[...] = (back_mid + norm_grad(back_norm, hat, scale, gain)).astype(LOW)


def whole(shape):
    return pl.BlockSpec(shape, lambda i: (0,) * len(shape), pipeline_mode=pl.Buffered(1))


def kept(shape):
    return pl.BlockSpec(shape, lambda i: (0,) * len(shape))


def smem():
    return pl.BlockSpec(memory_space=pltpu.SMEM)


def front(extents, vectors, x, wk, wv, wr, wo, rows):
    tokens, width = x.shape
    tiles, blocks = tokens // rows, rows // BLOCK
    tile = pl.BlockSpec((rows, width), lambda i: (i, 0))
    wide = jax.ShapeDtypeStruct((tokens, width), F32)
    low = jax.ShapeDtypeStruct((tokens, width), LOW)
    return pl.pallas_call(
        front_kernel,
        name="front",
        grid=(tiles,),
        in_specs=[smem(), whole(vectors.shape), tile] + [whole((width, width))] * 4,
        out_specs=[tile] * 7 + [pl.BlockSpec((blocks, 8, width), lambda i: (i, 0, 0)), kept((8, width))],
        out_shape=[wide] * 5
        + [
            low,
            wide,
            jax.ShapeDtypeStruct((tokens // BLOCK, 8, width), F32),
            jax.ShapeDtypeStruct((8, width), F32),
        ],
        scratch_shapes=[
            pltpu.VMEM((BLOCK, width), F32),
            pltpu.VMEM((BLOCK + EDGE, width), F32),
            pltpu.VMEM((8, width), F32),
            pltpu.VMEM((8, width), F32),
        ],
        compiler_params=pltpu.CompilerParams(vmem_limit_bytes=56 * MIB),
    )(extents, vectors, x, wk, wv, wr, wo)


def feed(extents, vectors, mid, upstream, w1, w2, wg, rows):
    tokens, width = mid.shape
    hidden = w1.shape[1]
    tiles = tokens // rows
    tile = pl.BlockSpec((rows, width), lambda i: (tiles - 1 - i, 0))
    deep = pl.BlockSpec((rows, hidden), lambda i: (tiles - 1 - i, 0))
    edge = pl.BlockSpec((EDGE, width), lambda i: (jnp.maximum((tiles - 1 - i) * (rows // EDGE) - 1, 0), 0))
    wide = jax.ShapeDtypeStruct((tokens, width), F32)
    low = jax.ShapeDtypeStruct((tokens, width), LOW)
    low_deep = jax.ShapeDtypeStruct((tokens, hidden), LOW)
    return pl.pallas_call(
        feed_kernel,
        name="feed",
        grid=(tiles,),
        in_specs=[smem(), whole(vectors.shape), tile, edge, tile, whole(w1.shape), whole(w2.shape), whole(wg.shape)],
        out_specs=[tile, tile, tile, tile, deep, tile, tile, deep, kept((48, width))],
        out_shape=[low, wide, low, low, low_deep, low, low, low_deep, jax.ShapeDtypeStruct((48, width), F32)],
        scratch_shapes=[pltpu.VMEM((rows, hidden), F32), pltpu.VMEM((8, width), F32)],
        compiler_params=pltpu.CompilerParams(vmem_limit_bytes=60 * MIB),
    )(extents, vectors, mid, mid, upstream, w1, w2, wg)


def back(extents, vectors, x, saved, states, back_mid, wk, wv, wr, wo, rows):
    tokens, width = x.shape
    tiles, blocks = tokens // rows, rows // BLOCK
    tile = pl.BlockSpec((rows, width), lambda i: (tiles - 1 - i, 0))
    edge = pl.BlockSpec((16, width), lambda i: (jnp.maximum((tiles - 1 - i) * (rows // 16) - 1, 0), 0))
    low = jax.ShapeDtypeStruct((tokens, width), LOW)
    return pl.pallas_call(
        back_kernel,
        name="back",
        grid=(tiles,),
        in_specs=[smem(), whole(vectors.shape), tile, edge]
        + [tile] * 5
        + [pl.BlockSpec((blocks, 8, width), lambda i: (tiles - 1 - i, 0, 0)), tile]
        + [whole((width, width))] * 4,
        out_specs=[tile] * 8 + [kept((56, width))],
        out_shape=[low] * 8 + [jax.ShapeDtypeStruct((56, width), F32)],
        scratch_shapes=[
            pltpu.VMEM((BLOCK + EDGE, width), F32),
            pltpu.VMEM((BLOCK, width), F32),
            pltpu.VMEM((8, width), F32),
            pltpu.VMEM((8, width), F32),
        ],
        compiler_params=pltpu.CompilerParams(vmem_limit_bytes=56 * MIB),
    )(extents, vectors, x, x, *saved, states, back_mid, wk, wv, wr, wo)


def layer(extents, vectors, x, upstream, wk, wv, wr, wo, w1, w2, wg):
    tokens, width = x.shape
    rows = min(256, tokens)
    *saved, blend, mid, states, attended_square = front(extents, vectors, x, wk, wv, wr, wo, rows)
    outcome, back_mid, fk, fg, sq, bl, bgate, lift, sums_two = feed(extents, vectors, mid, upstream, w1, w2, wg, rows)
    stream, ba, bk, bv, bg, mk, mv, mg, sums_one = back(
        extents, vectors, x, saved, states, back_mid, wk, wv, wr, wo, rows
    )
    grads = [dot_tn(mk, bk), dot_tn(mv, bv), dot_tn(mg, bg), dot_tn(blend, ba)]
    grads += [dot_tn(fk, lift), dot_tn(sq, bl), dot_tn(fg, bgate)]
    one = jnp.sum(sums_one.reshape(7, 8, width), axis=1)
    two = jnp.sum(sums_two.reshape(6, 8, width), axis=1)
    decay = one[4] * jnp.exp(vectors[FADING])
    small = jnp.stack(
        [one[0], one[1], one[2], decay, one[3], two[0], two[1], one[5], one[6], two[2], two[3]]
    )
    squares = jnp.stack([jnp.sum(two[4]), jnp.sum(attended_square), jnp.sum(two[5])])
    return outcome, stream, grads, small, squares


def body(residual_input, extents, *rest):
    parameters, upstream = rest[:18], rest[18]
    small_names = (0, 1, 2, 3, 4, 9, 10, 14, 15, 16, 17)
    large_names = (5, 6, 7, 8, 11, 12, 13)
    held = jnp.stack([parameters[i] for i in small_names])
    width = held.shape[1] * lax.axis_size(AXES)
    vectors = lax.all_gather(held, AXES, axis=1, tiled=True).astype(F32)
    vectors = jnp.pad(vectors, ((0, VECTORS - len(small_names)), (0, 0)))
    weights = [lax.all_gather(parameters[i], AXES, axis=0, tiled=True) for i in large_names]
    outcome, stream, grads, small, squares = layer(extents, vectors, residual_input, upstream, *weights)
    totals = lax.psum(squares, AXES)
    entries = residual_input.shape[0] * width * lax.axis_size(AXES)
    rms_values = jnp.sqrt(totals / entries)
    small = lax.psum_scatter(small, AXES, scatter_dimension=1, tiled=True)
    shards = [None] * 18
    for row, i in enumerate(small_names):
        shards[i] = small[row]
    for grad, i in zip(grads, large_names):
        shards[i] = lax.psum_scatter(grad, AXES, scatter_dimension=0, tiled=True)
    return (outcome, stream, *shards, rms_values)


def solution(mesh):
    rows, vector = P(AXES, None), P(AXES)
    kinds = [vector] * 5 + [rows] * 4 + [vector] * 2 + [rows] * 3 + [vector] * 4
    return jax.shard_map(
        body,
        mesh=mesh,
        in_specs=(rows, rows, *kinds, rows),
        out_specs=(rows, rows, *kinds, P()),
        check_vma=False,
    )
```

time: 1250 us -> 1340 us (1.072)
  waiting for transfers between devices: 402 us -> 1040 us
  matrix products: 317 us -> 62.9 us
  other arithmetic: 222 us -> 3.85 us
  local copies, waits for them, and re-layouts: 200 us -> 5.66 us
  Pallas kernels: 0 us -> 119 us
    reduce_scatter x7, waiting for transfers between devices: 355 us -> 693 us  [body(): shards[i] = lax.psum_scatter(grad, AXES, scatter_dimension=0, tiled=True)]
    all_gather x7, waiting for transfers between devices: 42.6 us -> 339 us  [body(): lax.all_gather(parameters[i], AXES, axis=0, tiled=True)]
    dot_general x117 -> x7, matrix products: 317 us -> 62.9 us  [dot_tn(): lax.dot_general(left, right, (((0,), (0,)), ((), ())), preferred_element_...]
    pallas_call x0 -> x3, Pallas kernels: none -> 119 us  [the longest x1 59.8 us: feed(): pl.pallas_call(feed_kernel, name='feed', grid=(tiles,), in_specs=[smem(),...]
    convert_element_type x79 -> x0, other arithmetic: 83.4 us -> none  [the longest x32 41.5 us: advance(): (positions >= start_block[block_rows - 1]).astype(lookup_segment_lines.dt...]
    reduce_sum x24 -> x4, other arithmetic: 69.8 us -> 1.3 us  [the longest x1 0.61 us: layer(): jnp.sum(two[4])]
    squeeze x48 -> x1, local copies, waits for them, and re-layouts: 46.5 us -> 0.65 us  [body(): shards[i] = small[row]]
    dynamic_update_slice x32 -> x0, local copies, waits for them, and re-layouts: 43.7 us -> none  [faded_lookup_lines(): lax.scan(jax.checkpoint(advance), (empty_state, empty_state), pieces)]
  transfers between devices with their start and end apart: 14 -> 14, of which waited for: 5 -> 13; matrix products, arithmetic and copies ran while one was open for 56% -> 5% of each run, Pallas kernels for 0% -> 2%
where the time goes in v1:
time: 1340 us; the launch traced here: 1330 us
  waiting for transfers between devices  1040 us (78%)
  Pallas kernels  119 us (9%)
  blocking collectives  83.7 us (6%)
  matrix products  62.9 us (5%)
  between operations  14.6 us (1%)
    reduce_scatter x7, waiting for transfers between devices, body(): shards[i] = lax.psum_scatter(grad, AXES, scatter_dimension=0, tiled=True)  693 us
    all_gather x7, waiting for transfers between devices, body(): lax.all_gather(parameters[i], AXES, axis=0, tiled=True)  339 us
    dot_general x7, matrix products, dot_tn(): lax.dot_general(left, right, (((0,), (0,)), ((), ())), preferred_element_...  62.9 us
    pallas_call x1, Pallas kernels, feed(): pl.pallas_call(feed_kernel, name='feed', grid=(tiles,), in_specs=[smem(),...  59.8 us
    all_gather x1, blocking collectives, body(): vectors = lax.all_gather(held, AXES, axis=1, tiled=True).astype(F32)  43.6 us
    unnamed x1, blocking collectives  40.1 us
    pallas_call x1, Pallas kernels, back(): pl.pallas_call(back_kernel, name='back', grid=(tiles,), in_specs=[smem(),...  34.4 us
  transfers between devices with their start and end apart: 14, of which 13 were waited for; matrix products, arithmetic and copies ran while one was open for 5% of the time, Pallas kernels for 2%

profile of v1, /device:TPU:0, one launch (start us, length us, event | category | flops | bytes accessed | tf_op | source)
XLA Modules:
  0.0 1327.4 jit_solution(12035675924759439711)
XLA Ops:
  7.2 0.7 all-gather.9.cloned.1.call-update
  8.0 0.7 all-gather.11.cloned.1.call-update
  11.2 0.7 all-gather.19.cloned.1.call-update
  11.9 1.5 stack.64
  13.5 43.6 %all-gather = bf16[32,24,11]{1,2,0:T(8,128)(2,1)S(1)} all-gather(bf16[1,24,11]{1,2,0:T(8,128)(2,1)S(1)} %bitcast.64), channel_id=1, replica_groups=mesh['wide'=8,'narrow'=4] {'wide','narrow'}, dimensions={0}, use_global_device_ids=true | all-gather | bytes 17424 | tf_op jit(solution)/shard_map/all_gather | solution.py:430
  58.1 9.7 all-gather.9.cloned.1.call-done.wk
  67.7 55.9 %all-gather.11.cloned.1.call-done.wv = bf16[768,768]{1,0:T(8,128)(2,1)} async-done(((bf16[24,768]{1,0:T(8,128)(2,1)}), bf16[768,768]{1,0:T(8,128)(2,1)}) %all-gather.11.cloned.1.call-update) | async-done | bytes 1179664 | tf_op jit(solution)/shard_map/all_gather | solution.py:432
  123.6 55.9 %all-gather.13.cloned.1.call-done.wr = bf16[768,768]{1,0:T(8,128)(2,1)} async-done(((bf16[24,768]{1,0:T(8,128)(2,1)}), bf16[768,768]{1,0:T(8,128)(2,1)}) %all-gather.13.cloned.1.call-update) | async-done | bytes 1179664 | tf_op jit(solution)/shard_map/all_gather | solution.py:432
  179.5 55.8 %all-gather.15.cloned.1.call-done.wo = bf16[768,768]{1,0:T(8,128)(2,1)} async-done(((bf16[24,768]{1,0:T(8,128)(2,1)}), bf16[768,768]{1,0:T(8,128)(2,1)}) %all-gather.15.cloned.1.call-update) | async-done | bytes 1179664 | tf_op jit(solution)/shard_map/all_gather | solution.py:432
  235.3 24.5 %front.1 = (f32[2048,768]{1,0:T(8,128)}, f32[2048,768]{1,0:T(8,128)}, f32[2048,768]{1,0:T(8,128)}, f32[2048,768]{1,0:T(8,128)}, f32[2048,768]{1,0:T(8,128)}, /*i...) custom-call(s32[1,4]{1,0:T(1,128)} %extents.5, ...), custom_call_target="tpu_custom_call" | custom-call | tf_op jit(solution)/shard_map/front/pallas_call | solution.py:333
  259.7 31.3 %all-gather.21.cloned.1.call-done.wg = bf16[768,768]{1,0:T(8,128)(2,1)} async-done(((bf16[24,768]{1,0:T(8,128)(2,1)}), bf16[768,768]{1,0:T(8,128)(2,1)}) %all-gather.21.cloned.1.call-update) | async-done | bytes 1179664 | tf_op jit(solution)/shard_map/all_gather | solution.py:432
  291.0 65.4 %all-gather.17.cloned.1.call-done.w1 = bf16[768,3072]{1,0:T(8,128)(2,1)} async-done(((bf16[24,3072]{1,0:T(8,128)(2,1)}), bf16[768,3072]{1,0:T(8,128)(2,1)}) %all-gather.17.cloned.1.call-update) | async-done | bytes 4718608 | tf_op jit(solution)/shard_map/all_gather | solution.py:432
  356.4 65.4 %all-gather.19.cloned.1.call-done.w2 = bf16[3072,768]{1,0:T(8,128)(2,1)} async-done(((bf16[96,768]{1,0:T(8,128)(2,1)}), bf16[3072,768]{1,0:T(8,128)(2,1)}) %all-gather.19.cloned.1.call-update) | async-done | bytes 4718608 | tf_op jit(solution)/shard_map/all_gather | solution.py:432
  421.8 59.8 %feed.1 = (bf16[2048,768]{1,0:T(8,128)(2,1)}, f32[2048,768]{1,0:T(8,128)}, bf16[2048,768]{1,0:T(8,128)(2,1)}, bf16[2048,768]{1,0:T(8,128)(2,1)}, bf16[2048,3072]...) custom-call(s32[1,4]{1,0:T(1,128)} %extents.5, ...), custom_call_target="tpu_custom_call" | custom-call | tf_op jit(solution)/shard_map/feed/pallas_call | solution.py:366
  481.6 34.4 %back.1 = (bf16[2048,768]{1,0:T(8,128)(2,1)}, bf16[2048,768]{1,0:T(8,128)(2,1)}, bf16[2048,768]{1,0:T(8,128)(2,1)}, bf16[2048,768]{1,0:T(8,128)(2,1)}, bf16[2048...) custom-call(s32[1,4]{1,0:T(1,128)} %extents.5, ...), custom_call_target="tpu_custom_call" | custom-call | tf_op jit(solution)/shard_map/back/pallas_call | solution.py:384
  516.1 6.2 fusion.6
  522.3 6.0 fusion.3
  528.4 7.1 fusion.4
  535.8 6.0 fusion.5
  541.9 7.1 fusion.9
  549.1 15.2 %fusion.7 = f32[768,3072]{1,0:T(8,128)} fusion(bf16[2048,768]{1,0:T(8,128)(2,1)S(1)} %copy-done.4, bf16[2048,3072]{1,0:T(8,128)(2,1)} %get-tuple-element.69), kind=kOutput, calls=%fused_computation.25 | convolution fusion | flops 9663676416 | bytes 25165824 | tf_op jit(solution)/shard_map/dot_general | solution.py:30
  564.7 1.6 copy-done.3
  566.3 15.2 %fusion.8 = f32[3072,768]{1,0:T(8,128)} fusion(bf16[2048,3072]{1,0:T(8,128)(2,1)} %get-tuple-element.70, bf16[2048,768]{1,0:T(8,128)(2,1)S(1)} %copy-done.3), kind=kOutput, calls=%fused_computation.26 | convolution fusion | flops 9663676416 | bytes 25165824 | tf_op jit(solution)/shard_map/dot_general | solution.py:30
  581.5 0.7 copy-done.2
  583.8 2.0 pad_maximum_fusion
  585.8 40.1 %all-reduce.2 = (f32[11,768]{1,0:T(8,128)S(1)}, f32[3]{0:T(128)S(1)}) all-reduce(f32[11,768]{1,0:T(8,128)S(1)} %stack.65, f32[3]{0:T(128)S(1)} %pad_maximum_fusion), channel_id=2, replica_groups=mesh['wide'=8,'narrow'=4] {'wide','narrow'}, use_global_device_ids=true, to_apply=%region_2.3.clone | all-reduce | flops 8451 | bytes 67608
  627.1 98.0 %reduce-scatter.9.cloned.1.call-done = f32[24,768]{1,0:T(8,128)} async-done(((f32[768,768]{1,0:T(8,128)}), f32[24,768]{1,0:T(8,128)}) %reduce-scatter.9.cloned.1.call-update) | async-done | bytes 73744 | tf_op jit(solution)/shard_map/reduce_scatter | solution.py:442
  725.1 103.8 %reduce-scatter.11.cloned.1.call-done = f32[24,768]{1,0:T(8,128)} async-done(((f32[768,768]{1,0:T(8,128)}), f32[24,768]{1,0:T(8,128)}) %reduce-scatter.11.cloned.1.call-update) | async-done | bytes 73744 | tf_op jit(solution)/shard_map/reduce_scatter | solution.py:442
  828.9 104.8 %reduce-scatter.13.cloned.1.call-done = f32[24,768]{1,0:T(8,128)} async-done(((f32[768,768]{1,0:T(8,128)}), f32[24,768]{1,0:T(8,128)}) %reduce-scatter.13.cloned.1.call-update) | async-done | bytes 73744 | tf_op jit(solution)/shard_map/reduce_scatter | solution.py:442
  933.7 103.8 %reduce-scatter.21.cloned.1.call-done = f32[24,768]{1,0:T(8,128)} async-done(((f32[768,768]{1,0:T(8,128)}), f32[24,768]{1,0:T(8,128)}) %reduce-scatter.21.cloned.1.call-update) | async-done | bytes 73744 | tf_op jit(solution)/shard_map/reduce_scatter | solution.py:442
  1037.5 142.1 %reduce-scatter.17.cloned.1.call-done = f32[24,3072]{1,0:T(8,128)} async-done(((f32[768,3072]{1,0:T(8,128)}), f32[24,3072]{1,0:T(8,128)}) %reduce-scatter.17.cloned.1.call-update) | async-done | bytes 294928 | tf_op jit(solution)/shard_map/reduce_scatter | solution.py:442
  1179.6 140.8 %reduce-scatter.19.cloned.1.call-done = f32[96,768]{1,0:T(8,128)} async-done(((f32[3072,768]{1,0:T(8,128)}), f32[96,768]{1,0:T(8,128)}) %reduce-scatter.19.cloned.1.call-update) | async-done | bytes 294928 | tf_op jit(solution)/shard_map/reduce_scatter | solution.py:442
  (55 shorter events, 7.1 us)
Async XLA Ops:
  7.2 60.5 %all-gather.9.cloned.1.call-start = ((), (), s32[]{:S(2)}) async-start(), calls=%async_computation.7 | async-start | bytes 1216512 | tf_op jit(solution)/shard_map/all_gather | solution.py:432
  7.9 115.7 %all-gather.11.cloned.1.call-start = ((), (), s32[]{:S(2)}) async-start(), calls=%async_computation.8 | async-start | bytes 1216512 | tf_op jit(solution)/shard_map/all_gather | solution.py:432
  8.7 170.8 %all-gather.13.cloned.1.call-start = ((), (), s32[]{:S(2)}) async-start(), calls=%async_computation.9 | async-start | bytes 1216512 | tf_op jit(solution)/shard_map/all_gather | solution.py:432
  9.4 225.9 %all-gather.15.cloned.1.call-start = ((), (), s32[]{:S(2)}) async-start(), calls=%async_computation.10 | async-start | bytes 1216512 | tf_op jit(solution)/shard_map/all_gather | solution.py:432
  10.0 281.0 %all-gather.21.cloned.1.call-start = ((), (), s32[]{:S(2)}) async-start(), calls=%async_computation.13 | async-start | bytes 1216512 | tf_op jit(solution)/shard_map/all_gather | solution.py:432
  10.6 345.8 %all-gather.17.cloned.1.call-start = ((), (), s32[]{:S(2)}) async-start(), calls=%async_computation.11 | async-start | bytes 4866048 | tf_op jit(solution)/shard_map/all_gather | solution.py:432
  11.2 410.6 %all-gather.19.cloned.1.call-start = ((), (), s32[]{:S(2)}) async-start(), calls=%async_computation.12 | async-start | bytes 4866048 | tf_op jit(solution)/shard_map/all_gather | solution.py:432
  11.9 615.2 %reduce-scatter.15.cloned.1.call-start = ((), (), s32[]{:S(2)}) async-start(), calls=%async_computation.17 | async-start | bytes 2433024 | tf_op jit(solution)/shard_map/reduce_scatter | solution.py:442
  481.6 34.5 %copy-start.6 = (bf16[2048,768]{1,0:T(8,128)(2,1)S(1)}, bf16[2048,768]{1,0:T(8,128)(2,1)}, u32[]{:S(2)}) copy-start(bf16[2048,768]{1,0:T(8,128)(2,1)} %get-tuple-element.66) | copy-start | bytes 9437188
  516.1 6.3 copy-start.7
  522.3 202.8 %reduce-scatter.9.cloned.1.call-start = ((), (), s32[]{:S(2)}) async-start(), calls=%async_computation.14 | async-start | bytes 2433024 | tf_op jit(solution)/shard_map/reduce_scatter | solution.py:442
  528.3 300.6 %reduce-scatter.11.cloned.1.call-start = ((), (), s32[]{:S(2)}) async-start(), calls=%async_computation.15 | async-start | bytes 2433024 | tf_op jit(solution)/shard_map/reduce_scatter | solution.py:442
  528.4 7.4 copy-start.5
  535.5 398.2 %reduce-scatter.13.cloned.1.call-start = ((), (), s32[]{:S(2)}) async-start(), calls=%async_computation.16 | async-start | bytes 2433024 | tf_op jit(solution)/shard_map/reduce_scatter | solution.py:442
  541.9 495.6 %reduce-scatter.21.cloned.1.call-start = ((), (), s32[]{:S(2)}) async-start(), calls=%async_computation.20 | async-start | bytes 2433024 | tf_op jit(solution)/shard_map/reduce_scatter | solution.py:442
  541.9 7.2 copy-start.4
  549.1 630.5 %reduce-scatter.17.cloned.1.call-start = ((), (), s32[]{:S(2)}) async-start(), calls=%async_computation.18 | async-start | bytes 9732096 | tf_op jit(solution)/shard_map/reduce_scatter | solution.py:442
  564.4 1.9 copy-start.3
  564.4 756.0 %reduce-scatter.19.cloned.1.call-start = ((), (), s32[]{:S(2)}) async-start(), calls=%async_computation.19 | async-start | bytes 9732096 | tf_op jit(solution)/shard_map/reduce_scatter | solution.py:442
  581.5 0.7 copy-start.2
  581.5 1.3 copy-start
  581.5 1.4 copy-start.1
Sparse Core Ops, SparseCore 0:
  10.9 56.7 all-gather.8
  70.6 52.9 all-gather.10
  126.5 52.9 all-gather.12
  182.3 52.9 all-gather.14
  238.0 52.9 all-gather.20
  293.8 62.5 all-gather.16
  359.3 62.4 all-gather.18
  522.4 97.9 reduce-scatter.14
  627.1 98.0 reduce-scatter.8
  730.8 98.0 reduce-scatter.10
  835.6 98.0 reduce-scatter.12
  939.4 97.9 reduce-scatter.20
  1045.0 134.5 reduce-scatter.16
  1185.9 134.4 reduce-scatter.18

commit v2 on v1

v2 whole, which is shorter than its diff:
```python
import functools

import jax
import jax.numpy as jnp
from jax import lax
from jax.experimental import pallas as pl
from jax.experimental.pallas import tpu as pltpu
from jax.sharding import PartitionSpec as P

F32 = jnp.float32
LOW = jnp.bfloat16
AXES = ("wide", "narrow")
BLOCK = 128
EDGE = 8
MIB = 2**20

(KEY_MIX, VALUE_MIX, GATE_MIX, FADING, REWARD, FEED_MIX, GATING_MIX, GAIN_ONE, BIAS_ONE, GAIN_TWO, BIAS_TWO) = range(11)
VECTORS = 16


def dot(left, right):
    return jnp.dot(left, right, preferred_element_type=F32)


def dot_nt(left, right):
    return lax.dot_general(left, right, (((1,), (1,)), ((), ())), preferred_element_type=F32)


def dot_tn(left, right):
    return lax.dot_general(left, right, (((0,), (0,)), ((), ())), preferred_element_type=F32)


def offsets_of(extents):
    offsets, total = [], 0
    for j in range(extents.shape[1] - 1):
        total = total + extents[0, j]
        offsets.append(total)
    return offsets


def start_of(places, offsets):
    begun = jnp.zeros_like(places)
    for offset in offsets:
        begun = jnp.where(places >= offset, offset, begun)
    return begun


def normed(x):
    centered = x - jnp.mean(x, axis=1, keepdims=True)
    scale = lax.rsqrt(jnp.mean(centered * centered, axis=1, keepdims=True) + 1e-05)
    return centered * scale, scale


def fold(x):
    return jnp.sum(x.reshape(x.shape[0] // 8, 8, x.shape[1]), axis=0)


def rows_of(shape, axis=0):
    return lax.broadcasted_iota(jnp.int32, shape, axis)


def shift_down(x, first, keep):
    return jnp.where(rows_of((x.shape[0], 1)) == 0, first, pltpu.roll(x, 1, 0)) * keep


def shift_up(x, last):
    rows = x.shape[0]
    return jnp.where(rows_of((rows, 1)) == rows - 1, last, pltpu.roll(x, rows - 1, 0))


def split(top, bottom):
    both = jnp.concatenate([top, bottom], axis=1)
    high = both.astype(LOW)
    low = (both - high.astype(F32)).astype(LOW)
    return jnp.concatenate([high, low], axis=0)


def norm_grad(back_normed, hat, scale, gain):
    back_hat = back_normed * gain
    return scale * (
        back_hat
        - jnp.mean(back_hat, axis=1, keepdims=True)
        - hat * jnp.mean(back_hat * hat, axis=1, keepdims=True)
    )


def vec(vectors, row):
    return vectors[row : row + 1, :]


def matrix(ref):
    return ref[...].reshape(-1, ref.shape[-1])


def front_tile(
    tile, extents, vectors, x_ref, wk, wv, wr, wo,
    k_out, v_out, s_out, y_out, d_out, blend_out, mid_out, state_out, square_out,
    grow, shrink, last, state,
):
    rows, width = x_ref.shape
    half = BLOCK // 2
    offsets = offsets_of(extents)
    rate = jnp.exp(vec(vectors, FADING))

    @pl.when(tile == 0)
    def _():
        local = rows_of((BLOCK + EDGE, 1)).astype(F32)
        shrink[...] = jnp.exp((half - local) * rate)
        grow[...] = jnp.exp((local[:BLOCK] + (1 - half)) * rate)
        last[...] = jnp.zeros_like(last)
        state[...] = jnp.zeros_like(state)
        square_out[...] = jnp.zeros_like(square_out)

    x = x_ref[...].astype(F32)
    hat, _ = normed(x)
    norm = hat * vec(vectors, GAIN_ONE) + vec(vectors, BIAS_ONE)
    places = tile * rows + rows_of((rows, 1))
    keep = (places != start_of(places, offsets)).astype(F32)
    before = shift_down(norm, last[0:1, :], keep)
    last[0:1, :] = norm[rows - 1 : rows, :]

    def mixed(row):
        mix = vec(vectors, row)
        return (norm * mix + before * (1.0 - mix)).astype(LOW)

    keys = dot(mixed(KEY_MIX), matrix(wk))
    values = dot(mixed(VALUE_MIX), matrix(wv))
    sig = jax.nn.sigmoid(dot(mixed(GATE_MIX), matrix(wr)))
    k_out[...] = keys
    v_out[...] = values
    s_out[...] = sig
    fade_half = jnp.exp(-half * rate)
    reward = vec(vectors, REWARD)
    for block in range(rows // BLOCK):
        here = slice(block * BLOCK, (block + 1) * BLOCK)
        key, value = keys[here], values[here]
        weight = grow[...] * jnp.exp(key)
        first = tile * rows + block * BLOCK
        after = first + rows_of((BLOCK + EDGE, 1))
        column = rows_of((1, 2 * BLOCK), 1)
        source = first + jnp.where(column >= BLOCK, column - BLOCK, column)
        begun = start_of(after, offsets)
        paired = ((source < after) & (source >= begun)).astype(LOW)
        sums = dot(paired, split(weight * value, weight))
        inherit = (begun < first).astype(F32)
        top = shrink[...] * (sums[:, :width] + inherit * (fade_half * state[0:1, :]))
        bottom = shrink[...] * (sums[:, width:] + inherit * (fade_half * state[1:2, :]))
        state[0:1, :] = top[BLOCK : BLOCK + 1]
        state[1:2, :] = bottom[BLOCK : BLOCK + 1]
        state_out[block, :, :] = state[...]
        own = jnp.exp(reward + key)
        inverse = 1.0 / (bottom[:BLOCK] + own)
        wkv = (top[:BLOCK] + own * value) * inverse
        y_out[here, :] = wkv
        d_out[here, :] = inverse
        blend_out[here, :] = (sig[here] * wkv).astype(LOW)
    attended = dot(blend_out[...], matrix(wo))
    mid_out[...] = x + attended
    square_out[...] += fold(attended * attended)


def front_kernel(extents, vectors, x_ref, weights, *rest):
    front_tile(pl.program_id(0), extents, vectors, x_ref, *[weights.at[u] for u in range(4)], *rest)


def feed_kernel(
    extents, vectors, mid_ref, edge_ref, up_ref, blend_ref, packed,
    out_out, back_out, acts, sums_out,
    lift, carry, wg, w1, w2, load,
):
    step = pl.program_id(0)
    tile = pl.num_programs(0) - 1 - step
    rows, width = mid_ref.shape
    hidden = lift.shape[1]
    offsets = offsets_of(extents)

    @pl.when(step == 0)
    def _():
        copies = [(packed.at[4], wg), (packed.at[5:9], w1)]
        copies += [(packed.at[9 + j], w2.at[:, :, :, :, j]) for j in range(4)]
        copies = [pltpu.make_async_copy(a, b, load.at[i]) for i, (a, b) in enumerate(copies)]
        for copy in copies:
            copy.start()
        for copy in copies:
            copy.wait()
        carry[...] = jnp.zeros_like(carry)
        sums_out[...] = jnp.zeros_like(sums_out)

    gain, bias = vec(vectors, GAIN_TWO), vec(vectors, BIAS_TWO)
    mid = mid_ref[...]
    hat, scale = normed(mid)
    norm = hat * gain + bias
    edge_hat, _ = normed(edge_ref[...])
    edge = (edge_hat * gain + bias)[EDGE - 1 : EDGE]
    places = tile * rows + rows_of((rows, 1))
    keep = (places != start_of(places, offsets)).astype(F32)
    before = shift_down(norm, edge, keep)
    mix_k, mix_g = vec(vectors, FEED_MIX), vec(vectors, GATING_MIX)
    feed_key = (norm * mix_k + before * (1.0 - mix_k)).astype(LOW)
    feed_gate = (norm * mix_g + before * (1.0 - mix_g)).astype(LOW)
    acts[0] = feed_key
    acts[5] = feed_gate
    acts[6] = blend_ref[...]
    lowered = None
    for j in range(hidden // width):
        chunk = slice(j * width, (j + 1) * width)
        lifted = jnp.maximum(dot(feed_key, matrix(w1.at[j])), 0.0)
        lift[:, chunk] = lifted
        squared = (lifted * lifted).astype(LOW)
        acts[1 + j] = squared
        part = dot(squared, matrix(w2.at[j]))
        lowered = part if lowered is None else lowered + part
    sig = jax.nn.sigmoid(dot(feed_gate, matrix(wg)))
    feed_out = sig * lowered
    result = mid + feed_out
    out_out[...] = result.astype(LOW)
    upstream = up_ref[...].astype(F32)
    back_lowered = (upstream * sig).astype(LOW)
    back_gate = (upstream * lowered * sig * (1.0 - sig)).astype(LOW)
    acts[11] = back_lowered
    acts[12] = back_gate
    back_key = None
    for j in range(hidden // width):
        chunk = slice(j * width, (j + 1) * width)
        back_lifted = (2.0 * lift[:, chunk] * dot_nt(back_lowered, matrix(w2.at[j]))).astype(LOW)
        acts[7 + j] = back_lifted
        part = dot_nt(back_lifted, matrix(w1.at[j]))
        back_key = part if back_key is None else back_key + part
    back_gating = dot_nt(back_gate, matrix(wg))
    late = norm - before
    back_before = keep * (back_key * (1.0 - mix_k) + back_gating * (1.0 - mix_g))
    back_norm = back_key * mix_k + back_gating * mix_g + shift_up(back_before, carry[0:1, :])
    carry[0:1, :] = back_before[0:1]
    back_mid = upstream + norm_grad(back_norm, hat, scale, gain)
    back_out[...] = back_mid
    acts[13] = back_mid.astype(LOW)
    for row, piece in enumerate(
        (back_key * late, back_gating * late, back_norm * hat, back_norm, result * result, feed_out * feed_out)
    ):
        sums_out[8 * row : 8 * row + 8, :] += fold(piece)


def back_tile(
    tile, begins, extents, vectors, x_ref, edge_ref, k_ref, v_ref, s_ref, y_ref, d_ref, state_ref, mid_ref, weights,
    stream_out, acts, sums_out,
    grow, shrink, carry, state,
):
    rows, width = x_ref.shape
    half = BLOCK // 2
    offsets = offsets_of(extents)
    rate = jnp.exp(vec(vectors, FADING))

    @pl.when(begins)
    def _():
        local = rows_of((BLOCK + EDGE, 1)).astype(F32)
        shrink[...] = jnp.exp((half - local[:BLOCK]) * rate)
        grow[...] = jnp.exp((local + (1 - EDGE - half)) * rate)
        carry[...] = jnp.zeros_like(carry)
        state[...] = jnp.zeros_like(state)
        sums_out[...] = jnp.zeros_like(sums_out)

    back_mid = mid_ref[...]
    back_attended = back_mid.astype(LOW)
    back_blend = dot_nt(back_attended, matrix(weights.at[3]))
    sig = s_ref[...]
    wkv = y_ref[...]
    acts[5] = (back_blend * wkv * sig * (1.0 - sig)).astype(LOW)
    back_top = back_blend * sig * d_ref[...]
    fade_half = jnp.exp(-half * rate)
    reward = vec(vectors, REWARD)
    for block in reversed(range(rows // BLOCK)):
        here = slice(block * BLOCK, (block + 1) * BLOCK)
        key, value = k_ref[here, :], v_ref[here, :]
        first = tile * rows + block * BLOCK
        source = first - EDGE + rows_of((BLOCK + EDGE, 1))
        column = rows_of((1, 2 * BLOCK), 1)
        after = first + jnp.where(column >= BLOCK, column - BLOCK, column)
        paired = ((source < after) & (source >= start_of(after, offsets))).astype(LOW)
        bt = back_top[here]
        weighted = shrink[...] * bt
        sums = dot(paired, split(weighted, -weighted * wkv[here]))
        following = start_of(first + BLOCK + jnp.zeros((1, 1), jnp.int32), offsets)
        tail = (source >= following).astype(F32)
        top = grow[...] * (sums[:, :width] + tail * (fade_half * state[0:1, :]))
        bottom = grow[...] * (sums[:, width:] + tail * (fade_half * state[1:2, :]))
        crossing = state_ref[block, :, :] * state[...]
        sums_out[32:40, :] += jnp.where(rows_of((8, 1)) < 2, crossing * (-1.0 * BLOCK), 0.0)
        state[0:1, :] = top[EDGE - 1 : EDGE]
        state[1:2, :] = bottom[EDGE - 1 : EDGE]
        weight = jnp.exp(key)
        own = jnp.exp(reward + key) * bt
        passed = weight * (value * top[EDGE:] + bottom[EDGE:])
        bonus = own * (value - wkv[here])
        back_key = passed + bonus
        acts[3, here, :] = back_key.astype(LOW)
        acts[4, here, :] = (weight * top[EDGE:] + own).astype(LOW)
        local = rows_of((BLOCK, 1)).astype(F32)
        sums_out[24:32, :] += fold(bonus)
        sums_out[32:40, :] += fold(local * back_key + passed)

    gain, bias = vec(vectors, GAIN_ONE), vec(vectors, BIAS_ONE)
    hat, scale = normed(x_ref[...].astype(F32))
    norm = hat * gain + bias
    edge_hat, _ = normed(edge_ref[...].astype(F32))
    edge = (edge_hat * gain + bias)[edge_ref.shape[0] - 1 : edge_ref.shape[0]]
    places = tile * rows + rows_of((rows, 1))
    keep = (places != start_of(places, offsets)).astype(F32)
    before = shift_down(norm, edge, keep)
    late = norm - before
    back_norm, back_before = None, None
    for number, mix_row in enumerate((KEY_MIX, VALUE_MIX, GATE_MIX)):
        mix = vec(vectors, mix_row)
        acts[number] = (norm * mix + before * (1.0 - mix)).astype(LOW)
        back_mixed = dot_nt(acts[3 + number], matrix(weights.at[number]))
        sums_out[8 * number : 8 * number + 8, :] += fold(back_mixed * late)
        one, two = back_mixed * mix, back_mixed * (1.0 - mix)
        back_norm = one if back_norm is None else back_norm + one
        back_before = two if back_before is None else back_before + two
    back_before = back_before * keep
    back_norm = back_norm + shift_up(back_before, carry[0:1, :])
    carry[0:1, :] = back_before[0:1]
    sums_out[40:48, :] += fold(back_norm * hat)
    sums_out[48:56, :] += fold(back_norm)
    stream_out[...] = (back_mid + norm_grad(back_norm, hat, scale, gain)).astype(LOW)


def back_kernel(*refs):
    step = pl.program_id(0)
    back_tile(pl.num_programs(0) - 1 - step, step == 0, *refs)


MESH = pl.DeviceIdType.MESH
GRID = (4, 2, 2, 2)
SMALL_ROWS = 16
HOPS = 11


def place():
    wide, narrow = lax.axis_index("wide"), lax.axis_index("narrow")
    return wide // 2, wide % 2, narrow // 2, narrow % 2


def device(z, y, x, c):
    return (z * 2 + y, x * 2 + c)


def greet():
    z, y, x, c = place()
    others = [(z, y, x, 1 - c), (z, y, 1 - x, c), (z, 1 - y, x, c)]
    others += [(lax.rem(z + k, GRID[0]), y, x, c) for k in range(1, GRID[0])]
    barrier = pltpu.get_barrier_semaphore()
    for other in others:
        pl.semaphore_signal(barrier, inc=1, device_id=device(*other), device_id_type=MESH)
    pl.semaphore_wait(barrier, len(others))


class Gather:
    def __init__(self, own, held, send, receive):
        self.own, self.held, self.send, self.receive = own, held, send, receive
        self.z, self.y, self.x, self.c = place()

    def column(self, y, x, c, half=None):
        if half is None:
            return self.held.at[:, y, x, c]
        part = GRID[0] // 2
        return self.held.at[pl.ds(half * part, part), y, x, c]

    def copy(self, number, source, target, to):
        return pltpu.make_async_remote_copy(
            src_ref=source,
            dst_ref=target,
            send_sem=self.send.at[number],
            recv_sem=self.receive.at[number],
            device_id=device(*to),
            device_id_type=MESH,
        )

    def along(self, k, mine):
        z = self.z if mine else lax.rem(self.z + GRID[0] - k, GRID[0])
        view = self.held.at[z, self.y, self.x, self.c]
        return self.copy(k - 1, self.own, view, (lax.rem(self.z + k, GRID[0]), self.y, self.x, self.c))

    def hop(self, number, mine):
        z, y, x, c = self.z, self.y, self.x, self.c
        if number < 3:
            return self.along(number + 1, mine)
        sent = (
            ((y, x, c), None, (z, y, 1 - x, c)),
            ((y, x, c), None, (z, 1 - y, x, c)),
            ((y, 1 - x, c), 0, (z, 1 - y, x, c)),
            ((1 - y, x, c), 1, (z, y, 1 - x, c)),
            ((y, x, c), None, (z, y, x, 1 - c)),
            ((y, 1 - x, c), None, (z, y, x, 1 - c)),
            ((1 - y, x, c), None, (z, y, x, 1 - c)),
            ((1 - y, 1 - x, c), None, (z, y, x, 1 - c)),
        )
        landing = (
            (y, 1 - x, c),
            (1 - y, x, c),
            (1 - y, 1 - x, c),
            (1 - y, 1 - x, c),
            (y, x, 1 - c),
            (y, 1 - x, 1 - c),
            (1 - y, x, 1 - c),
            (1 - y, 1 - x, 1 - c),
        )
        source, half, to = sent[number - 3]
        view = self.column(*(source if mine else landing[number - 3]), half)
        return self.copy(number, view, view, to)

    def start(self, *numbers):
        for number in numbers:
            self.hop(number, True).start()

    def arrived(self, *numbers):
        for number in numbers:
            self.hop(number, False).wait_recv()

    def sent(self):
        for number in range(HOPS):
            self.hop(number, True).wait_send()


def gather_kernel(
    tiles, extents, small, wk, wv, wr, wo, wg, w1, w2, x_ref,
    held, vectors, k_out, v_out, s_out, y_out, d_out, blend_out, mid_out, state_out, square_out,
    small_held, own, weights, grow, shrink, last, state, own_sem, load_sem, send, receive, small_send, small_receive,
):
    tick = pl.program_id(0)
    z, y, x, c = place()
    units = held.shape[0]
    width = x_ref.shape[1]
    first_tile = 7

    def unit(u):
        return Gather(own.at[u], held.at[u], send.at[lax.rem(u, 4)], receive.at[u])

    def small_unit():
        return Gather(small, small_held, small_send, small_receive)

    def keep(u):
        return pltpu.make_async_copy(own.at[u], held.at[u, z, y, x, c], own_sem.at[u])

    def load(u):
        return pltpu.make_async_copy(held.at[u], weights.at[u], load_sem.at[u])

    @pl.when(tick == 0)
    def _():
        for u, ref in enumerate((wk, wv, wr, wo, wg)):
            own[u] = ref[...]
        for j in range(4):
            own[5 + j] = w1[:, j * width : (j + 1) * width]
            own[9 + j] = w2[j]
        small_held[z, y, x, c] = small[...]
        for u in range(units):
            keep(u).start()
        greet()
        small_unit().start(0, 1, 2)
        unit(0).start(0, 1, 2)
        unit(1).start(0, 1, 2)

    @pl.when(tick < units)
    def _():
        keep(tick).wait()
        unit(tick).arrived(0, 1, 2)
        unit(tick).start(3, 4, 7)

    @pl.when(tick + 2 < units)
    def _():
        unit(tick + 2).start(0, 1, 2)

    @pl.when(tick == 0)
    def _():
        small_unit().arrived(0, 1, 2)
        small_unit().start(3, 4, 7)

    @pl.when(jnp.logical_and(tick >= 1, tick < units + 1))
    def _():
        unit(tick - 1).arrived(3, 4)
        unit(tick - 1).start(5, 6, 8, 9)

    @pl.when(tick == 1)
    def _():
        small_unit().arrived(3, 4)
        small_unit().start(5, 6, 8, 9)

    @pl.when(jnp.logical_and(tick >= 2, tick < units + 2))
    def _():
        unit(tick - 2).arrived(5, 6)
        unit(tick - 2).start(10)

    @pl.when(tick == 2)
    def _():
        small_unit().arrived(5, 6)
        small_unit().start(10)

    @pl.when(tick >= 3)
    def _():
        unit(tick - 3).arrived(7, 8, 9, 10)
        unit(tick - 3).sent()

    @pl.when(jnp.logical_and(tick >= 3, tick < 7))
    def _():
        load(tick - 3).start()

    @pl.when(tick == first_tile)
    def _():
        for u in range(4):
            load(u).wait()

    @pl.when(tick == 3)
    def _():
        small_unit().arrived(7, 8, 9, 10)
        small_unit().sent()
        share = width // (GRID[0] * 8)
        total = jnp.zeros((SMALL_ROWS, width), F32)
        empty = jnp.zeros((SMALL_ROWS, width - 128), F32)
        for number in range(GRID[0] * 8):
            block = small_held[number // 8, number // 4 % 2, number // 2 % 2, number % 2].astype(F32)
            total += pltpu.roll(jnp.concatenate([block, empty], axis=1), number * share, 1)
        vectors[...] = total

    @pl.when(jnp.logical_and(tick >= first_tile, tick < first_tile + tiles))
    def _():
        front_tile(
            tick - first_tile, extents, vectors, x_ref, *[weights.at[u] for u in range(4)],
            k_out, v_out, s_out, y_out, d_out, blend_out, mid_out, state_out, square_out,
            grow, shrink, last, state,
        )


class Order:
    def __init__(self, units, tiles, lead):
        self.units, self.tiles, self.lead = units, tiles, lead
        self.turns = 2 * (units - lead)
        last = lead - 1 if self.turns == 0 else lead + self.turns - 2
        self.ticks = max(units + tiles, last + 5)

    def units_before(self, tick):
        return jnp.minimum(jnp.minimum(tick, self.lead + jnp.maximum(tick - self.lead + 1, 0) // 2), self.units - 1)

    def tiles_before(self, tick):
        after = jnp.maximum(tick - self.lead, 0) // 2
        return jnp.clip(jnp.maximum(after, tick - self.units), 0, self.tiles - 1)

    def makes(self, tick):
        turn = jnp.logical_and(lax.rem(jnp.maximum(tick - self.lead, 0), 2) == 0, tick < self.lead + self.turns)
        return jnp.logical_and(tick >= 0, jnp.logical_or(tick < self.lead, turn))

    def tile_now(self, tick):
        return jnp.logical_and(jnp.logical_not(self.makes(tick)), tick < self.units + self.tiles)


class Reduce:
    def __init__(self, order, turned, out, mine, pairs, sides_x, sides_y, blocks_x, blocks_y, kept_sum, going, coming,
                 send, receive, turned_in=None, turned_receive=None):
        self.order, self.turned, self.out = order, turned, out
        self.mine, self.pairs, self.sides_x, self.sides_y = mine, pairs, sides_x, sides_y
        self.blocks_x, self.blocks_y, self.kept_sum, self.going, self.coming = blocks_x, blocks_y, kept_sum, going, coming
        self.send, self.receive, self.turned_in, self.turned_receive = send, receive, turned_in, turned_receive
        z, y, x, c = place()
        self.z, self.y, self.x, self.c = z, y, x, c
        self.core, self.over_x, self.over_y = (z, y, x, 1 - c), (z, y, 1 - x, c), (z, 1 - y, x, c)
        part = GRID[0] // 2
        self.low, self.high = pl.ds(0, part), pl.ds(part, part)

    def slot(self, u):
        return lax.rem(u, SLOTS)

    def remote(self, u, number, source, target, to, receive=None):
        return pltpu.make_async_remote_copy(
            src_ref=source,
            dst_ref=target,
            send_sem=self.send.at[self.slot(u), number],
            recv_sem=self.receive.at[u, number] if receive is None else receive,
            device_id=device(*to),
            device_id_type=MESH,
        )

    def pair(self, u):
        return self.remote(u, 0, self.mine.at[self.slot(u), 1 - self.c], self.pairs.at[u], self.core)

    def sides(self, u):
        held = self.mine.at[self.slot(u), self.c]
        y, x = 1 - self.y, 1 - self.x
        return (
            self.remote(u, 1, held.at[self.low, y, x], self.sides_x.at[u], self.over_x),
            self.remote(u, 2, held.at[self.high, y, x], self.sides_y.at[u], self.over_y),
        )

    def blocks(self, u):
        held = self.mine.at[self.slot(u), self.c]
        return (
            self.remote(u, 3, held.at[:, self.y, 1 - self.x], self.blocks_x.at[u], self.over_x),
            self.remote(u, 4, held.at[:, 1 - self.y, self.x], self.blocks_y.at[u], self.over_y),
        )

    def ends(self, u):
        found = []
        for k in range(1, GRID[0]):
            to = lax.rem(self.z + k, GRID[0])
            going = self.going.at[self.slot(u), to]
            found.append(self.remote(u, 4 + k, going, self.coming.at[u, k - 1], (to, self.y, self.x, self.c)))
        return found

    def turned_end(self, u, k):
        to = u - self.turned[0]
        return self.remote(
            u, 5, self.going.at[self.slot(u)], self.turned_in.at[k - 1], (to, self.y, self.x, self.c),
            self.turned_receive.at[k - 1],
        )

    def is_turned(self, u):
        return jnp.logical_and(u >= self.turned[0], u < self.turned[1])

    def make(self, tick, left, right):
        u = self.order.units_before(tick)

        @pl.when(self.order.makes(tick))
        def _():
            slot = self.slot(u)
            grad = dot_tn(left[0], right[0]).astype(LOW)
            depth, width = self.out.shape[-2:]
            z, y, x, c = GRID

            def even():
                blocks = grad.reshape(z, y, x, c, depth, width)
                for core in range(c):
                    self.mine[slot, core] = blocks[:, :, :, core]

            def turned():
                blocks = grad.reshape(y, x, c, z, depth, width)
                for core in range(c):
                    for j in range(y):
                        for i in range(x):
                            self.mine[slot, core, :, j, i] = blocks[j, i, core]

            if self.turned is None:
                even()
            else:
                pl.when(self.is_turned(u))(turned)
                pl.when(jnp.logical_not(self.is_turned(u)))(even)
            self.pair(u).start()

    def stage(self, tick, lag, work):
        u = self.order.units_before(tick - lag)
        pl.when(self.order.makes(tick - lag))(functools.partial(work, u))

    def add_pair(self, u):
        slot, c = self.slot(u), self.c
        self.pair(u).wait()
        self.mine[slot, c] = (self.mine[slot, c].astype(F32) + self.pairs[u].astype(F32)).astype(LOW)
        for copy in self.sides(u):
            copy.start()

    def add_sides(self, u):
        for copy in self.sides(u):
            copy.wait()
        held = self.mine.at[self.slot(u), self.c]
        low, high, y, x = self.low, self.high, self.y, self.x
        held[low, 1 - y, x] = (held[low, 1 - y, x].astype(F32) + self.sides_x[u].astype(F32)).astype(LOW)
        held[high, y, 1 - x] = (held[high, y, 1 - x].astype(F32) + self.sides_y[u].astype(F32)).astype(LOW)
        for copy in self.blocks(u):
            copy.start()

    def add_blocks(self, u):
        slot = self.slot(u)
        for copy in self.blocks(u):
            copy.wait()
        total = self.mine[slot, self.c, :, self.y, self.x].astype(F32)
        total = total + self.blocks_x[u].astype(F32) + self.blocks_y[u].astype(F32)
        self.kept_sum[slot] = total
        self.going[slot] = total.astype(LOW)

        def even():
            for copy in self.ends(u):
                copy.start()

        if self.turned is None:
            even()
        else:
            pl.when(jnp.logical_not(self.is_turned(u)))(even)
            for k in range(1, GRID[0]):
                away = lax.rem(self.z + GRID[0] - (u - self.turned[0]), GRID[0]) == k
                pl.when(jnp.logical_and(self.is_turned(u), away))(lambda k=k: self.turned_end(u, k).start())

    def add_ends(self, u):
        slot = self.slot(u)

        def even():
            for copy in self.ends(u):
                copy.wait()
            total = self.kept_sum[slot, self.z]
            for k in range(GRID[0] - 1):
                total += self.coming[u, k].astype(F32)
            self.out[u] = total

        def turned_here():
            total = self.kept_sum[slot]
            for k in range(1, GRID[0]):
                self.turned_end(u, k).wait_recv()
                total += self.turned_in[k - 1].astype(F32)
            self.out[self.turned[0] : self.turned[1]] = total

        if self.turned is None:
            even()
        else:
            pl.when(jnp.logical_not(self.is_turned(u)))(even)
            ahead = lax.rem(self.z + GRID[0] - (u - self.turned[0]), GRID[0])
            pl.when(jnp.logical_and(self.is_turned(u), ahead == 0))(turned_here)
            for k in range(1, GRID[0]):
                pl.when(jnp.logical_and(self.is_turned(u), ahead == k))(lambda k=k: self.turned_end(u, k).wait_send())

    def run(self, tick, left, right):
        self.make(tick, left, right)
        self.stage(tick, 1, self.add_pair)
        self.stage(tick, 2, self.add_sides)
        self.stage(tick, 3, self.add_blocks)
        self.stage(tick, 4, self.add_ends)


def back_reduce_kernel(order, *refs):
    inputs, refs = refs[:12], refs[12:]
    left, right, *refs = refs
    outputs, out, refs = refs[:3], refs[3], refs[4:]
    scratch, refs = refs[:4], refs[4:]
    tick = pl.program_id(0)
    pl.when(tick == 0)(greet)
    Reduce(order, (4, 8), out, *refs).run(tick, left, right)

    @pl.when(order.tile_now(tick))
    def _():
        number = order.tiles_before(tick)
        back_tile(order.tiles - 1 - number, number == 0, *inputs, *outputs, *scratch)


def last_reduce_kernel(order, vectors, sums_one, sums_two, square, left, right, out, small_out, *refs):
    *refs, sums, small_in, small_send, small_receive = refs
    tick = pl.program_id(0)
    z, y, x, c = place()
    partners = (
        (z, y, x, 1 - c),
        (z, y, 1 - x, c),
        (z, 1 - y, x, c),
        (z + 1 - 2 * lax.rem(z, 2), y, x, c),
        (lax.rem(z + 2, GRID[0]), y, x, c),
    )

    def exchange(step):
        return pltpu.make_async_remote_copy(
            src_ref=sums.at[step],
            dst_ref=small_in.at[step],
            send_sem=small_send.at[step],
            recv_sem=small_receive.at[step],
            device_id=device(*partners[step]),
            device_id_type=MESH,
        )

    @pl.when(tick == 0)
    def _():
        sums[0] = small_grads(vectors, sums_one, sums_two, square)
        greet()
        exchange(0).start()

    Reduce(order, None, out, *refs).run(tick, left, right)

    for step in range(1, 6):

        @pl.when(tick == step)
        def _():
            exchange(step - 1).wait()
            total = sums[step - 1] + small_in[step - 1]
            if step == 5:
                small_out[...] = total
            else:
                sums[step] = total
                exchange(step).start()


def whole(shape):
    return pl.BlockSpec(shape, lambda i: (0,) * len(shape), pipeline_mode=pl.Buffered(1))


def kept(shape):
    return pl.BlockSpec(shape, lambda i: (0,) * len(shape))


def smem():
    return pl.BlockSpec(memory_space=pltpu.SMEM)


ROWS = 256
UNITS = 13
SLOTS = 5
FEED_ACTS = 14


def four(packed):
    return pl.BlockSpec((4, *packed.shape[1:]), lambda i: (0,) * len(packed.shape), pipeline_mode=pl.Buffered(1))


def front_shapes(tokens, width):
    wide = jax.ShapeDtypeStruct((tokens, width), F32)
    low = jax.ShapeDtypeStruct((tokens, width), LOW)
    states = jax.ShapeDtypeStruct((tokens // BLOCK, 8, width), F32)
    return [wide] * 5 + [low, wide, states, jax.ShapeDtypeStruct((8, width), F32)]


def front_specs(width, index):
    tile = pl.BlockSpec((ROWS, width), lambda i: (index(i), 0))
    states = pl.BlockSpec((ROWS // BLOCK, 8, width), lambda i: (index(i), 0, 0))
    return [tile] * 7 + [states, kept((8, width))]


def front_scratch(width):
    return [
        pltpu.VMEM((BLOCK, width), F32),
        pltpu.VMEM((BLOCK + EDGE, width), F32),
        pltpu.VMEM((8, width), F32),
        pltpu.VMEM((8, width), F32),
    ]


def front(extents, vectors, x, packed):
    tokens, width = x.shape
    return pl.pallas_call(
        front_kernel,
        name="front",
        grid=(tokens // ROWS,),
        in_specs=[smem(), whole(vectors.shape), pl.BlockSpec((ROWS, width), lambda i: (i, 0)), four(packed)],
        out_specs=front_specs(width, lambda i: i),
        out_shape=front_shapes(tokens, width),
        scratch_shapes=front_scratch(width),
        compiler_params=pltpu.CompilerParams(vmem_limit_bytes=56 * MIB),
    )(extents, vectors, x, packed)


def gather_front(extents, small, shards, x):
    tokens, width = x.shape
    tiles = tokens // ROWS
    depth = shards[0].shape[0]
    anywhere = pl.BlockSpec(memory_space=pl.ANY)

    def index(i):
        return jnp.clip(i - 7, 0, tiles - 1)

    dma = pltpu.SemaphoreType.DMA
    return pl.pallas_call(
        functools.partial(gather_kernel, tiles),
        name="gather_front",
        grid=(max(UNITS + 3, tiles + 7),),
        in_specs=[smem()]
        + [whole(part.shape) for part in (small, *shards)]
        + [pl.BlockSpec((ROWS, width), lambda i: (index(i), 0))],
        out_specs=[anywhere, kept((SMALL_ROWS, width))] + front_specs(width, index),
        out_shape=[
            jax.ShapeDtypeStruct((UNITS, *GRID, depth, width), LOW),
            jax.ShapeDtypeStruct((SMALL_ROWS, width), F32),
        ]
        + front_shapes(tokens, width),
        scratch_shapes=[
            pltpu.VMEM((*GRID, *small.shape), LOW),
            pltpu.VMEM((UNITS, depth, width), LOW),
            pltpu.VMEM((4, *GRID, depth, width), LOW),
        ]
        + front_scratch(width)
        + [dma((UNITS,)), dma((4,)), dma((4, HOPS)), dma((UNITS, HOPS)), dma((HOPS,)), dma((HOPS,))],
        compiler_params=pltpu.CompilerParams(vmem_limit_bytes=56 * MIB, collective_id=0, has_side_effects=True),
    )(extents, small, *shards, x)


def feed(extents, vectors, mid, upstream, blend, packed):
    tokens, width = mid.shape
    hidden = 4 * width
    rows, tiles = ROWS, tokens // ROWS
    tile = pl.BlockSpec((rows, width), lambda i: (tiles - 1 - i, 0))
    edge = pl.BlockSpec((EDGE, width), lambda i: (jnp.maximum((tiles - 1 - i) * (rows // EDGE) - 1, 0), 0))
    block = packed.shape[1:]
    return pl.pallas_call(
        feed_kernel,
        name="feed",
        grid=(tiles,),
        in_specs=[smem(), whole(vectors.shape), tile, edge, tile, tile, pl.BlockSpec(memory_space=pl.ANY)],
        out_specs=[
            tile,
            tile,
            pl.BlockSpec((FEED_ACTS, rows, width), lambda i: (0, tiles - 1 - i, 0)),
            kept((48, width)),
        ],
        out_shape=[
            jax.ShapeDtypeStruct((tokens, width), LOW),
            jax.ShapeDtypeStruct((tokens, width), F32),
            jax.ShapeDtypeStruct((FEED_ACTS, tokens, width), LOW),
            jax.ShapeDtypeStruct((48, width), F32),
        ],
        scratch_shapes=[
            pltpu.VMEM((rows, hidden), F32),
            pltpu.VMEM((8, width), F32),
            pltpu.VMEM(block, LOW),
            pltpu.VMEM((4, *block), LOW),
            pltpu.VMEM((*block[:4], 4, *block[4:]), LOW),
            pltpu.SemaphoreType.DMA((6,)),
        ],
        compiler_params=pltpu.CompilerParams(vmem_limit_bytes=60 * MIB),
    )(extents, vectors, mid, mid, upstream, blend, packed)


def back_specs(tokens, width, packed, index):
    blocks = ROWS // BLOCK
    tile = pl.BlockSpec((ROWS, width), lambda i: (index(i), 0))
    edge = pl.BlockSpec((16, width), lambda i: (jnp.maximum(index(i) * (ROWS // 16) - 1, 0), 0))
    states = pl.BlockSpec((blocks, 8, width), lambda i: (index(i), 0, 0))
    inputs = [smem(), whole((SMALL_ROWS, width)), tile, edge] + [tile] * 5 + [states, tile, four(packed)]
    outputs = [tile, pl.BlockSpec((6, ROWS, width), lambda i: (0, index(i), 0)), kept((56, width))]
    shapes = [
        jax.ShapeDtypeStruct((tokens, width), LOW),
        jax.ShapeDtypeStruct((6, tokens, width), LOW),
        jax.ShapeDtypeStruct((56, width), F32),
    ]
    scratch = [
        pltpu.VMEM((BLOCK + EDGE, width), F32),
        pltpu.VMEM((BLOCK, width), F32),
        pltpu.VMEM((8, width), F32),
        pltpu.VMEM((8, width), F32),
    ]
    return inputs, outputs, shapes, scratch


def back(extents, vectors, x, saved, states, back_mid, packed):
    tokens, width = x.shape
    tiles = tokens // ROWS
    inputs, outputs, shapes, scratch = back_specs(tokens, width, packed, lambda i: tiles - 1 - i)
    return pl.pallas_call(
        back_kernel,
        name="back",
        grid=(tiles,),
        in_specs=inputs,
        out_specs=outputs,
        out_shape=shapes,
        scratch_shapes=scratch,
        compiler_params=pltpu.CompilerParams(vmem_limit_bytes=56 * MIB),
    )(extents, vectors, x, x, *saved, states, back_mid, packed)


def reduce_scratch(units, depth, width):
    z, y, x, c = GRID
    dma = pltpu.SemaphoreType.DMA
    return [
        pltpu.VMEM((SLOTS, c, z, y, x, depth, width), LOW),
        pltpu.VMEM((units, z, y, x, depth, width), LOW),
        pltpu.VMEM((units, z // 2, depth, width), LOW),
        pltpu.VMEM((units, z // 2, depth, width), LOW),
        pltpu.VMEM((units, z, depth, width), LOW),
        pltpu.VMEM((units, z, depth, width), LOW),
        pltpu.VMEM((SLOTS, z, depth, width), F32),
        pltpu.VMEM((SLOTS, z, depth, width), LOW),
        pltpu.VMEM((units, z - 1, depth, width), LOW),
        dma((SLOTS, 8)),
        dma((units, 8)),
    ]


def back_reduce(extents, vectors, x, saved, states, back_mid, packed, acts):
    tokens, width = x.shape
    tiles, depth, units, lead = tokens // ROWS, packed.shape[-2], 10, 4
    order = Order(units, tiles, lead)
    inputs, outputs, shapes, scratch = back_specs(tokens, width, packed, lambda i: tiles - 1 - order.tiles_before(i))
    left = pl.BlockSpec((1, tokens, width), lambda i: (jnp.maximum(order.units_before(i) - 3, 0), 0, 0))
    right = pl.BlockSpec(
        (1, tokens, width),
        lambda i: (7 + jnp.minimum(order.units_before(i), 4) + jnp.maximum(order.units_before(i) - 7, 0), 0, 0),
    )
    z, _, _, _ = GRID
    dma = pltpu.SemaphoreType.DMA
    return pl.pallas_call(
        functools.partial(back_reduce_kernel, order),
        name="back_reduce",
        grid=(order.ticks,),
        in_specs=inputs + [left, right],
        out_specs=outputs + [kept((units, depth, width))],
        out_shape=shapes + [jax.ShapeDtypeStruct((units, depth, width), F32)],
        scratch_shapes=scratch
        + reduce_scratch(units, depth, width)
        + [pltpu.VMEM((z - 1, z, depth, width), LOW), dma((z - 1,))],
        compiler_params=pltpu.CompilerParams(vmem_limit_bytes=63 * MIB, collective_id=1, has_side_effects=True),
    )(extents, vectors, x, x, *saved, states, back_mid, packed, acts, acts)


def last_reduce(vectors, acts, sums_one, sums_two, square, depth):
    tokens, width = acts.shape[1:]
    units = 3
    order = Order(units, 0, units)
    left = pl.BlockSpec((1, tokens, width), lambda i: (jnp.minimum(i, units - 1), 0, 0))
    right = pl.BlockSpec((1, tokens, width), lambda i: (units + jnp.minimum(i, units - 1), 0, 0))
    dma = pltpu.SemaphoreType.DMA
    small = (SMALL_ROWS, width)
    return pl.pallas_call(
        functools.partial(last_reduce_kernel, order),
        name="last_reduce",
        grid=(order.ticks,),
        in_specs=[whole(a.shape) for a in (vectors, sums_one, sums_two, square)] + [left, right],
        out_specs=[kept((units, depth, width)), kept(small)],
        out_shape=[jax.ShapeDtypeStruct((units, depth, width), F32), jax.ShapeDtypeStruct(small, F32)],
        scratch_shapes=reduce_scratch(units, depth, width)
        + [pltpu.VMEM((5, *small), F32), pltpu.VMEM((5, *small), F32), dma((5,)), dma((5,))],
        compiler_params=pltpu.CompilerParams(vmem_limit_bytes=56 * MIB, collective_id=2, has_side_effects=True),
    )(vectors, sums_one, sums_two, square, acts, acts)


def small_grads(vectors, sums_one, sums_two, square):
    width = vectors.shape[1]
    one = [jnp.sum(sums_one[8 * i : 8 * i + 8, :], axis=0, keepdims=True) for i in range(7)]
    two = [jnp.sum(sums_two[8 * i : 8 * i + 8, :], axis=0, keepdims=True) for i in range(6)]
    decay = one[4] * jnp.exp(vec(vectors, FADING))
    lane = rows_of((1, width), 1)
    squares = jnp.zeros((1, width), F32)
    for place_of, total in enumerate((two[4], jnp.sum(square[...], axis=0, keepdims=True), two[5])):
        squares = jnp.where(lane == place_of, jnp.sum(total, axis=1, keepdims=True), squares)
    rows = [one[0], one[1], one[2], decay, one[3], two[0], two[1], one[5], one[6], two[2], two[3], squares]
    return jnp.concatenate(rows + [jnp.zeros((SMALL_ROWS - len(rows), width), F32)], axis=0)


def pack(weights):
    *square, w1, w2 = weights
    depth, width = square[0].shape[-2:]
    parts = list(square)
    parts += [w1[..., j * width : (j + 1) * width] for j in range(4)]
    parts += [w2[..., j * depth : (j + 1) * depth, :] for j in range(4)]
    return jnp.stack(parts)


SMALL = (0, 1, 2, 3, 4, 9, 10, 14, 15, 16, 17)
LARGE = (5, 6, 7, 8, 13, 11, 12)


def finish(outcome, stream, large, small, squares, entries):
    shards = [None] * 18
    for row, i in enumerate(SMALL):
        shards[i] = small[row]
    for grad, i in zip(large, LARGE):
        shards[i] = grad
    return (outcome, stream, *shards, jnp.sqrt(squares / entries))


def body_any(residual_input, extents, *rest):
    parameters, upstream = rest[:18], rest[18]
    devices = lax.axis_size(AXES)
    held = jnp.stack([parameters[i] for i in SMALL])
    width = held.shape[1] * devices
    vectors = lax.all_gather(held, AXES, axis=1, tiled=True).astype(F32)
    vectors = jnp.pad(vectors, ((0, SMALL_ROWS - len(SMALL)), (0, 0)))
    blocks = 1
    for size in GRID:
        blocks *= size
    weights = [lax.all_gather(parameters[i], AXES, axis=0, tiled=True) for i in LARGE]
    packed = pack([w.reshape(blocks, -1, w.shape[1]) for w in weights])
    packed = packed.reshape(UNITS, *GRID, *packed.shape[2:])
    *saved, blend, mid, states, square = front(extents, vectors, residual_input, packed)
    outcome, back_mid, acts, sums_two = feed(extents, vectors, mid, upstream, blend, packed)
    stream, mixed, sums_one = back(extents, vectors, residual_input, saved, states, back_mid, packed)
    small = small_grads(vectors, sums_one, sums_two, square)
    grads = [dot_tn(mixed[i], mixed[3 + i]) for i in range(3)] + [dot_tn(acts[6], acts[13]), dot_tn(acts[5], acts[12])]
    grads.append(jnp.concatenate([dot_tn(acts[0], acts[7 + j]) for j in range(4)], axis=1))
    grads.append(jnp.concatenate([dot_tn(acts[1 + j], acts[11]) for j in range(4)], axis=0))
    squares = lax.psum(small[len(SMALL), :3], AXES)
    small = lax.psum_scatter(small[: len(SMALL)], AXES, scatter_dimension=1, tiled=True)
    large = [lax.psum_scatter(grad, AXES, scatter_dimension=0, tiled=True) for grad in grads]
    return finish(outcome, stream, large, small, squares, residual_input.shape[0] * width * devices)


def body(residual_input, extents, *rest):
    parameters, upstream = rest[:18], rest[18]
    devices = lax.axis_size(AXES)
    width = residual_input.shape[1]
    share = width // devices
    small = jnp.stack([parameters[i] for i in SMALL])
    small = jnp.pad(small, ((0, SMALL_ROWS - len(SMALL)), (0, 128 - share)))
    shards = [parameters[i] for i in LARGE]
    shards[6] = shards[6].reshape(4, share, width)
    packed, vectors, *saved, blend, mid, states, square = gather_front(extents, small, shards, residual_input)
    outcome, back_mid, acts, sums_two = feed(extents, vectors, mid, upstream, blend, packed)
    stream, mixed, sums_one, most = back_reduce(
        extents, vectors, residual_input, saved, states, back_mid, packed, acts
    )
    rest, small = last_reduce(vectors, mixed, sums_one, sums_two, square, share)
    mine = lax.axis_index(AXES)
    squares = small[len(SMALL), :3]
    small = lax.dynamic_slice(small, (0, mine * share), (len(SMALL), share))
    large = [rest[0], rest[1], rest[2], most[9], most[8]]
    large.append(jnp.concatenate([most[j] for j in range(4)], axis=1))
    large.append(most[4:8].reshape(4 * share, width))
    return finish(outcome, stream, large, small, squares, residual_input.shape[0] * width * devices)


def solution(mesh):
    rows, vector = P(AXES, None), P(AXES)
    kinds = [vector] * 5 + [rows] * 4 + [vector] * 2 + [rows] * 3 + [vector] * 4
    sizes = (mesh.shape["wide"], mesh.shape["narrow"])
    return jax.shard_map(
        body if sizes == (GRID[0] * GRID[1], GRID[2] * GRID[3]) else body_any,
        mesh=mesh,
        in_specs=(rows, rows, *kinds, rows),
        out_specs=(rows, rows, *kinds, P()),
        check_vma=False,
    )
```

time: 1340 us -> 301 us (0.22)
  waiting for transfers between devices: 1040 us -> 0 us
  Pallas kernels: 119 us -> 289 us
  blocking collectives: 83.7 us -> 0 us
  matrix products: 62.9 us -> 0 us
  between operations: 14.6 us -> 0.72 us
    reduce_scatter x7 -> x0, waiting for transfers between devices: 693 us -> none  [body(): shards[i] = lax.psum_scatter(grad, AXES, scatter_dimension=0, tiled=True)]
    all_gather x7 -> x0, waiting for transfers between devices: 339 us -> none  [body(): lax.all_gather(parameters[i], AXES, axis=0, tiled=True)]
    pallas_call x2 -> x3, Pallas kernels: 58.9 us -> 227 us  [the longest x1 105 us: back_reduce(): pl.pallas_call(functools.partial(back_reduce_kernel, order), name='back_r...]
    dot_general x7 -> x0, matrix products: 62.9 us -> none  [dot_tn(): lax.dot_general(left, right, (((0,), (0,)), ((), ())), preferred_element_...]
    all_gather x1 -> x0, blocking collectives: 43.6 us -> none  [body(): vectors = lax.all_gather(held, AXES, axis=1, tiled=True).astype(F32)]
    unnamed x1 -> x0, blocking collectives: 40.1 us -> none
  transfers between devices with their start and end apart: 14 -> 0, of which waited for: 13 -> 0; matrix products, arithmetic and copies ran while one was open for 5% -> 0% of each run, Pallas kernels for 2% -> 0%
where the time goes in v2:
time: 301 us
  Pallas kernels  289 us (96%)
  local copies, waits for them, and re-layouts  8.79 us (3%)
    pallas_call x1, Pallas kernels, back_reduce(): pl.pallas_call(functools.partial(back_reduce_kernel, order), name='back_r...  105 us
    pallas_call x1, Pallas kernels, gather_front(): pl.pallas_call(functools.partial(gather_kernel, tiles), name='gather_fron...  85.9 us
    pallas_call x1, Pallas kernels, feed(): pl.pallas_call(feed_kernel, name='feed', grid=(tiles,), in_specs=[smem(),...  62.4 us
    pallas_call x1, Pallas kernels, last_reduce(): pl.pallas_call(functools.partial(last_reduce_kernel, order), name='last_r...  36 us

profile of v2, /device:TPU:0, one launch (start us, length us, event | category | flops | bytes accessed | tf_op | source)
XLA Modules:
  0.0 300.9 jit_solution(448957318020837211)
XLA Ops:
  0.7 1.5 stack.47
  2.2 0.6 pad.4.small
  2.8 85.9 %gather_front.1 = (bf16[13,4,2,2,2,24,768]{6,5,4,3,2,1,0:T(8,128)(2,1)}, f32[16,768]{1,0:T(8,128)}, f32[2048,768]{1,0:T(8,128)}, f32[2048,768]{1,0:T(8,128)}, f3...) custom-call(s32[1,4]{1,0:T(1,128)} %refs_0_.1, ...), custom_call_target="tpu_custom_call" | custom-call | tf_op jit(solution)/shard_map/gather_front/pallas_call | solution.py:848
  88.7 62.4 %feed.1 = (bf16[2048,768]{1,0:T(8,128)(2,1)}, f32[2048,768]{1,0:T(8,128)}, bf16[14,2048,768]{2,1,0:T(8,128)(2,1)}, f32[48,768]{1,0:T(8,128)}) custom-call(s32[1,4]{1,0:T(1,128)} %refs_0_.1, f32[16,768]{1,0:T(8,128)} %get-tuple-element.42.vectors.refs_1_, f32[2048,768]{1,0:T(8,128)} %get-tuple-element.43.mid_ref.edge_ref, ...), custom_call_target="tpu_custom_call" | custom-call | tf_op jit(solution)/shard_map/feed/pallas_call | solution.py:879
  151.1 105.2 %back_reduce.1 = (bf16[2048,768]{1,0:T(8,128)(2,1)}, bf16[6,2048,768]{2,1,0:T(8,128)(2,1)}, f32[56,768]{1,0:T(8,128)}, f32[10,24,768]{2,1,0:T(8,128)}) custom-call(s32[1,4]{1,0:T(1,128)} %refs_0_.1, f32[16,768]{1,0:T(8,128)} %get-tuple-element.42.vectors.refs_1_, bf16[2048,768]{1,0:T(8,128)(2,1)} %refs_3_.1, bf16[2048,768]{1,0:T(8,128)(2,1)} %refs_3_.1, ...), custom_call_target="tpu_custom_call" | custom-call | tf_op jit(solution)/shard_map/back_reduce/pallas_call | solution.py:975
  256.3 0.0 copy-start.1
  256.3 0.0 copy-start
  256.3 36.0 %last_reduce.1 = (f32[3,24,768]{2,1,0:T(8,128)}, f32[16,768]{1,0:T(8,128)}) custom-call(f32[16,768]{1,0:T(8,128)} %get-tuple-element.42.vectors.refs_1_, f32[56,768]{1,0:T(8,128)} %get-tuple-element.56.sums_one, f32[48,768]{1,0:T(8,128)} %get-tuple-element.57.sums_two, f32[8,768]{1,0:T(8,128)} %get-tuple-element.58.square, ...), custom_call_target="tpu_custom_call" | custom-call | tf_op jit(solution)/shard_map/last_reduce/pallas_call | solution.py:997
  292.3 0.0 copy-done.1
  292.3 1.7 slice_bitcast_fusion
  294.0 0.7 pad_maximum_fusion
  294.8 1.6 dynamic-slice_bitcast_fusion
  296.4 1.2 sqrt_bitcast_fusion
  297.6 1.7 slice.81
  299.3 0.0 copy-done
  299.3 1.7 copy.43
Async XLA Ops:
  256.3 36.1 %copy-start.1 = (f32[10,24,768]{2,1,0:T(8,128)S(1)}, f32[10,24,768]{2,1,0:T(8,128)}, u32[]{:S(2)}) copy-start(f32[10,24,768]{2,1,0:T(8,128)} %get-tuple-element.62) | copy-start | bytes 2211844
  256.3 43.0 %copy-start = (bf16[2048,768]{1,0:T(8,128)(2,1)S(1)}, bf16[2048,768]{1,0:T(8,128)(2,1)}, u32[]{:S(2)}) copy-start(bf16[2048,768]{1,0:T(8,128)(2,1)} %get-tuple-element.108) | copy-start | bytes 9437188

commit v3 on v2

--- a/solution.py
+++ b/solution.py
@@ -243,7 +243,7 @@
 def back_tile(
     tile, begins, extents, vectors, x_ref, edge_ref, k_ref, v_ref, s_ref, y_ref, d_ref, state_ref, mid_ref, weights,
     stream_out, acts, sums_out,
-    grow, shrink, carry, state,
+    grow, shrink, carry, state, between=(),
 ):
     rows, width = x_ref.shape
     half = BLOCK // 2
@@ -259,6 +259,7 @@
         state[...] = jnp.zeros_like(state)
         sums_out[...] = jnp.zeros_like(sums_out)
 
+    between = iter(between)
     back_mid = mid_ref[...]
     back_attended = back_mid.astype(LOW)
     back_blend = dot_nt(back_attended, matrix(weights.at[3]))
@@ -269,6 +270,7 @@
     fade_half = jnp.exp(-half * rate)
     reward = vec(vectors, REWARD)
     for block in reversed(range(rows // BLOCK)):
+        next(between, int)()
         here = slice(block * BLOCK, (block + 1) * BLOCK)
         key, value = k_ref[here, :], v_ref[here, :]
         first = tile * rows + block * BLOCK
@@ -283,6 +285,7 @@
         tail = (source >= following).astype(F32)
         top = grow[...] * (sums[:, :width] + tail * (fade_half * state[0:1, :]))
         bottom = grow[...] * (sums[:, width:] + tail * (fade_half * state[1:2, :]))
+        next(between, int)()
         crossing = state_ref[block, :, :] * state[...]
         sums_out[32:40, :] += jnp.where(rows_of((8, 1)) < 2, crossing * (-1.0 * BLOCK), 0.0)
         state[0:1, :] = top[EDGE - 1 : EDGE]
@@ -309,6 +312,7 @@
     late = norm - before
     back_norm, back_before = None, None
     for number, mix_row in enumerate((KEY_MIX, VALUE_MIX, GATE_MIX)):
+        next(between, int)()
         mix = vec(vectors, mix_row)
         acts[number] = (norm * mix + before * (1.0 - mix)).astype(LOW)
         back_mixed = dot_nt(acts[3 + number], matrix(weights.at[number]))
@@ -433,7 +437,7 @@
     first_tile = 7
 
     def unit(u):
-        return Gather(own.at[u], held.at[u], send.at[lax.rem(u, 4)], receive.at[u])
+        return Gather(own.at[u], held.at[u], send.at[lax.rem(u, 6)], receive.at[u])
 
     def small_unit():
         return Gather(small, small_held, small_send, small_receive)
@@ -484,20 +488,27 @@
         small_unit().arrived(3, 4)
         small_unit().start(5, 6, 8, 9)
 
-    @pl.when(jnp.logical_and(tick >= 2, tick < units + 2))
-    def _():
-        unit(tick - 2).arrived(5, 6)
-        unit(tick - 2).start(10)
+    def diagonal(u):
+        unit(u).arrived(5, 6)
+        unit(u).start(10)
+
+    def complete(u):
+        unit(u).arrived(7, 8, 9, 10)
+        unit(u).sent()
+
+    def within(u, first, end):
+        return jnp.logical_and(u >= first, u < end)
+
+    pl.when(within(tick - 2, 0, 4))(lambda: diagonal(tick - 2))
+    pl.when(within(tick - 3, 4, units))(lambda: diagonal(tick - 3))
 
     @pl.when(tick == 2)
     def _():
         small_unit().arrived(5, 6)
         small_unit().start(10)
 
-    @pl.when(tick >= 3)
-    def _():
-        unit(tick - 3).arrived(7, 8, 9, 10)
-        unit(tick - 3).sent()
+    pl.when(within(tick - 3, 0, 4))(lambda: complete(tick - 3))
+    pl.when(within(tick - 5, 4, units))(lambda: complete(tick - 5))
 
     @pl.when(jnp.logical_and(tick >= 3, tick < 7))
     def _():
@@ -529,32 +540,10 @@
         )
 
 
-class Order:
-    def __init__(self, units, tiles, lead):
-        self.units, self.tiles, self.lead = units, tiles, lead
-        self.turns = 2 * (units - lead)
-        last = lead - 1 if self.turns == 0 else lead + self.turns - 2
-        self.ticks = max(units + tiles, last + 5)
-
-    def units_before(self, tick):
-        return jnp.minimum(jnp.minimum(tick, self.lead + jnp.maximum(tick - self.lead + 1, 0) // 2), self.units - 1)
-
-    def tiles_before(self, tick):
-        after = jnp.maximum(tick - self.lead, 0) // 2
-        return jnp.clip(jnp.maximum(after, tick - self.units), 0, self.tiles - 1)
-
-    def makes(self, tick):
-        turn = jnp.logical_and(lax.rem(jnp.maximum(tick - self.lead, 0), 2) == 0, tick < self.lead + self.turns)
-        return jnp.logical_and(tick >= 0, jnp.logical_or(tick < self.lead, turn))
-
-    def tile_now(self, tick):
-        return jnp.logical_and(jnp.logical_not(self.makes(tick)), tick < self.units + self.tiles)
-
-
 class Reduce:
-    def __init__(self, order, turned, out, mine, pairs, sides_x, sides_y, blocks_x, blocks_y, kept_sum, going, coming,
-                 send, receive, turned_in=None, turned_receive=None):
-        self.order, self.turned, self.out = order, turned, out
+    def __init__(self, out, mine, pairs, sides_x, sides_y, blocks_x, blocks_y, kept_sum, going, coming,
+                 turned_in, send, receive, turned_receive):
+        self.out = out
         self.mine, self.pairs, self.sides_x, self.sides_y = mine, pairs, sides_x, sides_y
         self.blocks_x, self.blocks_y, self.kept_sum, self.going, self.coming = blocks_x, blocks_y, kept_sum, going, coming
         self.send, self.receive, self.turned_in, self.turned_receive = send, receive, turned_in, turned_receive
@@ -578,7 +567,7 @@
         )
 
     def pair(self, u):
-        return self.remote(u, 0, self.mine.at[self.slot(u), 1 - self.c], self.pairs.at[u], self.core)
+        return self.remote(u, 0, self.mine.at[self.slot(u), 1 - self.c], self.pairs.at[self.slot(u)], self.core)
 
     def sides(self, u):
         held = self.mine.at[self.slot(u), self.c]
@@ -604,52 +593,42 @@
         return found
 
     def turned_end(self, u, k):
-        to = u - self.turned[0]
+        to = u - TURNED[0]
         return self.remote(
             u, 5, self.going.at[self.slot(u)], self.turned_in.at[k - 1], (to, self.y, self.x, self.c),
             self.turned_receive.at[k - 1],
         )
 
     def is_turned(self, u):
-        return jnp.logical_and(u >= self.turned[0], u < self.turned[1])
-
-    def make(self, tick, left, right):
-        u = self.order.units_before(tick)
-
-        @pl.when(self.order.makes(tick))
-        def _():
-            slot = self.slot(u)
-            grad = dot_tn(left[0], right[0]).astype(LOW)
-            depth, width = self.out.shape[-2:]
-            z, y, x, c = GRID
-
-            def even():
-                blocks = grad.reshape(z, y, x, c, depth, width)
-                for core in range(c):
-                    self.mine[slot, core] = blocks[:, :, :, core]
-
-            def turned():
-                blocks = grad.reshape(y, x, c, z, depth, width)
-                for core in range(c):
-                    for j in range(y):
-                        for i in range(x):
-                            self.mine[slot, core, :, j, i] = blocks[j, i, core]
-
-            if self.turned is None:
-                even()
-            else:
-                pl.when(self.is_turned(u))(turned)
-                pl.when(jnp.logical_not(self.is_turned(u)))(even)
-            self.pair(u).start()
+        return jnp.logical_and(u >= TURNED[0], u < TURNED[1])
+
+    def pieces(self, u, left, right):
+        slot, depth = self.slot(u), self.out.shape[-2]
+        z, y, x, c = GRID
+        turned = jnp.logical_and(u >= TURNED[0], u < TURNED[1]).astype(jnp.int32)
+
+        def piece(part, columns):
+            many = left.shape[-1] // PIECES[0]
+            wide = right.shape[-1] // PIECES[1]
+            lanes = slice(columns * wide, (columns + 1) * wide)
+            grad = dot_tn(left[:, part * many : (part + 1) * many], right[:, lanes]).astype(LOW)
+            blocks = grad.reshape(many // depth, depth, grad.shape[1])
+            for number in range(many // depth):
+                b = part * (many // depth) + number
+                even = (b % c, b // (x * y * c), b // (x * c) % y, b // c % x)
+                other = (b // z % c, b % z, b // (z * c * x), b // (z * c) % x)
+                where = [i + turned * (j - i) for i, j in zip(even, other)]
+                self.mine[slot, where[0], where[1], where[2], where[3], :, lanes] = blocks[number]
+
+        return [functools.partial(piece, i, j) for i in range(PIECES[0]) for j in range(PIECES[1])]
 
     def stage(self, tick, lag, work):
-        u = self.order.units_before(tick - lag)
-        pl.when(self.order.makes(tick - lag))(functools.partial(work, u))
+        pl.when(jnp.logical_and(tick >= lag, tick < lag + UNITS))(functools.partial(work, tick - lag))
 
     def add_pair(self, u):
         slot, c = self.slot(u), self.c
         self.pair(u).wait()
-        self.mine[slot, c] = (self.mine[slot, c].astype(F32) + self.pairs[u].astype(F32)).astype(LOW)
+        self.mine[slot, c] = (self.mine[slot, c].astype(F32) + self.pairs[slot].astype(F32)).astype(LOW)
         for copy in self.sides(u):
             copy.start()
 
@@ -676,13 +655,10 @@
             for copy in self.ends(u):
                 copy.start()
 
-        if self.turned is None:
-            even()
-        else:
-            pl.when(jnp.logical_not(self.is_turned(u)))(even)
-            for k in range(1, GRID[0]):
-                away = lax.rem(self.z + GRID[0] - (u - self.turned[0]), GRID[0]) == k
-                pl.when(jnp.logical_and(self.is_turned(u), away))(lambda k=k: self.turned_end(u, k).start())
+        pl.when(jnp.logical_not(self.is_turned(u)))(even)
+        for k in range(1, GRID[0]):
+            away = lax.rem(self.z + 2 * GRID[0] - jnp.minimum(u, 2 * GRID[0]), GRID[0]) == k
+            pl.when(jnp.logical_and(self.is_turned(u), away))(lambda k=k: self.turned_end(u, k).start())
 
     def add_ends(self, u):
         slot = self.slot(u)
@@ -700,44 +676,27 @@
             for k in range(1, GRID[0]):
                 self.turned_end(u, k).wait_recv()
                 total += self.turned_in[k - 1].astype(F32)
-            self.out[self.turned[0] : self.turned[1]] = total
-
-        if self.turned is None:
-            even()
-        else:
-            pl.when(jnp.logical_not(self.is_turned(u)))(even)
-            ahead = lax.rem(self.z + GRID[0] - (u - self.turned[0]), GRID[0])
-            pl.when(jnp.logical_and(self.is_turned(u), ahead == 0))(turned_here)
-            for k in range(1, GRID[0]):
-                pl.when(jnp.logical_and(self.is_turned(u), ahead == k))(lambda k=k: self.turned_end(u, k).wait_send())
-
-    def run(self, tick, left, right):
-        self.make(tick, left, right)
-        self.stage(tick, 1, self.add_pair)
-        self.stage(tick, 2, self.add_sides)
-        self.stage(tick, 3, self.add_blocks)
-        self.stage(tick, 4, self.add_ends)
-
-
-def back_reduce_kernel(order, *refs):
-    inputs, refs = refs[:12], refs[12:]
-    left, right, *refs = refs
-    outputs, out, refs = refs[:3], refs[3], refs[4:]
-    scratch, refs = refs[:4], refs[4:]
-    tick = pl.program_id(0)
-    pl.when(tick == 0)(greet)
-    Reduce(order, (4, 8), out, *refs).run(tick, left, right)
-
-    @pl.when(order.tile_now(tick))
-    def _():
-        number = order.tiles_before(tick)
-        back_tile(order.tiles - 1 - number, number == 0, *inputs, *outputs, *scratch)
-
-
-def last_reduce_kernel(order, vectors, sums_one, sums_two, square, left, right, out, small_out, *refs):
-    *refs, sums, small_in, small_send, small_receive = refs
+            self.out[TURNED[0] : TURNED[1]] = total
+
+        pl.when(jnp.logical_not(self.is_turned(u)))(even)
+        ahead = lax.rem(self.z + 2 * GRID[0] - jnp.minimum(u, 2 * GRID[0]), GRID[0])
+        pl.when(jnp.logical_and(self.is_turned(u), ahead == 0))(turned_here)
+        for k in range(1, GRID[0]):
+            pl.when(jnp.logical_and(self.is_turned(u), ahead == k))(lambda k=k: self.turned_end(u, k).wait_send())
+
+
+def reduce_kernel(
+    extents, vectors, x_ref, edge_ref, k_ref, v_ref, s_ref, y_ref, d_ref, state_ref, mid_ref, weights,
+    sums_two, square, acts,
+    stream_out, mixed, out, small_out,
+    grow, shrink, carry, state, staged, sums_one, lefts, rights, sums, small_in,
+    stage_sem, left_sem, right_sem, small_send, small_receive, *refs,
+):
     tick = pl.program_id(0)
     z, y, x, c = place()
+    rows = x_ref.shape[0]
+    tiles = mixed.shape[1] // rows
+    job = Reduce(out, *refs)
     partners = (
         (z, y, x, 1 - c),
         (z, y, 1 - x, c),
@@ -756,17 +715,84 @@
             device_id_type=MESH,
         )
 
+    def left_of(u):
+        return lax.rem(jnp.maximum(u - 3, 0), 2)
+
+    def right_of(u):
+        return lax.rem(jnp.minimum(u, 4) + jnp.maximum(u - 7, 0), 2)
+
+    def fetch_left(u, late):
+        source = mixed.at[u - FIRST_UNITS] if late else acts.at[jnp.maximum(u - 3, 0)]
+        return pltpu.make_async_copy(source, lefts.at[left_of(u)], left_sem.at[left_of(u)])
+
+    def fetch_right(u, late):
+        if late:
+            source = mixed.at[u - FIRST_UNITS + 3]
+        else:
+            source = acts.at[7 + jnp.minimum(u, 4) + jnp.maximum(u - 7, 0)]
+        return pltpu.make_async_copy(source, rights.at[right_of(u)], right_sem.at[right_of(u)])
+
+    def fetches(u, work):
+        early, late = u < FIRST_UNITS, jnp.logical_and(u >= FIRST_UNITS, u < UNITS)
+        pl.when(jnp.logical_and(early, jnp.logical_or(u == 0, u >= 4)))(lambda: work(fetch_left(u, False)))
+        pl.when(jnp.logical_and(early, jnp.logical_or(u <= 4, u >= 8)))(lambda: work(fetch_right(u, False)))
+        pl.when(late)(lambda: work(fetch_left(u, True)))
+        pl.when(late)(lambda: work(fetch_right(u, True)))
+
+    def keep(number):
+        two = lax.rem(number, 2)
+        where = pl.ds(pl.multiple_of((tiles - 1 - number) * rows, rows), rows)
+        return pltpu.make_async_copy(staged.at[two], mixed.at[:, where], stage_sem.at[two])
+
+    def start(copy):
+        copy.start()
+
+    def wait(copy):
+        copy.wait()
+
     @pl.when(tick == 0)
     def _():
+        fetches(tick, start)
+        greet()
+
+    number = tick - FIRST_TILE
+    pl.when(jnp.logical_and(number >= 2, number < tiles + 2))(lambda: keep(number - 2).wait())
+    fetches(tick + 1, start)
+    fetches(tick, wait)
+
+    inputs = (extents, vectors, x_ref, edge_ref, k_ref, v_ref, s_ref, y_ref, d_ref, state_ref, mid_ref, weights)
+
+    def pieces():
+        return job.pieces(tick, lefts.at[left_of(tick)], rights.at[right_of(tick)])
+
+    busy = jnp.logical_and(number >= 0, number < tiles)
+
+    @pl.when(busy)
+    def _():
+        back_tile(
+            tiles - 1 - number, number == 0, *inputs, stream_out, staged.at[lax.rem(number, 2)], sums_one,
+            grow, shrink, carry, state, between=pieces(),
+        )
+        keep(number).start()
+        job.pair(tick).start()
+
+    @pl.when(jnp.logical_and(jnp.logical_not(busy), tick < UNITS))
+    def _():
+        for piece in pieces():
+            piece()
+        job.pair(tick).start()
+
+    for lag, work in zip(LAGS, (job.add_pair, job.add_sides, job.add_blocks, job.add_ends)):
+        job.stage(tick, lag, work)
+
+    @pl.when(number == tiles)
+    def _():
         sums[0] = small_grads(vectors, sums_one, sums_two, square)
-        greet()
         exchange(0).start()
 
-    Reduce(order, None, out, *refs).run(tick, left, right)
-
     for step in range(1, 6):
 
-        @pl.when(tick == step)
+        @pl.when(number == tiles + step)
         def _():
             exchange(step - 1).wait()
             total = sums[step - 1] + small_in[step - 1]
@@ -791,7 +817,12 @@
 
 ROWS = 256
 UNITS = 13
-SLOTS = 5
+SLOTS = 6
+LAGS = (1, 2, 3, 6)
+PIECES = (2, 1)
+FIRST_UNITS = 10
+FIRST_TILE = 0
+TURNED = (4, 8)
 FEED_ACTS = 14
 
 
@@ -848,7 +879,7 @@
     return pl.pallas_call(
         functools.partial(gather_kernel, tiles),
         name="gather_front",
-        grid=(max(UNITS + 3, tiles + 7),),
+        grid=(max(UNITS + 5, tiles + 7),),
         in_specs=[smem()]
         + [whole(part.shape) for part in (small, *shards)]
         + [pl.BlockSpec((ROWS, width), lambda i: (index(i), 0))],
@@ -864,7 +895,7 @@
             pltpu.VMEM((4, *GRID, depth, width), LOW),
         ]
         + front_scratch(width)
-        + [dma((UNITS,)), dma((4,)), dma((4, HOPS)), dma((UNITS, HOPS)), dma((HOPS,)), dma((HOPS,))],
+        + [dma((UNITS,)), dma((4,)), dma((6, HOPS)), dma((UNITS, HOPS)), dma((HOPS,)), dma((HOPS,))],
         compiler_params=pltpu.CompilerParams(vmem_limit_bytes=56 * MIB, collective_id=0, has_side_effects=True),
     )(extents, small, *shards, x)
 
@@ -942,69 +973,58 @@
     )(extents, vectors, x, x, *saved, states, back_mid, packed)
 
 
-def reduce_scratch(units, depth, width):
-    z, y, x, c = GRID
-    dma = pltpu.SemaphoreType.DMA
-    return [
-        pltpu.VMEM((SLOTS, c, z, y, x, depth, width), LOW),
-        pltpu.VMEM((units, z, y, x, depth, width), LOW),
-        pltpu.VMEM((units, z // 2, depth, width), LOW),
-        pltpu.VMEM((units, z // 2, depth, width), LOW),
-        pltpu.VMEM((units, z, depth, width), LOW),
-        pltpu.VMEM((units, z, depth, width), LOW),
-        pltpu.VMEM((SLOTS, z, depth, width), F32),
-        pltpu.VMEM((SLOTS, z, depth, width), LOW),
-        pltpu.VMEM((units, z - 1, depth, width), LOW),
-        dma((SLOTS, 8)),
-        dma((units, 8)),
-    ]
-
-
-def back_reduce(extents, vectors, x, saved, states, back_mid, packed, acts):
+def reduce(extents, vectors, x, saved, states, back_mid, packed, acts, sums_two, square):
     tokens, width = x.shape
-    tiles, depth, units, lead = tokens // ROWS, packed.shape[-2], 10, 4
-    order = Order(units, tiles, lead)
-    inputs, outputs, shapes, scratch = back_specs(tokens, width, packed, lambda i: tiles - 1 - order.tiles_before(i))
-    left = pl.BlockSpec((1, tokens, width), lambda i: (jnp.maximum(order.units_before(i) - 3, 0), 0, 0))
-    right = pl.BlockSpec(
-        (1, tokens, width),
-        lambda i: (7 + jnp.minimum(order.units_before(i), 4) + jnp.maximum(order.units_before(i) - 7, 0), 0, 0),
+    tiles, depth = tokens // ROWS, packed.shape[-2]
+    inputs, outputs, shapes, scratch = back_specs(
+        tokens, width, packed, lambda i: tiles - 1 - jnp.clip(i - FIRST_TILE, 0, tiles - 1)
     )
-    z, _, _, _ = GRID
-    dma = pltpu.SemaphoreType.DMA
-    return pl.pallas_call(
-        functools.partial(back_reduce_kernel, order),
-        name="back_reduce",
-        grid=(order.ticks,),
-        in_specs=inputs + [left, right],
-        out_specs=outputs + [kept((units, depth, width))],
-        out_shape=shapes + [jax.ShapeDtypeStruct((units, depth, width), F32)],
-        scratch_shapes=scratch
-        + reduce_scratch(units, depth, width)
-        + [pltpu.VMEM((z - 1, z, depth, width), LOW), dma((z - 1,))],
-        compiler_params=pltpu.CompilerParams(vmem_limit_bytes=63 * MIB, collective_id=1, has_side_effects=True),
-    )(extents, vectors, x, x, *saved, states, back_mid, packed, acts, acts)
-
-
-def last_reduce(vectors, acts, sums_one, sums_two, square, depth):
-    tokens, width = acts.shape[1:]
-    units = 3
-    order = Order(units, 0, units)
-    left = pl.BlockSpec((1, tokens, width), lambda i: (jnp.minimum(i, units - 1), 0, 0))
-    right = pl.BlockSpec((1, tokens, width), lambda i: (units + jnp.minimum(i, units - 1), 0, 0))
+    stream, mixed, sums_one = shapes
+    anywhere = pl.BlockSpec(memory_space=pl.ANY)
+    z, y, x_size, c = GRID
     dma = pltpu.SemaphoreType.DMA
     small = (SMALL_ROWS, width)
     return pl.pallas_call(
-        functools.partial(last_reduce_kernel, order),
-        name="last_reduce",
-        grid=(order.ticks,),
-        in_specs=[whole(a.shape) for a in (vectors, sums_one, sums_two, square)] + [left, right],
-        out_specs=[kept((units, depth, width)), kept(small)],
-        out_shape=[jax.ShapeDtypeStruct((units, depth, width), F32), jax.ShapeDtypeStruct(small, F32)],
-        scratch_shapes=reduce_scratch(units, depth, width)
-        + [pltpu.VMEM((5, *small), F32), pltpu.VMEM((5, *small), F32), dma((5,)), dma((5,))],
-        compiler_params=pltpu.CompilerParams(vmem_limit_bytes=56 * MIB, collective_id=2, has_side_effects=True),
-    )(vectors, sums_one, sums_two, square, acts, acts)
+        reduce_kernel,
+        name="reduce",
+        grid=(UNITS + LAGS[3],),
+        in_specs=inputs + [whole(sums_two.shape), whole(square.shape), anywhere],
+        out_specs=[outputs[0], anywhere, kept((UNITS, depth, width)), kept(small)],
+        out_shape=[
+            stream,
+            mixed,
+            jax.ShapeDtypeStruct((UNITS, depth, width), F32),
+            jax.ShapeDtypeStruct(small, F32),
+        ],
+        scratch_shapes=scratch
+        + [
+            pltpu.VMEM((2, 6, ROWS, width), LOW),
+            pltpu.VMEM(sums_one.shape, F32),
+            pltpu.VMEM((2, tokens, width), LOW),
+            pltpu.VMEM((2, tokens, width), LOW),
+            pltpu.VMEM((5, *small), F32),
+            pltpu.VMEM((5, *small), F32),
+            dma((2,)),
+            dma((2,)),
+            dma((2,)),
+            dma((5,)),
+            dma((5,)),
+            pltpu.VMEM((SLOTS, c, z, y, x_size, depth, width), LOW),
+            pltpu.VMEM((SLOTS, z, y, x_size, depth, width), LOW),
+            pltpu.VMEM((UNITS, z // 2, depth, width), LOW),
+            pltpu.VMEM((UNITS, z // 2, depth, width), LOW),
+            pltpu.VMEM((UNITS, z, depth, width), LOW),
+            pltpu.VMEM((UNITS, z, depth, width), LOW),
+            pltpu.VMEM((SLOTS, z, depth, width), F32),
+            pltpu.VMEM((SLOTS, z, depth, width), LOW),
+            pltpu.VMEM((UNITS, z - 1, depth, width), LOW),
+            pltpu.VMEM((z - 1, z, depth, width), LOW),
+            dma((SLOTS, 8)),
+            dma((UNITS, 8)),
+            dma((z - 1,)),
+        ],
+        compiler_params=pltpu.CompilerParams(vmem_limit_bytes=63 * MIB, collective_id=1, has_side_effects=True),
+    )(extents, vectors, x, x, *saved, states, back_mid, packed, sums_two, square, acts)
 
 
 def small_grads(vectors, sums_one, sums_two, square):
@@ -1079,16 +1099,15 @@
     shards[6] = shards[6].reshape(4, share, width)
     packed, vectors, *saved, blend, mid, states, square = gather_front(extents, small, shards, residual_input)
     outcome, back_mid, acts, sums_two = feed(extents, vectors, mid, upstream, blend, packed)
-    stream, mixed, sums_one, most = back_reduce(
-        extents, vectors, residual_input, saved, states, back_mid, packed, acts
+    stream, _, total, small = reduce(
+        extents, vectors, residual_input, saved, states, back_mid, packed, acts, sums_two, square
     )
-    rest, small = last_reduce(vectors, mixed, sums_one, sums_two, square, share)
     mine = lax.axis_index(AXES)
     squares = small[len(SMALL), :3]
     small = lax.dynamic_slice(small, (0, mine * share), (len(SMALL), share))
-    large = [rest[0], rest[1], rest[2], most[9], most[8]]
-    large.append(jnp.concatenate([most[j] for j in range(4)], axis=1))
-    large.append(most[4:8].reshape(4 * share, width))
+    large = [total[10], total[11], total[12], total[9], total[8]]
+    large.append(jnp.concatenate([total[j] for j in range(4)], axis=1))
+    large.append(total[4:8].reshape(4 * share, width))
     return finish(outcome, stream, large, small, squares, residual_input.shape[0] * width * devices)
 
 

time: 301 us -> 267 us (0.89)
  Pallas kernels: 289 us -> 253 us
    pallas_call x2 -> x1, Pallas kernels: 141 us -> 106 us  [reduce(): pl.pallas_call(reduce_kernel, name='reduce', grid=(UNITS + LAGS[3],), in_...]
where the time goes in v3:
time: 267 us
  Pallas kernels  253 us (95%)
  local copies, waits for them, and re-layouts  11.1 us (4%)
    pallas_call x1, Pallas kernels, reduce(): pl.pallas_call(reduce_kernel, name='reduce', grid=(UNITS + LAGS[3],), in_...  106 us
    pallas_call x1, Pallas kernels, gather_front(): pl.pallas_call(functools.partial(gather_kernel, tiles), name='gather_fron...  84.2 us
    pallas_call x1, Pallas kernels, feed(): pl.pallas_call(feed_kernel, name='feed', grid=(tiles,), in_specs=[smem(),...  62.4 us

profile of v3, /device:TPU:0, one launch (start us, length us, event | category | flops | bytes accessed | tf_op | source)
XLA Modules:
  0.0 266.7 jit_solution(5721132145857309552)
XLA Ops:
  0.7 1.5 stack.47
  2.2 0.6 pad.4.small
  2.8 84.2 %gather_front.1 = (bf16[13,4,2,2,2,24,768]{6,5,4,3,2,1,0:T(8,128)(2,1)}, f32[16,768]{1,0:T(8,128)}, f32[2048,768]{1,0:T(8,128)}, f32[2048,768]{1,0:T(8,128)}, f3...) custom-call(s32[1,4]{1,0:T(1,128)} %extents.5, ...), custom_call_target="tpu_custom_call" | custom-call | tf_op jit(solution)/shard_map/gather_front/pallas_call | solution.py:879
  87.0 62.4 %feed.1 = (bf16[2048,768]{1,0:T(8,128)(2,1)}, f32[2048,768]{1,0:T(8,128)}, bf16[14,2048,768]{2,1,0:T(8,128)(2,1)}, f32[48,768]{1,0:T(8,128)}) custom-call(s32[1,4]{1,0:T(1,128)} %extents.5, f32[16,768]{1,0:T(8,128)} %get-tuple-element.39.vectors, f32[2048,768]{1,0:T(8,128)} %get-tuple-element.40.mid_ref.edge_ref, ...), custom_call_target="tpu_custom_call" | custom-call | tf_op jit(solution)/shard_map/feed/pallas_call | solution.py:910
  149.4 106.4 %reduce.1 = (bf16[2048,768]{1,0:T(8,128)(2,1)}, bf16[6,2048,768]{2,1,0:T(8,128)(2,1)}, f32[13,24,768]{2,1,0:T(8,128)}, f32[16,768]{1,0:T(8,128)}) custom-call(s32[1,4]{1,0:T(1,128)} %extents.5, f32[16,768]{1,0:T(8,128)} %get-tuple-element.39.vectors, bf16[2048,768]{1,0:T(8,128)(2,1)} %edge_ref.1, bf16[2048,768]{1,0:T(8,128)(2,1)} %edge_ref.1, ...), custom_call_target="tpu_custom_call" | custom-call | tf_op jit(solution)/shard_map/reduce/pallas_call | solution.py:987
  255.7 1.7 dynamic-slice_bitcast_fusion
  257.4 1.9 slice_bitcast_fusion
  259.3 0.7 pad_maximum_fusion
  260.0 1.7 slice.81
  261.7 1.2 sqrt_bitcast_fusion
  262.9 3.8 %copy.43 = bf16[2048,768]{1,0:T(8,128)(2,1)} copy(bf16[2048,768]{1,0:T(8,128)(2,1)} %get-tuple-element.99) | data formatting | bytes 6291456

commit v4 on v3

--- a/solution.py
+++ b/solution.py
@@ -336,7 +336,7 @@
 MESH = pl.DeviceIdType.MESH
 GRID = (4, 2, 2, 2)
 SMALL_ROWS = 16
-HOPS = 11
+HOPS = 13
 
 
 def place():
@@ -362,12 +362,6 @@
     def __init__(self, own, held, send, receive):
         self.own, self.held, self.send, self.receive = own, held, send, receive
         self.z, self.y, self.x, self.c = place()
-
-    def column(self, y, x, c, half=None):
-        if half is None:
-            return self.held.at[:, y, x, c]
-        part = GRID[0] // 2
-        return self.held.at[pl.ds(half * part, part), y, x, c]
 
     def copy(self, number, source, target, to):
         return pltpu.make_async_remote_copy(
@@ -388,28 +382,37 @@
         z, y, x, c = self.z, self.y, self.x, self.c
         if number < 3:
             return self.along(number + 1, mine)
+        partner = (z + 1 - 2 * lax.rem(z, 2), y, x, c)
+        everything = slice(None)
+        one = lax.rem(z, 2)
+        two = one + 2
+        core = (z, y, x, 1 - c)
         sent = (
-            ((y, x, c), None, (z, y, 1 - x, c)),
-            ((y, x, c), None, (z, 1 - y, x, c)),
-            ((y, 1 - x, c), 0, (z, 1 - y, x, c)),
-            ((1 - y, x, c), 1, (z, y, 1 - x, c)),
-            ((y, x, c), None, (z, y, x, 1 - c)),
-            ((y, 1 - x, c), None, (z, y, x, 1 - c)),
-            ((1 - y, x, c), None, (z, y, x, 1 - c)),
-            ((1 - y, 1 - x, c), None, (z, y, x, 1 - c)),
+            ((everything, y, x, c), (z, y, 1 - x, c)),
+            ((everything, y, x, c), (z, 1 - y, x, c)),
+            ((one, y, 1 - x, c), (z, 1 - y, x, c)),
+            ((two, 1 - y, x, c), (z, y, 1 - x, c)),
+            ((everything, y, x, c), core),
+            ((everything, y, 1 - x, c), core),
+            ((everything, 1 - y, x, c), core),
+            ((everything, 1 - y, 1 - x, c), core),
+            ((one, 1 - y, 1 - x, c), partner),
+            ((two, 1 - y, 1 - x, c), partner),
         )
         landing = (
-            (y, 1 - x, c),
-            (1 - y, x, c),
-            (1 - y, 1 - x, c),
-            (1 - y, 1 - x, c),
-            (y, x, 1 - c),
-            (y, 1 - x, 1 - c),
-            (1 - y, x, 1 - c),
-            (1 - y, 1 - x, 1 - c),
+            (everything, y, 1 - x, c),
+            (everything, 1 - y, x, c),
+            (one, 1 - y, 1 - x, c),
+            (two, 1 - y, 1 - x, c),
+            (everything, y, x, 1 - c),
+            (everything, y, 1 - x, 1 - c),
+            (everything, 1 - y, x, 1 - c),
+            (everything, 1 - y, 1 - x, 1 - c),
+            (1 - one, 1 - y, 1 - x, c),
+            (3 - one, 1 - y, 1 - x, c),
         )
-        source, half, to = sent[number - 3]
-        view = self.column(*(source if mine else landing[number - 3]), half)
+        source, to = sent[number - 3]
+        view = self.held.at[source if mine else landing[number - 3]]
         return self.copy(number, view, view, to)
 
     def start(self, *numbers):
@@ -434,10 +437,10 @@
     z, y, x, c = place()
     units = held.shape[0]
     width = x_ref.shape[1]
-    first_tile = 7
+    first_tile = 8
 
     def unit(u):
-        return Gather(own.at[u], held.at[u], send.at[lax.rem(u, 6)], receive.at[u])
+        return Gather(own.at[u], held.at[u], send.at[lax.rem(u, 9)], receive.at[u])
 
     def small_unit():
         return Gather(small, small_held, small_send, small_receive)
@@ -490,6 +493,10 @@
 
     def diagonal(u):
         unit(u).arrived(5, 6)
+        unit(u).start(11, 12)
+
+    def partners(u):
+        unit(u).arrived(11, 12)
         unit(u).start(10)
 
     def complete(u):
@@ -505,21 +512,29 @@
     @pl.when(tick == 2)
     def _():
         small_unit().arrived(5, 6)
+        small_unit().start(11, 12)
+
+    pl.when(within(tick - 3, 0, 4))(lambda: partners(tick - 3))
+    pl.when(within(tick - 5, 4, units))(lambda: partners(tick - 5))
+
+    @pl.when(tick == 3)
+    def _():
+        small_unit().arrived(11, 12)
         small_unit().start(10)
 
-    pl.when(within(tick - 3, 0, 4))(lambda: complete(tick - 3))
-    pl.when(within(tick - 5, 4, units))(lambda: complete(tick - 5))
-
-    @pl.when(jnp.logical_and(tick >= 3, tick < 7))
-    def _():
-        load(tick - 3).start()
+    pl.when(within(tick - 4, 0, 4))(lambda: complete(tick - 4))
+    pl.when(within(tick - 6, 4, units))(lambda: complete(tick - 6))
+
+    @pl.when(jnp.logical_and(tick >= 4, tick < 8))
+    def _():
+        load(tick - 4).start()
 
     @pl.when(tick == first_tile)
     def _():
         for u in range(4):
             load(u).wait()
 
-    @pl.when(tick == 3)
+    @pl.when(tick == 4)
     def _():
         small_unit().arrived(7, 8, 9, 10)
         small_unit().sent()
@@ -756,7 +771,8 @@
         greet()
 
     number = tick - FIRST_TILE
-    pl.when(jnp.logical_and(number >= 2, number < tiles + 2))(lambda: keep(number - 2).wait())
+    pl.when(jnp.logical_and(number >= 2, number < tiles + 1))(lambda: keep(number - 2).wait())
+    pl.when(number == tiles)(lambda: keep(number - 1).wait())
     fetches(tick + 1, start)
     fetches(tick, wait)
 
@@ -821,7 +837,7 @@
 LAGS = (1, 2, 3, 6)
 PIECES = (2, 1)
 FIRST_UNITS = 10
-FIRST_TILE = 0
+FIRST_TILE = 1
 TURNED = (4, 8)
 FEED_ACTS = 14
 
@@ -873,13 +889,13 @@
     anywhere = pl.BlockSpec(memory_space=pl.ANY)
 
     def index(i):
-        return jnp.clip(i - 7, 0, tiles - 1)
+        return jnp.clip(i - 8, 0, tiles - 1)
 
     dma = pltpu.SemaphoreType.DMA
     return pl.pallas_call(
         functools.partial(gather_kernel, tiles),
         name="gather_front",
-        grid=(max(UNITS + 5, tiles + 7),),
+        grid=(max(UNITS + 6, tiles + 8),),
         in_specs=[smem()]
         + [whole(part.shape) for part in (small, *shards)]
         + [pl.BlockSpec((ROWS, width), lambda i: (index(i), 0))],
@@ -895,7 +911,7 @@
             pltpu.VMEM((4, *GRID, depth, width), LOW),
         ]
         + front_scratch(width)
-        + [dma((UNITS,)), dma((4,)), dma((6, HOPS)), dma((UNITS, HOPS)), dma((HOPS,)), dma((HOPS,))],
+        + [dma((UNITS,)), dma((4,)), dma((9, HOPS)), dma((UNITS, HOPS)), dma((HOPS,)), dma((HOPS,))],
         compiler_params=pltpu.CompilerParams(vmem_limit_bytes=56 * MIB, collective_id=0, has_side_effects=True),
     )(extents, small, *shards, x)
 
@@ -1027,6 +1043,44 @@
     )(extents, vectors, x, x, *saved, states, back_mid, packed, sums_two, square, acts)
 
 
+def finish_kernel(entries, share, stream_ref, total, small, stream_out, *outs):
+    *squares, w1, w2, rms = outs[:8]
+    lines = outs[8:]
+    stream_out[...] = stream_ref[...]
+
+    @pl.when(pl.program_id(0) == 0)
+    def _():
+        width = small.shape[1]
+        for out, u in zip(squares, (10, 11, 12, 9, 8)):
+            out[...] = total[u]
+        for j in range(4):
+            w1[:, j * width : (j + 1) * width] = total[j]
+            w2[j] = total[4 + j]
+        sums = small[...]
+        rms[...] = jnp.sqrt(sums[len(SMALL), :3] / entries)
+        mine = lax.axis_index("wide") * lax.axis_size("narrow") + lax.axis_index("narrow")
+        turned = pltpu.roll(sums, lax.rem(width - mine * share, width), 1)
+        for row, out in enumerate(lines):
+            out[...] = turned[row, :share]
+
+
+def finish_up(stream, total, small, entries):
+    tokens, width = stream.shape
+    depth = total.shape[1]
+    parts = 4
+    tile = pl.BlockSpec((tokens // parts, width), lambda i: (i, 0))
+    shapes = [(depth, width)] * 5 + [(depth, 4 * width), (4, depth, width), (3,)] + [(depth,)] * len(SMALL)
+    return pl.pallas_call(
+        functools.partial(finish_kernel, entries, depth),
+        name="finish_up",
+        grid=(parts,),
+        in_specs=[tile, whole(total.shape), whole(small.shape)],
+        out_specs=[tile] + [kept(shape) for shape in shapes],
+        out_shape=[jax.ShapeDtypeStruct(stream.shape, LOW)] + [jax.ShapeDtypeStruct(shape, F32) for shape in shapes],
+        compiler_params=pltpu.CompilerParams(vmem_limit_bytes=60 * MIB),
+    )(stream, total, small)
+
+
 def small_grads(vectors, sums_one, sums_two, square):
     width = vectors.shape[1]
     one = [jnp.sum(sums_one[8 * i : 8 * i + 8, :], axis=0, keepdims=True) for i in range(7)]
@@ -1102,13 +1156,15 @@
     stream, _, total, small = reduce(
         extents, vectors, residual_input, saved, states, back_mid, packed, acts, sums_two, square
     )
-    mine = lax.axis_index(AXES)
-    squares = small[len(SMALL), :3]
-    small = lax.dynamic_slice(small, (0, mine * share), (len(SMALL), share))
-    large = [total[10], total[11], total[12], total[9], total[8]]
-    large.append(jnp.concatenate([total[j] for j in range(4)], axis=1))
-    large.append(total[4:8].reshape(4 * share, width))
-    return finish(outcome, stream, large, small, squares, residual_input.shape[0] * width * devices)
+    stream, *rest = finish_up(stream, total, small, residual_input.shape[0] * width * devices)
+    large, rms, lines = rest[:7], rest[7], rest[8:]
+    large[6] = large[6].reshape(4 * share, width)
+    shards = [None] * 18
+    for line, i in zip(lines, SMALL):
+        shards[i] = line
+    for grad, i in zip(large, LARGE):
+        shards[i] = grad
+    return (outcome, stream, *shards, rms)
 
 
 def solution(mesh):

time: 267 us -> 256 us (0.959)
  local copies, waits for them, and re-layouts: 11.1 us -> 2.11 us
    pallas_call x0 -> x1, Pallas kernels: none -> 5.02 us  [finish_up(): pl.pallas_call(functools.partial(finish_kernel, entries, depth), name='fi...]
    unnamed x1 -> x0, local copies, waits for them, and re-layouts: 3.75 us -> none
    squeeze x2 -> x0, local copies, waits for them, and re-layouts: 3.56 us -> none  [the longest x1 1.91 us: body(): large = [total[10], total[11], total[12], total[9], total[8]]]
    pallas_call x1, Pallas kernels: 106 us -> 103 us  [reduce(): pl.pallas_call(reduce_kernel, name='reduce', grid=(UNITS + LAGS[3],), in_...]
where the time goes in v4:
time: 256 us
  Pallas kernels  253 us (99%)
    pallas_call x1, Pallas kernels, reduce(): pl.pallas_call(reduce_kernel, name='reduce', grid=(UNITS + LAGS[3],), in_...  103 us
    pallas_call x1, Pallas kernels, gather_front(): pl.pallas_call(functools.partial(gather_kernel, tiles), name='gather_fron...  82.4 us
    pallas_call x1, Pallas kernels, feed(): pl.pallas_call(feed_kernel, name='feed', grid=(tiles,), in_specs=[smem(),...  62.4 us

profile of v4, /device:TPU:0, one launch (start us, length us, event | category | flops | bytes accessed | tf_op | source)
XLA Modules:
  0.0 255.8 jit_solution(14584127248122319013)
XLA Ops:
  0.7 1.5 stack.47
  2.2 0.6 pad.4.small
  2.8 82.4 %gather_front.1 = (bf16[13,4,2,2,2,24,768]{6,5,4,3,2,1,0:T(8,128)(2,1)}, f32[16,768]{1,0:T(8,128)}, f32[2048,768]{1,0:T(8,128)}, f32[2048,768]{1,0:T(8,128)}, f3...) custom-call(s32[1,4]{1,0:T(1,128)} %extents.5, ...), custom_call_target="tpu_custom_call" | custom-call | tf_op jit(solution)/shard_map/gather_front/pallas_call | solution.py:895
  85.2 62.4 %feed.1 = (bf16[2048,768]{1,0:T(8,128)(2,1)}, f32[2048,768]{1,0:T(8,128)}, bf16[14,2048,768]{2,1,0:T(8,128)(2,1)}, f32[48,768]{1,0:T(8,128)}) custom-call(s32[1,4]{1,0:T(1,128)} %extents.5, f32[16,768]{1,0:T(8,128)} %get-tuple-element.59.vectors, f32[2048,768]{1,0:T(8,128)} %get-tuple-element.60.mid_ref.edge_ref, ...), custom_call_target="tpu_custom_call" | custom-call | tf_op jit(solution)/shard_map/feed/pallas_call | solution.py:926
  147.5 103.1 %reduce.1 = (bf16[2048,768]{1,0:T(8,128)(2,1)}, bf16[6,2048,768]{2,1,0:T(8,128)(2,1)}, f32[13,24,768]{2,1,0:T(8,128)}, f32[16,768]{1,0:T(8,128)}) custom-call(s32[1,4]{1,0:T(1,128)} %extents.5, f32[16,768]{1,0:T(8,128)} %get-tuple-element.59.vectors, bf16[2048,768]{1,0:T(8,128)(2,1)} %edge_ref.1, bf16[2048,768]{1,0:T(8,128)(2,1)} %edge_ref.1, ...), custom_call_target="tpu_custom_call" | custom-call | tf_op jit(solution)/shard_map/reduce/pallas_call | solution.py:1003
  250.6 5.0 %finish_up.1 = (bf16[2048,768]{1,0:T(8,128)(2,1)}, f32[24,768]{1,0:T(8,128)}, f32[24,768]{1,0:T(8,128)}, f32[24,768]{1,0:T(8,128)}, f32[24,768]{1,0:T(8,128)}, /...) custom-call(bf16[2048,768]{1,0:T(8,128)(2,1)} %get-tuple-element.74., ...), custom_call_target="tpu_custom_call" | custom-call | tf_op jit(solution)/shard_map/finish_up/pallas_call | solution.py:1073

commit v5 on v4

--- a/solution.py
+++ b/solution.py
@@ -337,6 +337,7 @@
 GRID = (4, 2, 2, 2)
 SMALL_ROWS = 16
 HOPS = 13
+LATE = 11
 
 
 def place():
@@ -429,9 +430,16 @@
 
 
 def gather_kernel(
-    tiles, extents, small, wk, wv, wr, wo, wg, w1, w2, x_ref,
+    tiles, extents, wk, wv, wr, wo, wg, w1, w2, x_ref, *refs
+):
+    lines, refs = refs[: len(SMALL)], refs[len(SMALL) :]
+    gather_steps(tiles, lines, extents, wk, wv, wr, wo, wg, w1, w2, x_ref, *refs)
+
+
+def gather_steps(
+    tiles, lines, extents, wk, wv, wr, wo, wg, w1, w2, x_ref,
     held, vectors, k_out, v_out, s_out, y_out, d_out, blend_out, mid_out, state_out, square_out,
-    small_held, own, weights, grow, shrink, last, state, own_sem, load_sem, send, receive, small_send, small_receive,
+    small, small_held, own, weights, grow, shrink, last, state, own_sem, load_sem, send, receive, small_send, small_receive,
 ):
     tick = pl.program_id(0)
     z, y, x, c = place()
@@ -453,6 +461,9 @@
 
     @pl.when(tick == 0)
     def _():
+        small[...] = jnp.zeros_like(small)
+        for row, line in enumerate(lines):
+            small[row, : line.shape[0]] = line[...].astype(F32)
         for u, ref in enumerate((wk, wv, wr, wo, wg)):
             own[u] = ref[...]
         for j in range(4):
@@ -506,24 +517,24 @@
     def within(u, first, end):
         return jnp.logical_and(u >= first, u < end)
 
-    pl.when(within(tick - 2, 0, 4))(lambda: diagonal(tick - 2))
-    pl.when(within(tick - 3, 4, units))(lambda: diagonal(tick - 3))
+    pl.when(jnp.logical_or(within(tick - 2, 0, 4), within(tick - 2, LATE, units)))(lambda: diagonal(tick - 2))
+    pl.when(within(tick - 3, 4, LATE))(lambda: diagonal(tick - 3))
 
     @pl.when(tick == 2)
     def _():
         small_unit().arrived(5, 6)
         small_unit().start(11, 12)
 
-    pl.when(within(tick - 3, 0, 4))(lambda: partners(tick - 3))
-    pl.when(within(tick - 5, 4, units))(lambda: partners(tick - 5))
+    pl.when(jnp.logical_or(within(tick - 3, 0, 4), within(tick - 3, LATE, units)))(lambda: partners(tick - 3))
+    pl.when(within(tick - 5, 4, LATE))(lambda: partners(tick - 5))
 
     @pl.when(tick == 3)
     def _():
         small_unit().arrived(11, 12)
         small_unit().start(10)
 
-    pl.when(within(tick - 4, 0, 4))(lambda: complete(tick - 4))
-    pl.when(within(tick - 6, 4, units))(lambda: complete(tick - 6))
+    pl.when(jnp.logical_or(within(tick - 4, 0, 4), within(tick - 4, LATE, units)))(lambda: complete(tick - 4))
+    pl.when(within(tick - 6, 4, LATE))(lambda: complete(tick - 6))
 
     @pl.when(jnp.logical_and(tick >= 4, tick < 8))
     def _():
@@ -542,7 +553,7 @@
         total = jnp.zeros((SMALL_ROWS, width), F32)
         empty = jnp.zeros((SMALL_ROWS, width - 128), F32)
         for number in range(GRID[0] * 8):
-            block = small_held[number // 8, number // 4 % 2, number // 2 % 2, number % 2].astype(F32)
+            block = small_held[number // 8, number // 4 % 2, number // 2 % 2, number % 2]
             total += pltpu.roll(jnp.concatenate([block, empty], axis=1), number * share, 1)
         vectors[...] = total
 
@@ -701,10 +712,10 @@
 
 
 def reduce_kernel(
-    extents, vectors, x_ref, edge_ref, k_ref, v_ref, s_ref, y_ref, d_ref, state_ref, mid_ref, weights,
+    extents, vectors, x_ref, edge_ref, k_ref, v_ref, s_ref, y_ref, d_ref, state_ref, mid_ref, packed,
     sums_two, square, acts,
     stream_out, mixed, out, small_out,
-    grow, shrink, carry, state, staged, sums_one, lefts, rights, sums, small_in,
+    grow, shrink, carry, state, weights, weight_sem, staged, sums_one, lefts, rights, sums, small_in,
     stage_sem, left_sem, right_sem, small_send, small_receive, *refs,
 ):
     tick = pl.program_id(0)
@@ -768,7 +779,12 @@
     @pl.when(tick == 0)
     def _():
         fetches(tick, start)
+        pltpu.make_async_copy(packed.at[0:4], weights, weight_sem).start()
         greet()
+
+    @pl.when(tick == FIRST_TILE)
+    def _():
+        pltpu.make_async_copy(packed.at[0:4], weights, weight_sem).wait()
 
     number = tick - FIRST_TILE
     pl.when(jnp.logical_and(number >= 2, number < tiles + 1))(lambda: keep(number - 2).wait())
@@ -882,7 +898,7 @@
     )(extents, vectors, x, packed)
 
 
-def gather_front(extents, small, shards, x):
+def gather_front(extents, lines, shards, x):
     tokens, width = x.shape
     tiles = tokens // ROWS
     depth = shards[0].shape[0]
@@ -895,10 +911,11 @@
     return pl.pallas_call(
         functools.partial(gather_kernel, tiles),
         name="gather_front",
-        grid=(max(UNITS + 6, tiles + 8),),
+        grid=(max(UNITS + 4, LATE + 6, tiles + 8),),
         in_specs=[smem()]
-        + [whole(part.shape) for part in (small, *shards)]
-        + [pl.BlockSpec((ROWS, width), lambda i: (index(i), 0))],
+        + [whole(part.shape) for part in shards]
+        + [pl.BlockSpec((ROWS, width), lambda i: (index(i), 0))]
+        + [whole(line.shape) for line in lines],
         out_specs=[anywhere, kept((SMALL_ROWS, width))] + front_specs(width, index),
         out_shape=[
             jax.ShapeDtypeStruct((UNITS, *GRID, depth, width), LOW),
@@ -906,14 +923,15 @@
         ]
         + front_shapes(tokens, width),
         scratch_shapes=[
-            pltpu.VMEM((*GRID, *small.shape), LOW),
+            pltpu.VMEM((SMALL_ROWS, 128), F32),
+            pltpu.VMEM((*GRID, SMALL_ROWS, 128), F32),
             pltpu.VMEM((UNITS, depth, width), LOW),
             pltpu.VMEM((4, *GRID, depth, width), LOW),
         ]
         + front_scratch(width)
         + [dma((UNITS,)), dma((4,)), dma((9, HOPS)), dma((UNITS, HOPS)), dma((HOPS,)), dma((HOPS,))],
         compiler_params=pltpu.CompilerParams(vmem_limit_bytes=56 * MIB, collective_id=0, has_side_effects=True),
-    )(extents, small, *shards, x)
+    )(extents, *shards, x, *lines)
 
 
 def feed(extents, vectors, mid, upstream, blend, packed):
@@ -1004,7 +1022,7 @@
         reduce_kernel,
         name="reduce",
         grid=(UNITS + LAGS[3],),
-        in_specs=inputs + [whole(sums_two.shape), whole(square.shape), anywhere],
+        in_specs=inputs[:-1] + [anywhere, whole(sums_two.shape), whole(square.shape), anywhere],
         out_specs=[outputs[0], anywhere, kept((UNITS, depth, width)), kept(small)],
         out_shape=[
             stream,
@@ -1014,6 +1032,8 @@
         ],
         scratch_shapes=scratch
         + [
+            pltpu.VMEM((4, *packed.shape[1:]), LOW),
+            dma,
             pltpu.VMEM((2, 6, ROWS, width), LOW),
             pltpu.VMEM(sums_one.shape, F32),
             pltpu.VMEM((2, tokens, width), LOW),
@@ -1067,7 +1087,7 @@
 def finish_up(stream, total, small, entries):
     tokens, width = stream.shape
     depth = total.shape[1]
-    parts = 4
+    parts = 2
     tile = pl.BlockSpec((tokens // parts, width), lambda i: (i, 0))
     shapes = [(depth, width)] * 5 + [(depth, 4 * width), (4, depth, width), (3,)] + [(depth,)] * len(SMALL)
     return pl.pallas_call(
@@ -1147,11 +1167,11 @@
     devices = lax.axis_size(AXES)
     width = residual_input.shape[1]
     share = width // devices
-    small = jnp.stack([parameters[i] for i in SMALL])
-    small = jnp.pad(small, ((0, SMALL_ROWS - len(SMALL)), (0, 128 - share)))
     shards = [parameters[i] for i in LARGE]
     shards[6] = shards[6].reshape(4, share, width)
-    packed, vectors, *saved, blend, mid, states, square = gather_front(extents, small, shards, residual_input)
+    packed, vectors, *saved, blend, mid, states, square = gather_front(
+        extents, [parameters[i] for i in SMALL], shards, residual_input
+    )
     outcome, back_mid, acts, sums_two = feed(extents, vectors, mid, upstream, blend, packed)
     stream, _, total, small = reduce(
         extents, vectors, residual_input, saved, states, back_mid, packed, acts, sums_two, square

time: 256 us -> 250 us (0.977)
  Pallas kernels: 253 us -> 249 us
    pallas_call x1, Pallas kernels: 103 us -> 99.5 us  [reduce(): pl.pallas_call(reduce_kernel, name='reduce', grid=(UNITS + LAGS[3],), in_...]
where the time goes in v5:
time: 250 us; the launch traced here: 249 us
  Pallas kernels  249 us (100%)
    pallas_call x1, Pallas kernels, reduce(): pl.pallas_call(reduce_kernel, name='reduce', grid=(UNITS + LAGS[3],), in_...  99.5 us
    pallas_call x1, Pallas kernels, gather_front(): pl.pallas_call(functools.partial(gather_kernel, tiles), name='gather_fron...  82.8 us
    pallas_call x1, Pallas kernels, feed(): pl.pallas_call(feed_kernel, name='feed', grid=(tiles,), in_specs=[smem(),...  62.4 us

profile of v5, /device:TPU:0, one launch (start us, length us, event | category | flops | bytes accessed | tf_op | source)
XLA Modules:
  0.0 249.4 jit_solution(7490479807281223755)
XLA Ops:
  0.7 82.8 %gather_front.1 = (bf16[13,4,2,2,2,24,768]{6,5,4,3,2,1,0:T(8,128)(2,1)}, f32[16,768]{1,0:T(8,128)}, f32[2048,768]{1,0:T(8,128)}, f32[2048,768]{1,0:T(8,128)}, f3...) custom-call(s32[1,4]{1,0:T(1,128)} %extents.5, ...), custom_call_target="tpu_custom_call" | custom-call | tf_op jit(solution)/shard_map/gather_front/pallas_call | solution.py:911
  83.5 62.4 %feed.1 = (bf16[2048,768]{1,0:T(8,128)(2,1)}, f32[2048,768]{1,0:T(8,128)}, bf16[14,2048,768]{2,1,0:T(8,128)(2,1)}, f32[48,768]{1,0:T(8,128)}) custom-call(s32[1,4]{1,0:T(1,128)} %extents.5, f32[16,768]{1,0:T(8,128)} %get-tuple-element.59.vectors, f32[2048,768]{1,0:T(8,128)} %get-tuple-element.60.mid_ref.edge_ref, ...), custom_call_target="tpu_custom_call" | custom-call | tf_op jit(solution)/shard_map/feed/pallas_call | solution.py:944
  145.9 99.5 %reduce.1 = (bf16[2048,768]{1,0:T(8,128)(2,1)}, bf16[6,2048,768]{2,1,0:T(8,128)(2,1)}, f32[13,24,768]{2,1,0:T(8,128)}, f32[16,768]{1,0:T(8,128)}) custom-call(s32[1,4]{1,0:T(1,128)} %extents.5, f32[16,768]{1,0:T(8,128)} %get-tuple-element.59.vectors, bf16[2048,768]{1,0:T(8,128)(2,1)} %edge_ref.1, bf16[2048,768]{1,0:T(8,128)(2,1)} %edge_ref.1, ...), custom_call_target="tpu_custom_call" | custom-call | tf_op jit(solution)/shard_map/reduce/pallas_call | solution.py:1021
  245.3 4.0 %finish_up.1 = (bf16[2048,768]{1,0:T(8,128)(2,1)}, f32[24,768]{1,0:T(8,128)}, f32[24,768]{1,0:T(8,128)}, f32[24,768]{1,0:T(8,128)}, f32[24,768]{1,0:T(8,128)}, /...) custom-call(bf16[2048,768]{1,0:T(8,128)(2,1)} %get-tuple-element.74., ...), custom_call_target="tpu_custom_call" | custom-call | tf_op jit(solution)/shard_map/finish_up/pallas_call | solution.py:1093

commit v6 on v5

--- a/solution.py
+++ b/solution.py
@@ -164,7 +164,7 @@
 
 
 def feed_kernel(
-    extents, vectors, mid_ref, edge_ref, up_ref, blend_ref, packed,
+    extents, vectors, mid_ref, edge_ref, up_ref, packed,
     out_out, back_out, acts, sums_out,
     lift, carry, wg, w1, w2, load,
 ):
@@ -200,16 +200,19 @@
     feed_gate = (norm * mix_g + before * (1.0 - mix_g)).astype(LOW)
     acts[0] = feed_key
     acts[5] = feed_gate
-    acts[6] = blend_ref[...]
     lowered = None
+    group = []
     for j in range(hidden // width):
         chunk = slice(j * width, (j + 1) * width)
         lifted = jnp.maximum(dot(feed_key, matrix(w1.at[j])), 0.0)
-        lift[:, chunk] = lifted
+        lift[:, chunk] = lifted.astype(LOW)
         squared = (lifted * lifted).astype(LOW)
         acts[1 + j] = squared
-        part = dot(squared, matrix(w2.at[j]))
-        lowered = part if lowered is None else lowered + part
+        group.append(squared)
+        if len(group) == GROUP:
+            part = dot(jnp.concatenate(group, axis=1), matrix(w2.at[j + 1 - GROUP : j + 1]))
+            lowered = part if lowered is None else lowered + part
+            group = []
     sig = jax.nn.sigmoid(dot(feed_gate, matrix(wg)))
     feed_out = sig * lowered
     result = mid + feed_out
@@ -217,15 +220,18 @@
     upstream = up_ref[...].astype(F32)
     back_lowered = (upstream * sig).astype(LOW)
     back_gate = (upstream * lowered * sig * (1.0 - sig)).astype(LOW)
-    acts[11] = back_lowered
-    acts[12] = back_gate
-    back_key = None
+    acts[10] = back_lowered
+    acts[11] = back_gate
+    group = []
     for j in range(hidden // width):
         chunk = slice(j * width, (j + 1) * width)
-        back_lifted = (2.0 * lift[:, chunk] * dot_nt(back_lowered, matrix(w2.at[j]))).astype(LOW)
-        acts[7 + j] = back_lifted
-        part = dot_nt(back_lifted, matrix(w1.at[j]))
-        back_key = part if back_key is None else back_key + part
+        back_lifted = (2.0 * lift[:, chunk].astype(F32) * dot_nt(back_lowered, matrix(w2.at[j]))).astype(LOW)
+        acts[6 + j] = back_lifted
+        group.append(back_lifted)
+    back_key = dot_nt(
+        jnp.concatenate(group, axis=1),
+        jnp.concatenate([matrix(w1.at[j]) for j in range(hidden // width)], axis=1),
+    )
     back_gating = dot_nt(back_gate, matrix(wg))
     late = norm - before
     back_before = keep * (back_key * (1.0 - mix_k) + back_gating * (1.0 - mix_g))
@@ -233,7 +239,7 @@
     carry[0:1, :] = back_before[0:1]
     back_mid = upstream + norm_grad(back_norm, hat, scale, gain)
     back_out[...] = back_mid
-    acts[13] = back_mid.astype(LOW)
+    acts[12] = back_mid.astype(LOW)
     for row, piece in enumerate(
         (back_key * late, back_gating * late, back_norm * hat, back_norm, result * result, feed_out * feed_out)
     ):
@@ -713,7 +719,7 @@
 
 def reduce_kernel(
     extents, vectors, x_ref, edge_ref, k_ref, v_ref, s_ref, y_ref, d_ref, state_ref, mid_ref, packed,
-    sums_two, square, acts,
+    sums_two, square, acts, blend,
     stream_out, mixed, out, small_out,
     grow, shrink, carry, state, weights, weight_sem, staged, sums_one, lefts, rights, sums, small_in,
     stage_sem, left_sem, right_sem, small_send, small_receive, *refs,
@@ -747,20 +753,24 @@
     def right_of(u):
         return lax.rem(jnp.minimum(u, 4) + jnp.maximum(u - 7, 0), 2)
 
-    def fetch_left(u, late):
-        source = mixed.at[u - FIRST_UNITS] if late else acts.at[jnp.maximum(u - 3, 0)]
+    def fetch_left(u, late, last=False):
+        if late:
+            source = mixed.at[u - FIRST_UNITS]
+        else:
+            source = blend if last else acts.at[jnp.maximum(u - 3, 0)]
         return pltpu.make_async_copy(source, lefts.at[left_of(u)], left_sem.at[left_of(u)])
 
     def fetch_right(u, late):
         if late:
             source = mixed.at[u - FIRST_UNITS + 3]
         else:
-            source = acts.at[7 + jnp.minimum(u, 4) + jnp.maximum(u - 7, 0)]
+            source = acts.at[6 + jnp.minimum(u, 4) + jnp.maximum(u - 7, 0)]
         return pltpu.make_async_copy(source, rights.at[right_of(u)], right_sem.at[right_of(u)])
 
     def fetches(u, work):
         early, late = u < FIRST_UNITS, jnp.logical_and(u >= FIRST_UNITS, u < UNITS)
-        pl.when(jnp.logical_and(early, jnp.logical_or(u == 0, u >= 4)))(lambda: work(fetch_left(u, False)))
+        pl.when(jnp.logical_or(u == 0, jnp.logical_and(u >= 4, u < FIRST_UNITS - 1)))(lambda: work(fetch_left(u, False)))
+        pl.when(u == FIRST_UNITS - 1)(lambda: work(fetch_left(u, False, True)))
         pl.when(jnp.logical_and(early, jnp.logical_or(u <= 4, u >= 8)))(lambda: work(fetch_right(u, False)))
         pl.when(late)(lambda: work(fetch_left(u, True)))
         pl.when(late)(lambda: work(fetch_right(u, True)))
@@ -817,14 +827,14 @@
     for lag, work in zip(LAGS, (job.add_pair, job.add_sides, job.add_blocks, job.add_ends)):
         job.stage(tick, lag, work)
 
-    @pl.when(number == tiles)
+    @pl.when(number == tiles - 1)
     def _():
         sums[0] = small_grads(vectors, sums_one, sums_two, square)
         exchange(0).start()
 
     for step in range(1, 6):
 
-        @pl.when(number == tiles + step)
+        @pl.when(number == tiles - 1 + step)
         def _():
             exchange(step - 1).wait()
             total = sums[step - 1] + small_in[step - 1]
@@ -855,7 +865,8 @@
 FIRST_UNITS = 10
 FIRST_TILE = 1
 TURNED = (4, 8)
-FEED_ACTS = 14
+FEED_ACTS = 13
+GROUP = 4
 
 
 def four(packed):
@@ -934,7 +945,7 @@
     )(extents, *shards, x, *lines)
 
 
-def feed(extents, vectors, mid, upstream, blend, packed):
+def feed(extents, vectors, mid, upstream, packed):
     tokens, width = mid.shape
     hidden = 4 * width
     rows, tiles = ROWS, tokens // ROWS
@@ -945,7 +956,7 @@
         feed_kernel,
         name="feed",
         grid=(tiles,),
-        in_specs=[smem(), whole(vectors.shape), tile, edge, tile, tile, pl.BlockSpec(memory_space=pl.ANY)],
+        in_specs=[smem(), whole(vectors.shape), tile, edge, tile, pl.BlockSpec(memory_space=pl.ANY)],
         out_specs=[
             tile,
             tile,
@@ -959,7 +970,7 @@
             jax.ShapeDtypeStruct((48, width), F32),
         ],
         scratch_shapes=[
-            pltpu.VMEM((rows, hidden), F32),
+            pltpu.VMEM((rows, hidden), LOW),
             pltpu.VMEM((8, width), F32),
             pltpu.VMEM(block, LOW),
             pltpu.VMEM((4, *block), LOW),
@@ -967,7 +978,7 @@
             pltpu.SemaphoreType.DMA((6,)),
         ],
         compiler_params=pltpu.CompilerParams(vmem_limit_bytes=60 * MIB),
-    )(extents, vectors, mid, mid, upstream, blend, packed)
+    )(extents, vectors, mid, mid, upstream, packed)
 
 
 def back_specs(tokens, width, packed, index):
@@ -1007,7 +1018,7 @@
     )(extents, vectors, x, x, *saved, states, back_mid, packed)
 
 
-def reduce(extents, vectors, x, saved, states, back_mid, packed, acts, sums_two, square):
+def reduce(extents, vectors, x, saved, states, back_mid, packed, acts, blend, sums_two, square):
     tokens, width = x.shape
     tiles, depth = tokens // ROWS, packed.shape[-2]
     inputs, outputs, shapes, scratch = back_specs(
@@ -1022,7 +1033,7 @@
         reduce_kernel,
         name="reduce",
         grid=(UNITS + LAGS[3],),
-        in_specs=inputs[:-1] + [anywhere, whole(sums_two.shape), whole(square.shape), anywhere],
+        in_specs=inputs[:-1] + [anywhere, whole(sums_two.shape), whole(square.shape), anywhere, anywhere],
         out_specs=[outputs[0], anywhere, kept((UNITS, depth, width)), kept(small)],
         out_shape=[
             stream,
@@ -1060,7 +1071,7 @@
             dma((z - 1,)),
         ],
         compiler_params=pltpu.CompilerParams(vmem_limit_bytes=63 * MIB, collective_id=1, has_side_effects=True),
-    )(extents, vectors, x, x, *saved, states, back_mid, packed, sums_two, square, acts)
+    )(extents, vectors, x, x, *saved, states, back_mid, packed, sums_two, square, acts, blend)
 
 
 def finish_kernel(entries, share, stream_ref, total, small, stream_out, *outs):
@@ -1150,12 +1161,12 @@
     packed = pack([w.reshape(blocks, -1, w.shape[1]) for w in weights])
     packed = packed.reshape(UNITS, *GRID, *packed.shape[2:])
     *saved, blend, mid, states, square = front(extents, vectors, residual_input, packed)
-    outcome, back_mid, acts, sums_two = feed(extents, vectors, mid, upstream, blend, packed)
+    outcome, back_mid, acts, sums_two = feed(extents, vectors, mid, upstream, packed)
     stream, mixed, sums_one = back(extents, vectors, residual_input, saved, states, back_mid, packed)
     small = small_grads(vectors, sums_one, sums_two, square)
-    grads = [dot_tn(mixed[i], mixed[3 + i]) for i in range(3)] + [dot_tn(acts[6], acts[13]), dot_tn(acts[5], acts[12])]
-    grads.append(jnp.concatenate([dot_tn(acts[0], acts[7 + j]) for j in range(4)], axis=1))
-    grads.append(jnp.concatenate([dot_tn(acts[1 + j], acts[11]) for j in range(4)], axis=0))
+    grads = [dot_tn(mixed[i], mixed[3 + i]) for i in range(3)] + [dot_tn(blend, acts[12]), dot_tn(acts[5], acts[11])]
+    grads.append(jnp.concatenate([dot_tn(acts[0], acts[6 + j]) for j in range(4)], axis=1))
+    grads.append(jnp.concatenate([dot_tn(acts[1 + j], acts[10]) for j in range(4)], axis=0))
     squares = lax.psum(small[len(SMALL), :3], AXES)
     small = lax.psum_scatter(small[: len(SMALL)], AXES, scatter_dimension=1, tiled=True)
     large = [lax.psum_scatter(grad, AXES, scatter_dimension=0, tiled=True) for grad in grads]
@@ -1172,9 +1183,9 @@
     packed, vectors, *saved, blend, mid, states, square = gather_front(
         extents, [parameters[i] for i in SMALL], shards, residual_input
     )
-    outcome, back_mid, acts, sums_two = feed(extents, vectors, mid, upstream, blend, packed)
+    outcome, back_mid, acts, sums_two = feed(extents, vectors, mid, upstream, packed)
     stream, _, total, small = reduce(
-        extents, vectors, residual_input, saved, states, back_mid, packed, acts, sums_two, square
+        extents, vectors, residual_input, saved, states, back_mid, packed, acts, blend, sums_two, square
     )
     stream, *rest = finish_up(stream, total, small, residual_input.shape[0] * width * devices)
     large, rms, lines = rest[:7], rest[7], rest[8:]

time: 250 us -> 247 us (0.988)
  Pallas kernels: 249 us -> 246 us
where the time goes in v6:
time: 247 us
  Pallas kernels  246 us (100%)
    pallas_call x1, Pallas kernels, reduce(): pl.pallas_call(reduce_kernel, name='reduce', grid=(UNITS + LAGS[3],), in_...  99.1 us
    pallas_call x1, Pallas kernels, gather_front(): pl.pallas_call(functools.partial(gather_kernel, tiles), name='gather_fron...  82.7 us
    pallas_call x1, Pallas kernels, feed(): pl.pallas_call(feed_kernel, name='feed', grid=(tiles,), in_specs=[smem(),...  60.2 us

profile of v6, /device:TPU:0, one launch (start us, length us, event | category | flops | bytes accessed | tf_op | source)
XLA Modules:
  0.0 246.9 jit_solution(3805014449801940111)
XLA Ops:
  0.7 82.7 %gather_front.1 = (bf16[13,4,2,2,2,24,768]{6,5,4,3,2,1,0:T(8,128)(2,1)}, f32[16,768]{1,0:T(8,128)}, f32[2048,768]{1,0:T(8,128)}, f32[2048,768]{1,0:T(8,128)}, f3...) custom-call(s32[1,4]{1,0:T(1,128)} %extents.5, ...), custom_call_target="tpu_custom_call" | custom-call | tf_op jit(solution)/shard_map/gather_front/pallas_call | solution.py:922
  83.4 60.2 %feed.1 = (bf16[2048,768]{1,0:T(8,128)(2,1)}, f32[2048,768]{1,0:T(8,128)}, bf16[13,2048,768]{2,1,0:T(8,128)(2,1)}, f32[48,768]{1,0:T(8,128)}) custom-call(s32[1,4]{1,0:T(1,128)} %extents.5, f32[16,768]{1,0:T(8,128)} %get-tuple-element.59.vectors, f32[2048,768]{1,0:T(8,128)} %get-tuple-element.60.mid_ref.edge_ref, ...), custom_call_target="tpu_custom_call" | custom-call | tf_op jit(solution)/shard_map/feed/pallas_call | solution.py:955
  143.6 99.1 %reduce.1 = (bf16[2048,768]{1,0:T(8,128)(2,1)}, bf16[6,2048,768]{2,1,0:T(8,128)(2,1)}, f32[13,24,768]{2,1,0:T(8,128)}, f32[16,768]{1,0:T(8,128)}) custom-call(s32[1,4]{1,0:T(1,128)} %extents.5, f32[16,768]{1,0:T(8,128)} %get-tuple-element.59.vectors, bf16[2048,768]{1,0:T(8,128)(2,1)} %edge_ref.1, bf16[2048,768]{1,0:T(8,128)(2,1)} %edge_ref.1, ...), custom_call_target="tpu_custom_call" | custom-call | tf_op jit(solution)/shard_map/reduce/pallas_call | solution.py:1032
  242.8 4.0 %finish_up.1 = (bf16[2048,768]{1,0:T(8,128)(2,1)}, f32[24,768]{1,0:T(8,128)}, f32[24,768]{1,0:T(8,128)}, f32[24,768]{1,0:T(8,128)}, f32[24,768]{1,0:T(8,128)}, /...) custom-call(bf16[2048,768]{1,0:T(8,128)(2,1)} %get-tuple-element.74., ...), custom_call_target="tpu_custom_call" | custom-call | tf_op jit(solution)/shard_map/finish_up/pallas_call | solution.py:1104

commit v7 on v6

--- a/solution.py
+++ b/solution.py
@@ -1098,7 +1098,7 @@
 def finish_up(stream, total, small, entries):
     tokens, width = stream.shape
     depth = total.shape[1]
-    parts = 2
+    parts = 1
     tile = pl.BlockSpec((tokens // parts, width), lambda i: (i, 0))
     shapes = [(depth, width)] * 5 + [(depth, 4 * width), (4, depth, width), (3,)] + [(depth,)] * len(SMALL)
     return pl.pallas_call(

time: 247 us -> 247 us (level)
  no operation moved by 1% of the time
where the time goes in v7:
time: 247 us
  Pallas kernels  246 us (100%)
    pallas_call x1, Pallas kernels, reduce(): pl.pallas_call(reduce_kernel, name='reduce', grid=(UNITS + LAGS[3],), in_...  99.1 us
    pallas_call x1, Pallas kernels, gather_front(): pl.pallas_call(functools.partial(gather_kernel, tiles), name='gather_fron...  82.7 us
    pallas_call x1, Pallas kernels, feed(): pl.pallas_call(feed_kernel, name='feed', grid=(tiles,), in_specs=[smem(),...  60.2 us

profile of v7, /device:TPU:0, one launch (start us, length us, event | category | flops | bytes accessed | tf_op | source)
XLA Modules:
  0.0 247.2 jit_solution(18193722302656709526)
XLA Ops:
  0.7 82.7 %gather_front.1 = (bf16[13,4,2,2,2,24,768]{6,5,4,3,2,1,0:T(8,128)(2,1)}, f32[16,768]{1,0:T(8,128)}, f32[2048,768]{1,0:T(8,128)}, f32[2048,768]{1,0:T(8,128)}, f3...) custom-call(s32[1,4]{1,0:T(1,128)} %extents.5, ...), custom_call_target="tpu_custom_call" | custom-call | tf_op jit(solution)/shard_map/gather_front/pallas_call | solution.py:922
  83.4 60.2 %feed.1 = (bf16[2048,768]{1,0:T(8,128)(2,1)}, f32[2048,768]{1,0:T(8,128)}, bf16[13,2048,768]{2,1,0:T(8,128)(2,1)}, f32[48,768]{1,0:T(8,128)}) custom-call(s32[1,4]{1,0:T(1,128)} %extents.5, f32[16,768]{1,0:T(8,128)} %get-tuple-element.59.vectors, f32[2048,768]{1,0:T(8,128)} %get-tuple-element.60.mid_ref.edge_ref, ...), custom_call_target="tpu_custom_call" | custom-call | tf_op jit(solution)/shard_map/feed/pallas_call | solution.py:955
  143.6 99.1 %reduce.1 = (bf16[2048,768]{1,0:T(8,128)(2,1)}, bf16[6,2048,768]{2,1,0:T(8,128)(2,1)}, f32[13,24,768]{2,1,0:T(8,128)}, f32[16,768]{1,0:T(8,128)}) custom-call(s32[1,4]{1,0:T(1,128)} %extents.5, f32[16,768]{1,0:T(8,128)} %get-tuple-element.59.vectors, bf16[2048,768]{1,0:T(8,128)(2,1)} %edge_ref.1, bf16[2048,768]{1,0:T(8,128)(2,1)} %edge_ref.1, ...), custom_call_target="tpu_custom_call" | custom-call | tf_op jit(solution)/shard_map/reduce/pallas_call | solution.py:1032
  242.8 4.3 %finish_up.1 = (bf16[2048,768]{1,0:T(8,128)(2,1)}, f32[24,768]{1,0:T(8,128)}, f32[24,768]{1,0:T(8,128)}, f32[24,768]{1,0:T(8,128)}, f32[24,768]{1,0:T(8,128)}, /...) custom-call(bf16[2048,768]{1,0:T(8,128)(2,1)} %get-tuple-element.74., ...), custom_call_target="tpu_custom_call" | custom-call | tf_op jit(solution)/shard_map/finish_up/pallas_call | solution.py:1104
